TPU v7x, 128 devices: a whole 4x4x4 slice. The times are simulated.
128 devices in a mesh: row: 8 (over x_hi, y), col: 16 (over x_lo, z, core).
Axes of the slice: x: 4 (x_hi: 2, x_lo: 2; x = x_hi * 2 + x_lo), y: 4, z: 4, core: 2. Of those that a mesh axis runs over, the one named last changes fastest.
Arguments:
- tokens: bfloat16 [8192, 12288], P('row', 'col'), may hold values from -6 to 6
- joined_weight: bfloat16 [12288, 8192], P('row', 'col'), may hold values from -0.0546875 to 0.0546875
- positions: int32 [8192], P('row'), may hold values from 0 to 8191
Outputs:
- queries: bfloat16 [8192, 6144], P(('row', 'col'))
- rotated_keys: bfloat16 [8192, 1024], P(('row', 'col'))
- values: bfloat16 [8192, 1024], P(('row', 'col'))
All inputs are finite; a program needn't handle non-finite values.
Results may differ from a plain program's by a relative error of at most 0.001.
Values may be sent and summed in bfloat16 or wider, within the bound.
No kernel may reach another device: no remote copies, remote signals or barrier semaphores. Data moves between devices by JAX's collectives and lax.ppermute only.
A program may use at most 128 MiB of HBM per device.

v0:
```python
import math

import jax
import jax.numpy as jnp
from jax import lax
from jax.sharding import PartitionSpec as P

HEAD_WIDTH = 128
QUERY_HEADS = 48
KEY_VALUE_HEADS = 8


rope_base = 1000000.0


def rotary_tables(positions, head_size):
    half_size = head_size // 2
    column_ids = jnp.arange(head_size, dtype=jnp.int32)
    exponent = (column_ids % half_size).astype(jnp.float32) * (
        -2.0 * math.log(rope_base) / head_size
    )
    frequency = jnp.exp(exponent)
    angles = positions.astype(jnp.float32)[:, None] * frequency[None, :]
    sign_table = jnp.where(column_ids < half_size, -1.0, 1.0).astype(jnp.float32)
    return (jnp.cos(angles), jnp.sin(angles) * sign_table[None, :])


def rotate(head_groups, positions):
    cosine, sine_table = rotary_tables(positions, head_groups.shape[-1])
    swapped = jnp.roll(head_groups, head_groups.shape[-1] // 2, axis=-1)
    return head_groups * cosine[:, None, :] + swapped * sine_table[:, None, :]


def shards(tokens, joined_weight, positions):
    tok_count = tokens.shape[0]
    whole_rows = lax.all_gather(tokens, "col", axis=1, tiled=True)
    projected_rows = jnp.dot(
        whole_rows,
        lax.all_gather(joined_weight, "row", axis=0, tiled=True),
        preferred_element_type=jnp.float32,
    )
    rotated_columns = (QUERY_HEADS + KEY_VALUE_HEADS) * HEAD_WIDTH
    received_blocks = lax.all_to_all(projected_rows, "col", split_axis=0, concat_axis=1, tiled=True)
    device_share = tok_count // lax.axis_size("col")
    local_positions = lax.dynamic_slice_in_dim(
        positions, lax.axis_index("col") * device_share, device_share, 0
    )
    head_groups = received_blocks[:, :rotated_columns].reshape(
        device_share, QUERY_HEADS + KEY_VALUE_HEADS, HEAD_WIDTH
    )
    turned = (
        rotate(head_groups, local_positions)
        .reshape(device_share, rotated_columns)
        .astype(jnp.bfloat16)
    )
    regrouped = jnp.concatenate(
        [turned, received_blocks[:, rotated_columns:].astype(jnp.bfloat16)], axis=1
    )
    queries = regrouped[:, : QUERY_HEADS * HEAD_WIDTH]
    rotated_keys = regrouped[:, QUERY_HEADS * HEAD_WIDTH : rotated_columns]
    values = regrouped[:, rotated_columns:]
    return (queries, rotated_keys, values)


def solution(mesh):
    in_specs = (P("row", "col"), P("row", "col"), P("row"))
    out_specs = (P(("row", "col"), None), P(("row", "col"), None), P(("row", "col"), None))
    return jax.shard_map(shards, mesh=mesh, in_specs=in_specs, out_specs=out_specs, check_vma=False)
```

profile of v0, /device:TPU:1, one launch (start us, length us, event | category | flops | bytes accessed | tf_op | source)
XLA Modules:
  0.0 355.8 jit_solution(15941559933943566686)
XLA Ops:
  7.2 0.0 all-gather.5.cloned.1.call-start
  7.2 0.7 all-gather.5.cloned.1.call-update
  7.9 0.0 all-gather.3.cloned.1.call-start
  7.9 0.7 all-gather.3.cloned.1.call-update
  8.6 149.3 %all-gather.5.cloned.1.call-done = bf16[12288,512]{1,0:T(8,128)(2,1)} async-done(((bf16[1536,512]{1,0:T(8,128)(2,1)}), bf16[12288,512]{1,0:T(8,128)(2,1)}) %all-gather.5.cloned.1.call-update) | async-done | bytes 12582928 | tf_op jit(solution)/shard_map/all_gather | solution.py:39
  158.0 131.6 %all-gather.3.cloned.1.call-done = bf16[1024,12288]{1,0:T(8,128)(2,1)} async-done(((bf16[1024,768]{1,0:T(8,128)(2,1)}), bf16[1024,12288]{1,0:T(8,128)(2,1)}) %all-gather.3.cloned.1.call-update) | async-done | bytes 25165840 | tf_op jit(solution)/shard_map/all_gather | solution.py:36
  289.5 21.4 %fusion.6 = f32[1024,512]{1,0:T(8,128)} fusion(bf16[1024,12288]{1,0:T(8,128)(2,1)} %all-gather.3.cloned.1.call-done, bf16[12288,512]{1,0:T(8,128)(2,1)} %all-gather.5.cloned.1.call-done), kind=kOutput, calls=%fused_computation.16 | convolution fusion | flops 12884901888 | bytes 39845888 | tf_op jit(solution)/shard_map/dot_general | solution.py:37
  310.9 5.1 %all-to-all-start = ((f32[16,64,512]{2,1,0:T(8,128)}), f32[16,64,512]{2,1,0:T(8,128)S(1)}, u32[]{:S(2)}, u32[]{:S(2)}) async-start(f32[16,64,512]{2,1,0:T(8,128)} %bitcast.26), calls=%async_computation | async-start | bytes 4194304 | tf_op jit(solution)/shard_map/all_to_all | solution.py:43
  316.0 0.8 dynamic-slice_convert_fusion
  316.8 0.2 multiply_cosine_fusion
  317.0 27.0 %all-to-all-done = f32[16,64,512]{2,1,0:T(8,128)S(1)} async-done(((f32[16,64,512]{2,1,0:T(8,128)}), f32[16,64,512]{2,1,0:T(8,128)S(1)}, u32[]{:S(2)}, u32[]{:S(2)}) %all-to-all-start) | async-done | bytes 2097184 | tf_op jit(solution)/shard_map/all_to_all | solution.py:43
  344.0 0.2 copy.7
  344.2 0.1 slice_bitcast_fusion
  344.3 0.3 copy.9
  344.7 0.6 fusion.5
  345.3 0.6 maximum_multiply_fusion
  345.9 0.1 mul.74
  346.0 0.6 fusion
  346.7 0.9 slice.30
  347.6 0.7 slice.31
  348.2 0.7 slice.36
  (1 shorter events, 0.0 us)
Async XLA Ops:
  7.2 150.8 %all-gather.5.cloned.1.call-start = ((), (), s32[]{:S(2)}) async-start(), calls=%async_computation.2 | async-start | bytes 14155776 | tf_op jit(solution)/shard_map/all_gather | solution.py:39
  7.9 281.6 %all-gather.3.cloned.1.call-start = ((), (), s32[]{:S(2)}) async-start(), calls=%async_computation.1 | async-start | bytes 26738688 | tf_op jit(solution)/shard_map/all_gather | solution.py:36
  310.9 33.1 %all-to-all-start = ((f32[16,64,512]{2,1,0:T(8,128)}), f32[16,64,512]{2,1,0:T(8,128)S(1)}, u32[]{:S(2)}, u32[]{:S(2)}) async-start(f32[16,64,512]{2,1,0:T(8,128)} %bitcast.26), calls=%async_computation | async-start | bytes 4194304 | tf_op jit(solution)/shard_map/all_to_all | solution.py:43
Sparse Core Ops, SparseCore 0:
  10.3 147.6 all-gather.4
  159.6 129.8 all-gather.2
where the time goes:
time: 356 us
  waiting for transfers between devices  309 us (87%)
  matrix products  21.4 us (6%)
  between operations  14.1 us (4%)
  starting transfers between devices  5.15 us (1%)
  local copies, waits for them, and re-layouts  3.61 us (1%)
    all_gather x1, waiting for transfers between devices, shards(): lax.all_gather(joined_weight, 'row', axis=0, tiled=True)  149 us
    all_gather x1, waiting for transfers between devices, shards(): whole_rows = lax.all_gather(tokens, 'col', axis=1, tiled=True)  132 us
    all_to_all x1, waiting for transfers between devices, shards(): lax.all_to_all(projected_rows, 'col', split_axis=0, concat_axis=1, tiled=...  27 us
    dot_general x1, matrix products, shards(): jnp.dot(whole_rows, lax.all_gather(joined_weight, 'row', axis=0, tiled=Tr...  21.4 us
  transfers between devices with their start and end apart: 3, of which 3 were waited for; matrix products, arithmetic and copies ran while one was open for 0% of the time, Pallas kernels for 0%

commit v1 on v0

v1 whole, which is shorter than its diff:
```python
import math

import jax
import jax.numpy as jnp
import numpy as np
from jax import lax
from jax.experimental import pallas as pl
from jax.experimental.pallas import tpu as pltpu
from jax.sharding import Mesh
from jax.sharding import PartitionSpec as P

HEAD_WIDTH = 128
QUERY_HEADS = 48
KEY_VALUE_HEADS = 8

rope_base = 1000000.0
SWAP = ((0, 1), (1, 0))


def rotary_tables(positions, head_size):
    half_size = head_size // 2
    column_ids = jnp.arange(head_size, dtype=jnp.int32)
    exponent = (column_ids % half_size).astype(jnp.float32) * (
        -2.0 * math.log(rope_base) / head_size
    )
    frequency = jnp.exp(exponent)
    angles = positions.astype(jnp.float32)[:, None] * frequency[None, :]
    sign_table = jnp.where(column_ids < half_size, -1.0, 1.0).astype(jnp.float32)
    return (jnp.cos(angles), jnp.sin(angles) * sign_table[None, :])


def ring_step(block, axis):
    pairs = [
        (i * 2 + c, ((i + (1, -1)[c]) % 4) * 2 + c) for i in range(4) for c in range(2)
    ]
    return lax.ppermute(block, (axis, "c"), pairs)


def ring(block, axis):
    blocks = [block]
    for _ in range(3):
        blocks.append(ring_step(blocks[-1], axis))
    return blocks


def piece_table():
    table = np.zeros((2, 4, 2, 4, 2, 16, 2), np.int32)
    for xh in range(2):
        for y in range(4):
            for xl in range(2):
                for z in range(4):
                    for c in range(2):
                        rows = []
                        for which in range(2):
                            half = c if which == 0 else 1 - c
                            toward = 1 if half == 0 else -1
                            for partner in range(2):
                                for step in range(4):
                                    block = (xl ^ partner, (z - toward * step) % 4)
                                    own = 1 if c == 0 else -1
                                    b_step = ((y - block[1]) * own) % 4
                                    b_partner = xh ^ block[0]
                                    late = max(partner * 4 + step, b_partner * 4 + b_step)
                                    rows.append(
                                        (late, which * 8 + partner * 4 + step, (b_partner * 4 + b_step) * 2 + half)
                                    )
                        rows.sort()
                        table[xh, y, xl, z, c] = [r[1:] for r in rows]
    return table


TABLE = piece_table()


def product(table, first, count, a_pieces, b_pieces, total=None, tables=None):
    chunks = len(a_pieces[0])
    chunk_rows, depth = a_pieces[0][0].shape
    rows = chunk_rows * chunks
    columns = b_pieces[0].shape[1]
    n_a, n_b = len(a_pieces), len(b_pieces)
    slots = 3
    tile = 256
    last = tables is not None

    def kernel(table_ref, *refs):
        a_refs = [refs[p * chunks : (p + 1) * chunks] for p in range(n_a)]
        refs = refs[n_a * chunks :]
        b_refs, refs = refs[:n_b], refs[n_b:]
        if total is not None:
            total_ref, refs = refs[0], refs[1:]
        if last:
            (cos_ref, sin_ref), refs = refs[:2], refs[2:]
        out_ref, a_buf, b_buf, acc, sems = refs

        def start(k):
            slot = lax.rem(k, slots)
            a_id = table_ref[(first + k) * 2]
            b_id = table_ref[(first + k) * 2 + 1]
            for p in range(n_a):

                @pl.when(a_id == p)
                def _():
                    for j in range(chunks):
                        pltpu.make_async_copy(
                            a_refs[p][j],
                            a_buf.at[slot, pl.ds(j * chunk_rows, chunk_rows), :],
                            sems.at[slot, j],
                        ).start()

            for q in range(n_b):

                @pl.when(b_id == q)
                def _():
                    pltpu.make_async_copy(b_refs[q], b_buf.at[slot], sems.at[slot, chunks]).start()

        def wait(k):
            slot = lax.rem(k, slots)
            for j in range(chunks):
                part = a_buf.at[slot, pl.ds(j * chunk_rows, chunk_rows), :]
                pltpu.make_async_copy(part, part, sems.at[slot, j]).wait()
            pltpu.make_async_copy(b_buf.at[slot], b_buf.at[slot], sems.at[slot, chunks]).wait()

        def spans(body):
            @pl.loop(0, rows // tile)
            def _(i):
                body(pl.ds(pl.multiple_of(i * tile, tile), tile))

        sum_ref = acc if last else out_ref

        @pl.loop(0, slots - 1)
        def _(k):
            start(k)

        def begin(span):
            if total is None:
                sum_ref[span, :] = jnp.zeros((tile, columns), jnp.float32)
            else:
                sum_ref[span, :] = total_ref[span, :]

        spans(begin)

        @pl.loop(0, count)
        def _(k):
            wait(k)

            @pl.when(k + slots - 1 < count)
            def _():
                start(k + slots - 1)

            slot = lax.rem(k, slots)

            def add(span):
                sum_ref[span, :] += jnp.dot(
                    a_buf[slot, span, :], b_buf[slot], preferred_element_type=jnp.float32
                )

            spans(add)

        def turn(span):
            cosine, sine = cos_ref[span, :], sin_ref[span, :]
            for h in range(columns // HEAD_WIDTH):
                head = acc[span, h * HEAD_WIDTH : (h + 1) * HEAD_WIDTH]
                swapped = pltpu.roll(head, HEAD_WIDTH // 2, 1)
                out_ref[span, h * HEAD_WIDTH : (h + 1) * HEAD_WIDTH] = (
                    head * cosine + swapped * sine
                ).astype(jnp.bfloat16)

        if last:
            spans(turn)

    anywhere = pl.BlockSpec(memory_space=pl.ANY)
    vmem = pl.BlockSpec(memory_space=pltpu.VMEM)
    operands = [table.reshape(-1)]
    in_specs = [pl.BlockSpec(memory_space=pltpu.SMEM)]
    for piece in a_pieces:
        operands += piece
        in_specs += [anywhere] * chunks
    operands += b_pieces
    in_specs += [anywhere] * n_b
    if total is not None:
        operands.append(total)
        in_specs.append(vmem)
    if last:
        operands += tables
        in_specs += [vmem] * 2
    return pl.pallas_call(
        kernel,
        out_shape=jax.ShapeDtypeStruct((rows, columns), jnp.bfloat16 if last else jnp.float32),
        in_specs=in_specs,
        out_specs=vmem,
        scratch_shapes=[
            pltpu.VMEM((slots, rows, depth), a_pieces[0][0].dtype),
            pltpu.VMEM((slots, depth, columns), b_pieces[0].dtype),
            pltpu.VMEM((rows, columns), jnp.float32),
            pltpu.SemaphoreType.DMA((slots, chunks + 1)),
        ],
        compiler_params=pltpu.CompilerParams(vmem_limit_bytes=24 * 1024 * 1024),
        cost_estimate=pl.CostEstimate(
            flops=2 * rows * columns * depth * count,
            bytes_accessed=(rows + columns) * depth * 2 * count,
            transcendentals=0,
        ),
    )(*operands)


CHUNKS = 2


def shards(tokens, joined_weight, positions):
    rows, depth = tokens.shape
    columns = joined_weight.shape[1]
    place = [lax.axis_index(a) for a in ("xh", "y", "xl", "z", "c")]
    table = jnp.asarray(TABLE)[tuple(place)]

    part = rows // CHUNKS
    a_chunks, b_chunks = [], []
    for k in range(CHUNKS):
        own = tokens[k * part : (k + 1) * part]
        a_chunks.append(ring(own, "z") + ring(lax.ppermute(own, "xl", SWAP), "z"))
    for k in range(2):
        own = joined_weight[k * depth : (k + 1) * depth]
        b_chunks.append(ring(own, "y") + ring(lax.ppermute(own, "xh", SWAP), "y"))
    a_pieces = [[a_chunks[k][i] for k in range(CHUNKS)] for i in range(8)]
    a_pieces += [[lax.ppermute(v, "c", SWAP) for v in piece] for piece in a_pieces]
    b_pieces = [b_chunks[k][i] for i in range(8) for k in range(2)]

    column_block = (place[2] * 4 + place[3]) * 2 + place[4]
    rotated = column_block * columns < (QUERY_HEADS + KEY_VALUE_HEADS) * HEAD_WIDTH
    cosine, sine = rotary_tables(positions, HEAD_WIDTH)
    tables = [jnp.where(rotated, cosine, 1.0), jnp.where(rotated, sine, 0.0)]

    turned = product(table, 0, 16, a_pieces, b_pieces, None, tables)
    received = lax.all_to_all(turned, ("xl", "z", "c"), split_axis=0, concat_axis=1, tiled=True)
    query_columns = QUERY_HEADS * HEAD_WIDTH
    rotated_columns = (QUERY_HEADS + KEY_VALUE_HEADS) * HEAD_WIDTH
    return (
        received[:, :query_columns],
        received[:, query_columns:rotated_columns],
        received[:, rotated_columns:],
    )


def solution(mesh):
    fine = Mesh(mesh.devices.reshape(2, 4, 2, 4, 2), ("xh", "y", "xl", "z", "c"))
    row, col = ("xh", "y"), ("xl", "z", "c")
    in_specs = (P(row, col), P(row, col), P(row))
    out_specs = (P(row + col, None),) * 3
    return jax.shard_map(shards, mesh=fine, in_specs=in_specs, out_specs=out_specs, check_vma=False)
```

time: 356 us -> 284 us (0.80)
  waiting for transfers between devices: 309 us -> 100 us
  starting transfers between devices: 5.15 us -> 65.6 us
  local copies, waits for them, and re-layouts: 3.61 us -> 61.2 us
  Pallas kernels: 0 us -> 30.2 us
  blocking collectives: 0 us -> 22.6 us
  matrix products: 21.4 us -> 0 us
  between operations: 14.1 us -> 0.85 us
    all_gather x2 -> x0, waiting for transfers between devices: 281 us -> none  [the longest x1 149 us: shards(): lax.all_gather(joined_weight, 'row', axis=0, tiled=True)]
    ppermute x0 -> x44, waiting for transfers between devices: none -> 100 us  [the longest x24 49.2 us: ring_step(): return lax.ppermute(block, (axis, 'c'), pairs)]
    ppermute x0 -> x44, starting transfers between devices: none -> 65.6 us  [the longest x24 41 us: ring_step(): return lax.ppermute(block, (axis, 'c'), pairs)]
    unnamed x2 -> x126, local copies, waits for them, and re-layouts: 0.45 us -> 57 us
    pallas_call x0 -> x1, Pallas kernels: none -> 30.2 us  [product(): pl.pallas_call(kernel, out_shape=jax.ShapeDtypeStruct((rows, columns), jn...]
    all_to_all x1 -> x0, waiting for transfers between devices: 27 us -> none  [shards(): lax.all_to_all(projected_rows, 'col', split_axis=0, concat_axis=1, tiled=...]
    all_to_all x0 -> x1, blocking collectives: none -> 22.6 us  [shards(): lax.all_to_all(turned, ('xl', 'z', 'c'), split_axis=0, concat_axis=1, til...]
    dot_general x1 -> x0, matrix products: 21.4 us -> none  [shards(): jnp.dot(whole_rows, lax.all_gather(joined_weight, 'row', axis=0, tiled=Tr...]
  transfers between devices with their start and end apart: 3 -> 44, of which waited for: 3 -> 16; matrix products, arithmetic and copies ran while one was open for 0% -> 1% of each run, Pallas kernels for 0% -> 0%
where the time goes in v1:
time: 284 us; the launch traced here: 282 us
  waiting for transfers between devices  100 us (35%)
  starting transfers between devices  65.6 us (23%)
  local copies, waits for them, and re-layouts  61.2 us (22%)
  Pallas kernels  30.2 us (11%)
  blocking collectives  22.6 us (8%)
    unnamed x126, local copies, waits for them, and re-layouts  57 us
    ppermute x24, waiting for transfers between devices, ring_step(): return lax.ppermute(block, (axis, 'c'), pairs)  49.2 us
    ppermute x24, starting transfers between devices, ring_step(): return lax.ppermute(block, (axis, 'c'), pairs)  41 us
    pallas_call x1, Pallas kernels, product(): pl.pallas_call(kernel, out_shape=jax.ShapeDtypeStruct((rows, columns), jn...  30.2 us
    ppermute x2, waiting for transfers between devices, shards(): b_chunks.append(ring(own, 'y') + ring(lax.ppermute(own, 'xh', SWAP), 'y'))  28.3 us
    ppermute x2, waiting for transfers between devices, shards(): a_chunks.append(ring(own, 'z') + ring(lax.ppermute(own, 'xl', SWAP), 'z'))  22.6 us
    all_to_all x1, blocking collectives, shards(): lax.all_to_all(turned, ('xl', 'z', 'c'), split_axis=0, concat_axis=1, til...  22.6 us
    ppermute x16, starting transfers between devices, shards(): lax.ppermute(v, 'c', SWAP)  20 us
  transfers between devices with their start and end apart: 44, of which 16 were waited for; matrix products, arithmetic and copies ran while one was open for 1% of the time, Pallas kernels for 0%

profile of v1, /device:TPU:1, one launch (start us, length us, event | category | flops | bytes accessed | tf_op | source)
XLA Modules:
  0.0 282.4 jit_solution(16918066647033670796)
XLA Ops:
  0.6 1.6 fusion.7
  2.2 1.5 collective-permute-start.15
  3.7 1.3 collective-permute-start.7
  5.0 3.8 %collective-permute-start.1 = (bf16[512,768]{1,0:T(8,128)(2,1)S(1)}, bf16[512,768]{1,0:T(8,128)(2,1)S(1)}, u32[]{:S(2)}, u32[]{:S(2)}) collective-permute-start(bf16[512,768]{1,0:T(8,128)(2,1)S(1)} %get-tuple-element.5.refs_1_), channel_id=1, source_target_pairs={{0,2},{1,7},{2,4},{3,1},{4,6},{5,3},{6,0},{7,5},{8,10},{9,15},{10,... | collective-permute-start | bytes 2359304 | tf_op jit(solution)/shard_map/ppermute | solution.py:36
  10.4 12.4 %collective-permute-done.7.refs_9_ = bf16[512,768]{1,0:T(8,128)(2,1)S(1)} collective-permute-done((bf16[512,768]{1,0:T(8,128)(2,1)S(1)}, bf16[512,768]{1,0:T(8,128)(2,1)S(1)}, u32[]{:S(2)}, u32[]{:S(2)}) %collective-permute-start.7) | collective-permute-done | bytes 786464 | tf_op jit(solution)/shard_map/ppermute | solution.py:219
  22.8 2.8 %collective-permute-start.37 = (bf16[768,512]{1,0:T(8,128)(2,1)S(1)}, bf16[768,512]{1,0:T(8,128)(2,1)S(1)}, u32[]{:S(2)}, u32[]{:S(2)}) collective-permute-start(bf16[768,512]{1,0:T(8,128)(2,1)S(1)} %get-tuple-element.3.refs_33_), channel_id=1, source_target_pairs={{0,64},{64,0},{1,65},{65,1},{2,66},{66,2},{3,67},{67,3},{4,68},{68... | collective-permute-start | bytes 2359304 | tf_op jit(solution)/shard_map/ppermute | solution.py:222
  25.7 2.7 collective-permute-start.31
  29.5 10.2 %collective-permute-done.6.refs_8_ = bf16[512,768]{1,0:T(8,128)(2,1)S(1)} collective-permute-done((bf16[512,768]{1,0:T(8,128)(2,1)S(1)}, bf16[512,768]{1,0:T(8,128)(2,1)S(1)}, u32[]{:S(2)}, u32[]{:S(2)}) %collective-permute-start.6) | collective-permute-done | bytes 786464 | tf_op jit(solution)/shard_map/ppermute | solution.py:219
  39.7 2.8 collective-permute-start.30
  42.7 16.1 %collective-permute-done.37.refs_41_ = bf16[768,512]{1,0:T(8,128)(2,1)S(1)} collective-permute-done((bf16[768,512]{1,0:T(8,128)(2,1)S(1)}, bf16[768,512]{1,0:T(8,128)(2,1)S(1)}, u32[]{:S(2)}, u32[]{:S(2)}) %collective-permute-start.37) | collective-permute-done | bytes 786464 | tf_op jit(solution)/shard_map/ppermute | solution.py:222
  58.8 3.8 %collective-permute-start.9 = (bf16[512,768]{1,0:T(8,128)(2,1)S(1)}, bf16[512,768]{1,0:T(8,128)(2,1)S(1)}, u32[]{:S(2)}, u32[]{:S(2)}) collective-permute-start(bf16[512,768]{1,0:T(8,128)(2,1)S(1)} %collective-permute-done.7.refs_9_), channel_id=1, source_target_pairs={{0,2},{1,7},{2,4},{3,1},{4,6},{5,3},{6,0},{7,5},{8,10},{9,15},{10,... | collective-permute-start | bytes 2359304 | tf_op jit(solution)/shard_map/ppermute | solution.py:36
  63.5 12.2 %collective-permute-done.36.refs_40_ = bf16[768,512]{1,0:T(8,128)(2,1)S(1)} collective-permute-done((bf16[768,512]{1,0:T(8,128)(2,1)S(1)}, bf16[768,512]{1,0:T(8,128)(2,1)S(1)}, u32[]{:S(2)}, u32[]{:S(2)}) %collective-permute-start.36) | collective-permute-done | bytes 786464 | tf_op jit(solution)/shard_map/ppermute | solution.py:222
  75.7 3.8 %collective-permute-start.3 = (bf16[512,768]{1,0:T(8,128)(2,1)S(1)}, bf16[512,768]{1,0:T(8,128)(2,1)S(1)}, u32[]{:S(2)}, u32[]{:S(2)}) collective-permute-start(bf16[512,768]{1,0:T(8,128)(2,1)S(1)} %collective-permute-done.1.refs_3_), channel_id=1, source_target_pairs={{0,2},{1,7},{2,4},{3,1},{4,6},{5,3},{6,0},{7,5},{8,10},{9,15},{10,... | collective-permute-start | bytes 2359304 | tf_op jit(solution)/shard_map/ppermute | solution.py:36
  84.0 2.5 collective-permute-start.2
  88.4 2.7 collective-permute-start.39
  93.4 3.4 %collective-permute-done.8.refs_10_ = bf16[512,768]{1,0:T(8,128)(2,1)S(1)} collective-permute-done((bf16[512,768]{1,0:T(8,128)(2,1)S(1)}, bf16[512,768]{1,0:T(8,128)(2,1)S(1)}, u32[]{:S(2)}, u32[]{:S(2)}) %collective-permute-start.8) | collective-permute-done | bytes 786464 | tf_op jit(solution)/shard_map/ppermute | solution.py:36
  96.8 2.7 collective-permute-start.38
  101.9 3.4 %collective-permute-done.2.refs_4_ = bf16[512,768]{1,0:T(8,128)(2,1)S(1)} collective-permute-done((bf16[512,768]{1,0:T(8,128)(2,1)S(1)}, bf16[512,768]{1,0:T(8,128)(2,1)S(1)}, u32[]{:S(2)}, u32[]{:S(2)}) %collective-permute-start.2) | collective-permute-done | bytes 786464 | tf_op jit(solution)/shard_map/ppermute | solution.py:36
  105.2 2.2 collective-permute-start.25
  107.4 1.7 collective-permute-start.11
  110.1 2.1 collective-permute-start.19
  112.2 4.7 %collective-permute-done.38.refs_42_ = bf16[768,512]{1,0:T(8,128)(2,1)S(1)} collective-permute-done((bf16[768,512]{1,0:T(8,128)(2,1)S(1)}, bf16[768,512]{1,0:T(8,128)(2,1)S(1)}, u32[]{:S(2)}, u32[]{:S(2)}) %collective-permute-start.38) | collective-permute-done | bytes 786464 | tf_op jit(solution)/shard_map/ppermute | solution.py:36
  116.9 3.1 %collective-permute-start.5 = (bf16[512,768]{1,0:T(8,128)(2,1)S(1)}, bf16[512,768]{1,0:T(8,128)(2,1)S(1)}, u32[]{:S(2)}, u32[]{:S(2)}) collective-permute-start(bf16[512,768]{1,0:T(8,128)(2,1)S(1)} %collective-permute-done.3.refs_5_), channel_id=1, source_target_pairs={{0,2},{1,7},{2,4},{3,1},{4,6},{5,3},{6,0},{7,5},{8,10},{9,15},{10,... | collective-permute-start | bytes 2359304 | tf_op jit(solution)/shard_map/ppermute | solution.py:36
  121.0 4.3 %collective-permute-done.32.refs_36_ = bf16[768,512]{1,0:T(8,128)(2,1)S(1)} collective-permute-done((bf16[768,512]{1,0:T(8,128)(2,1)S(1)}, bf16[768,512]{1,0:T(8,128)(2,1)S(1)}, u32[]{:S(2)}, u32[]{:S(2)}) %collective-permute-start.32) | collective-permute-done | bytes 786464 | tf_op jit(solution)/shard_map/ppermute | solution.py:36
  125.3 3.7 %collective-permute-start.24 = (bf16[512,768]{1,0:T(8,128)(2,1)S(1)}, bf16[512,768]{1,0:T(8,128)(2,1)S(1)}, u32[]{:S(2)}, u32[]{:S(2)}) collective-permute-start(bf16[512,768]{1,0:T(8,128)(2,1)S(1)} %collective-permute-done.8.refs_10_), channel_id=1, source_target_pairs={{0,1},{1,0},{2,3},{3,2},{4,5},{5,4},{6,7},{7,6},{8,9},{9,8},{10,11... | collective-permute-start | bytes 2359304 | tf_op jit(solution)/shard_map/ppermute | solution.py:224
  129.9 1.7 collective-permute-start.10
  133.5 1.2 collective-permute-start.4
  135.6 1.5 collective-permute-start.41
  139.4 1.8 collective-permute-done.10.refs_12_
  141.2 1.5 collective-permute-start.40
  144.9 4.7 %collective-permute-done.4.refs_6_ = bf16[512,768]{1,0:T(8,128)(2,1)} collective-permute-done((bf16[512,768]{1,0:T(8,128)(2,1)S(1)}, bf16[512,768]{1,0:T(8,128)(2,1)}, u32[]{:S(2)}, u32[]{:S(2)}) %collective-permute-start.4) | collective-permute-done | bytes 786464 | tf_op jit(solution)/shard_map/ppermute | solution.py:36
  149.6 2.1 collective-permute-start.27
  153.5 1.8 collective-permute-done.35.refs_39_
  155.2 1.4 collective-permute-start.21
  157.5 6.2 %collective-permute-done.40.refs_44_ = bf16[768,512]{1,0:T(8,128)(2,1)} collective-permute-done((bf16[768,512]{1,0:T(8,128)(2,1)S(1)}, bf16[768,512]{1,0:T(8,128)(2,1)}, u32[]{:S(2)}, u32[]{:S(2)}) %collective-permute-start.40) | collective-permute-done | bytes 786464 | tf_op jit(solution)/shard_map/ppermute | solution.py:36
  163.7 1.4 collective-permute-start.26
  165.0 7.0 %collective-permute-done.34.refs_38_ = bf16[768,512]{1,0:T(8,128)(2,1)S(1)} collective-permute-done((bf16[768,512]{1,0:T(8,128)(2,1)S(1)}, bf16[768,512]{1,0:T(8,128)(2,1)S(1)}, u32[]{:S(2)}, u32[]{:S(2)}) %collective-permute-start.34) | collective-permute-done | bytes 786464 | tf_op jit(solution)/shard_map/ppermute | solution.py:36
  174.3 2.0 collective-permute-start.20
  178.9 4.3 %collective-permute-done.12.refs_14_ = bf16[512,768]{1,0:T(8,128)(2,1)} collective-permute-done((bf16[512,768]{1,0:T(8,128)(2,1)S(1)}, bf16[512,768]{1,0:T(8,128)(2,1)}, u32[]{:S(2)}, u32[]{:S(2)}) %collective-permute-start.12) | collective-permute-done | bytes 786464 | tf_op jit(solution)/shard_map/ppermute | solution.py:36
  183.2 3.4 %collective-permute-start.28 = (bf16[512,768]{1,0:T(8,128)(2,1)}, bf16[512,768]{1,0:T(8,128)(2,1)}, u32[]{:S(2)}, u32[]{:S(2)}) collective-permute-start(bf16[512,768]{1,0:T(8,128)(2,1)} %collective-permute-done.12.refs_14_), channel_id=1, source_target_pairs={{0,1},{1,0},{2,3},{3,2},{4,5},{5,4},{6,7},{7,6},{8,9},{9,8},{10,11... | collective-permute-start | bytes 2359304 | tf_op jit(solution)/shard_map/ppermute | solution.py:224
  187.5 1.9 fusion.2
  189.5 6.7 %collective-permute-done.42.refs_46_ = bf16[768,512]{1,0:T(8,128)(2,1)} collective-permute-done((bf16[768,512]{1,0:T(8,128)(2,1)}, bf16[768,512]{1,0:T(8,128)(2,1)}, u32[]{:S(2)}, u32[]{:S(2)}) %collective-permute-start.42) | collective-permute-done | bytes 786464 | tf_op jit(solution)/shard_map/ppermute | solution.py:36
  196.2 1.1 copy-done.1
  197.3 1.1 copy-done.3
  200.7 1.1 copy-done.9
  201.9 1.1 copy-done.11
  227.9 30.2 %shard_map.67 = bf16[1024,512]{1,0:T(8,128)(2,1)} custom-call(s32[32]{0:T(128)S(1)} %reshape_squeeze.3.table_ref, bf16[512,768]{1,0:T(8,128)(2,1)S(1)} %get-tuple-element.6.refs_0_, bf16[512,768]{1,0:T(8,128)(2,1)S(1)} %get-tuple-element.5.refs_1_, bf16[512,768]{1,0:T(8,128)(2,1)S(1)} %copy-done.11, bf16[512,768]{1,0:T(8,128)(2,1)S(1)} %copy-done.5, ...), custom_call_target="tpu_custom_call" | custom-call | flops 12884901888 | bytes 37748736 | tf_op jit(solution)/shard_map/pallas_call | solution.py:186
  258.1 22.6 %all_to_all.19 = bf16[16,64,512]{2,1,0:T(8,128)(2,1)S(1)} all-to-all(bf16[16,64,512]{2,1,0:T(8,128)(2,1)} %bitcast.9), channel_id=1, replica_groups=mesh['xh'=2,'y'=4,'xl'=2,'z'=4,'c'=2] {'xl','z','c'}, dimensions={0} | all-to-all | bytes 2097152 | tf_op jit(solution)/shard_map/all_to_all | solution.py:233
  (178 shorter events, 62.1 us)
Async XLA Ops:
  2.2 6.9 %collective-permute-start.15 = (bf16[512,768]{1,0:T(8,128)(2,1)S(1)}, bf16[512,768]{1,0:T(8,128)(2,1)S(1)}, u32[]{:S(2)}, u32[]{:S(2)}) collective-permute-start(bf16[512,768]{1,0:T(8,128)(2,1)S(1)} %get-tuple-element.5.refs_1_), channel_id=1, source_target_pairs={{0,1},{1,0},{2,3},{3,2},{4,5},{5,4},{6,7},{7,6},{8,9},{9,8},{10,11... | collective-permute-start | bytes 2359304 | tf_op jit(solution)/shard_map/ppermute | solution.py:224
  3.7 19.1 %collective-permute-start.7 = (bf16[512,768]{1,0:T(8,128)(2,1)S(1)}, bf16[512,768]{1,0:T(8,128)(2,1)S(1)}, u32[]{:S(2)}, u32[]{:S(2)}) collective-permute-start(bf16[512,768]{1,0:T(8,128)(2,1)S(1)} %get-tuple-element.5.refs_1_), channel_id=1, source_target_pairs={{0,8},{8,0},{1,9},{9,1},{2,10},{10,2},{3,11},{11,3},{4,12},{12,4},... | collective-permute-start | bytes 2359304 | tf_op jit(solution)/shard_map/ppermute | solution.py:219
  5.0 20.6 %collective-permute-start.1 = (bf16[512,768]{1,0:T(8,128)(2,1)S(1)}, bf16[512,768]{1,0:T(8,128)(2,1)S(1)}, u32[]{:S(2)}, u32[]{:S(2)}) collective-permute-start(bf16[512,768]{1,0:T(8,128)(2,1)S(1)} %get-tuple-element.5.refs_1_), channel_id=1, source_target_pairs={{0,2},{1,7},{2,4},{3,1},{4,6},{5,3},{6,0},{7,5},{8,10},{9,15},{10,... | collective-permute-start | bytes 2359304 | tf_op jit(solution)/shard_map/ppermute | solution.py:36
  8.8 177.9 %copy-start.57 = (s32[1024]{0:T(1024)S(1)}, s32[1024]{0:T(1024)}, u32[]{:S(2)}) copy-start(s32[1024]{0:T(1024)} %param.6) | copy-start | bytes 12292
  8.8 19.6 %collective-permute-start.14 = (bf16[512,768]{1,0:T(8,128)(2,1)S(1)}, bf16[512,768]{1,0:T(8,128)(2,1)S(1)}, u32[]{:S(2)}, u32[]{:S(2)}) collective-permute-start(bf16[512,768]{1,0:T(8,128)(2,1)S(1)} %get-tuple-element.6.refs_0_), channel_id=1, source_target_pairs={{0,1},{1,0},{2,3},{3,2},{4,5},{5,4},{6,7},{7,6},{8,9},{9,8},{10,11... | collective-permute-start | bytes 2359304 | tf_op jit(solution)/shard_map/ppermute | solution.py:224
  8.8 30.9 %collective-permute-start.6 = (bf16[512,768]{1,0:T(8,128)(2,1)S(1)}, bf16[512,768]{1,0:T(8,128)(2,1)S(1)}, u32[]{:S(2)}, u32[]{:S(2)}) collective-permute-start(bf16[512,768]{1,0:T(8,128)(2,1)S(1)} %get-tuple-element.6.refs_0_), channel_id=1, source_target_pairs={{0,8},{8,0},{1,9},{9,1},{2,10},{10,2},{3,11},{11,3},{4,12},{12,4},... | collective-permute-start | bytes 2359304 | tf_op jit(solution)/shard_map/ppermute | solution.py:219
  10.1 32.4 %collective-permute-start = (bf16[512,768]{1,0:T(8,128)(2,1)S(1)}, bf16[512,768]{1,0:T(8,128)(2,1)S(1)}, u32[]{:S(2)}, u32[]{:S(2)}) collective-permute-start(bf16[512,768]{1,0:T(8,128)(2,1)S(1)} %get-tuple-element.6.refs_0_), channel_id=1, source_target_pairs={{0,2},{1,7},{2,4},{3,1},{4,6},{5,3},{6,0},{7,5},{8,10},{9,15},{10,... | collective-permute-start | bytes 2359304 | tf_op jit(solution)/shard_map/ppermute | solution.py:36
  22.8 36.0 %collective-permute-start.37 = (bf16[768,512]{1,0:T(8,128)(2,1)S(1)}, bf16[768,512]{1,0:T(8,128)(2,1)S(1)}, u32[]{:S(2)}, u32[]{:S(2)}) collective-permute-start(bf16[768,512]{1,0:T(8,128)(2,1)S(1)} %get-tuple-element.3.refs_33_), channel_id=1, source_target_pairs={{0,64},{64,0},{1,65},{65,1},{2,66},{66,2},{3,67},{67,3},{4,68},{68... | collective-permute-start | bytes 2359304 | tf_op jit(solution)/shard_map/ppermute | solution.py:222
  25.7 37.8 %collective-permute-start.31 = (bf16[768,512]{1,0:T(8,128)(2,1)S(1)}, bf16[768,512]{1,0:T(8,128)(2,1)S(1)}, u32[]{:S(2)}, u32[]{:S(2)}) collective-permute-start(bf16[768,512]{1,0:T(8,128)(2,1)S(1)} %get-tuple-element.3.refs_33_), channel_id=1, source_target_pairs={{0,16},{1,49},{16,32},{17,1},{32,48},{33,17},{48,0},{49,33},{2,18}... | collective-permute-start | bytes 2359304 | tf_op jit(solution)/shard_map/ppermute | solution.py:36
  29.3 46.4 %collective-permute-start.36 = (bf16[768,512]{1,0:T(8,128)(2,1)S(1)}, bf16[768,512]{1,0:T(8,128)(2,1)S(1)}, u32[]{:S(2)}, u32[]{:S(2)}) collective-permute-start(bf16[768,512]{1,0:T(8,128)(2,1)S(1)} %get-tuple-element.4.refs_32_), channel_id=1, source_target_pairs={{0,64},{64,0},{1,65},{65,1},{2,66},{66,2},{3,67},{67,3},{4,68},{68... | collective-permute-start | bytes 2359304 | tf_op jit(solution)/shard_map/ppermute | solution.py:222
  39.7 40.7 %collective-permute-start.30 = (bf16[768,512]{1,0:T(8,128)(2,1)S(1)}, bf16[768,512]{1,0:T(8,128)(2,1)S(1)}, u32[]{:S(2)}, u32[]{:S(2)}) collective-permute-start(bf16[768,512]{1,0:T(8,128)(2,1)S(1)} %get-tuple-element.4.refs_32_), channel_id=1, source_target_pairs={{0,16},{1,49},{16,32},{17,1},{32,48},{33,17},{48,0},{49,33},{2,18}... | collective-permute-start | bytes 2359304 | tf_op jit(solution)/shard_map/ppermute | solution.py:36
  42.5 37.9 %collective-permute-start.23 = (bf16[512,768]{1,0:T(8,128)(2,1)S(1)}, bf16[512,768]{1,0:T(8,128)(2,1)S(1)}, u32[]{:S(2)}, u32[]{:S(2)}) collective-permute-start(bf16[512,768]{1,0:T(8,128)(2,1)S(1)} %collective-permute-done.7.refs_9_), channel_id=1, source_target_pairs={{0,1},{1,0},{2,3},{3,2},{4,5},{5,4},{6,7},{7,6},{8,9},{9,8},{10,11... | collective-permute-start | bytes 2359304 | tf_op jit(solution)/shard_map/ppermute | solution.py:224
  58.8 50.3 %copy-start.58 = (bf16[768,512]{1,0:T(8,128)(2,1)}, bf16[768,512]{1,0:T(8,128)(2,1)S(1)}, u32[]{:S(2)}) copy-start(bf16[768,512]{1,0:T(8,128)(2,1)S(1)} %collective-permute-done.37.refs_41_) | copy-start | bytes 2359300
  58.8 24.3 %collective-permute-start.9 = (bf16[512,768]{1,0:T(8,128)(2,1)S(1)}, bf16[512,768]{1,0:T(8,128)(2,1)S(1)}, u32[]{:S(2)}, u32[]{:S(2)}) collective-permute-start(bf16[512,768]{1,0:T(8,128)(2,1)S(1)} %collective-permute-done.7.refs_9_), channel_id=1, source_target_pairs={{0,2},{1,7},{2,4},{3,1},{4,6},{5,3},{6,0},{7,5},{8,10},{9,15},{10,... | collective-permute-start | bytes 2359304 | tf_op jit(solution)/shard_map/ppermute | solution.py:36
  63.5 19.7 %collective-permute-start.17 = (bf16[512,768]{1,0:T(8,128)(2,1)S(1)}, bf16[512,768]{1,0:T(8,128)(2,1)S(1)}, u32[]{:S(2)}, u32[]{:S(2)}) collective-permute-start(bf16[512,768]{1,0:T(8,128)(2,1)S(1)} %collective-permute-done.1.refs_3_), channel_id=1, source_target_pairs={{0,1},{1,0},{2,3},{3,2},{4,5},{5,4},{6,7},{7,6},{8,9},{9,8},{10,11... | collective-permute-start | bytes 2359304 | tf_op jit(solution)/shard_map/ppermute | solution.py:224
  75.7 12.7 %collective-permute-start.3 = (bf16[512,768]{1,0:T(8,128)(2,1)S(1)}, bf16[512,768]{1,0:T(8,128)(2,1)S(1)}, u32[]{:S(2)}, u32[]{:S(2)}) collective-permute-start(bf16[512,768]{1,0:T(8,128)(2,1)S(1)} %collective-permute-done.1.refs_3_), channel_id=1, source_target_pairs={{0,2},{1,7},{2,4},{3,1},{4,6},{5,3},{6,0},{7,5},{8,10},{9,15},{10,... | collective-permute-start | bytes 2359304 | tf_op jit(solution)/shard_map/ppermute | solution.py:36
  80.4 10.7 %collective-permute-start.22 = (bf16[512,768]{1,0:T(8,128)(2,1)S(1)}, bf16[512,768]{1,0:T(8,128)(2,1)S(1)}, u32[]{:S(2)}, u32[]{:S(2)}) collective-permute-start(bf16[512,768]{1,0:T(8,128)(2,1)S(1)} %collective-permute-done.6.refs_8_), channel_id=1, source_target_pairs={{0,1},{1,0},{2,3},{3,2},{4,5},{5,4},{6,7},{7,6},{8,9},{9,8},{10,11... | collective-permute-start | bytes 2359304 | tf_op jit(solution)/shard_map/ppermute | solution.py:224
  81.3 15.5 %collective-permute-start.8 = (bf16[512,768]{1,0:T(8,128)(2,1)S(1)}, bf16[512,768]{1,0:T(8,128)(2,1)S(1)}, u32[]{:S(2)}, u32[]{:S(2)}) collective-permute-start(bf16[512,768]{1,0:T(8,128)(2,1)S(1)} %collective-permute-done.6.refs_8_), channel_id=1, source_target_pairs={{0,2},{1,7},{2,4},{3,1},{4,6},{5,3},{6,0},{7,5},{8,10},{9,15},{10,... | collective-permute-start | bytes 2359304 | tf_op jit(solution)/shard_map/ppermute | solution.py:36
  83.1 16.4 %collective-permute-start.16 = (bf16[512,768]{1,0:T(8,128)(2,1)S(1)}, bf16[512,768]{1,0:T(8,128)(2,1)S(1)}, u32[]{:S(2)}, u32[]{:S(2)}) collective-permute-start(bf16[512,768]{1,0:T(8,128)(2,1)S(1)} %collective-permute-done.refs_2_), channel_id=1, source_target_pairs={{0,1},{1,0},{2,3},{3,2},{4,5},{5,4},{6,7},{7,6},{8,9},{9,8},{10,11... | collective-permute-start | bytes 2359304 | tf_op jit(solution)/shard_map/ppermute | solution.py:224
  84.0 21.2 %collective-permute-start.2 = (bf16[512,768]{1,0:T(8,128)(2,1)S(1)}, bf16[512,768]{1,0:T(8,128)(2,1)S(1)}, u32[]{:S(2)}, u32[]{:S(2)}) collective-permute-start(bf16[512,768]{1,0:T(8,128)(2,1)S(1)} %collective-permute-done.refs_2_), channel_id=1, source_target_pairs={{0,2},{1,7},{2,4},{3,1},{4,6},{5,3},{6,0},{7,5},{8,10},{9,15},{10,... | collective-permute-start | bytes 2359304 | tf_op jit(solution)/shard_map/ppermute | solution.py:36
  88.4 19.0 %collective-permute-start.39 = (bf16[768,512]{1,0:T(8,128)(2,1)S(1)}, bf16[768,512]{1,0:T(8,128)(2,1)S(1)}, u32[]{:S(2)}, u32[]{:S(2)}) collective-permute-start(bf16[768,512]{1,0:T(8,128)(2,1)S(1)} %collective-permute-done.37.refs_41_), channel_id=1, source_target_pairs={{0,16},{1,49},{16,32},{17,1},{32,48},{33,17},{48,0},{49,33},{2,18}... | collective-permute-start | bytes 2359304 | tf_op jit(solution)/shard_map/ppermute | solution.py:36
  92.0 18.1 %collective-permute-start.33 = (bf16[768,512]{1,0:T(8,128)(2,1)S(1)}, bf16[768,512]{1,0:T(8,128)(2,1)S(1)}, u32[]{:S(2)}, u32[]{:S(2)}) collective-permute-start(bf16[768,512]{1,0:T(8,128)(2,1)S(1)} %collective-permute-done.31.refs_35_), channel_id=1, source_target_pairs={{0,16},{1,49},{16,32},{17,1},{32,48},{33,17},{48,0},{49,33},{2,18}... | collective-permute-start | bytes 2359304 | tf_op jit(solution)/shard_map/ppermute | solution.py:36
  96.8 20.1 %collective-permute-start.38 = (bf16[768,512]{1,0:T(8,128)(2,1)S(1)}, bf16[768,512]{1,0:T(8,128)(2,1)S(1)}, u32[]{:S(2)}, u32[]{:S(2)}) collective-permute-start(bf16[768,512]{1,0:T(8,128)(2,1)S(1)} %collective-permute-done.36.refs_40_), channel_id=1, source_target_pairs={{0,16},{1,49},{16,32},{17,1},{32,48},{33,17},{48,0},{49,33},{2,18}... | collective-permute-start | bytes 2359304 | tf_op jit(solution)/shard_map/ppermute | solution.py:36
  100.5 24.8 %collective-permute-start.32 = (bf16[768,512]{1,0:T(8,128)(2,1)S(1)}, bf16[768,512]{1,0:T(8,128)(2,1)S(1)}, u32[]{:S(2)}, u32[]{:S(2)}) collective-permute-start(bf16[768,512]{1,0:T(8,128)(2,1)S(1)} %collective-permute-done.30.refs_34_), channel_id=1, source_target_pairs={{0,16},{1,49},{16,32},{17,1},{32,48},{33,17},{48,0},{49,33},{2,18}... | collective-permute-start | bytes 2359304 | tf_op jit(solution)/shard_map/ppermute | solution.py:36
  105.2 23.8 %collective-permute-start.25 = (bf16[512,768]{1,0:T(8,128)(2,1)S(1)}, bf16[512,768]{1,0:T(8,128)(2,1)S(1)}, u32[]{:S(2)}, u32[]{:S(2)}) collective-permute-start(bf16[512,768]{1,0:T(8,128)(2,1)S(1)} %collective-permute-done.9.refs_11_), channel_id=1, source_target_pairs={{0,1},{1,0},{2,3},{3,2},{4,5},{5,4},{6,7},{7,6},{8,9},{9,8},{10,11... | collective-permute-start | bytes 2359304 | tf_op jit(solution)/shard_map/ppermute | solution.py:224
  107.4 75.8 %copy-start.60 = (bf16[768,512]{1,0:T(8,128)(2,1)}, bf16[768,512]{1,0:T(8,128)(2,1)S(1)}, u32[]{:S(2)}) copy-start(bf16[768,512]{1,0:T(8,128)(2,1)S(1)} %collective-permute-done.39.refs_43_) | copy-start | bytes 2359300
  107.4 25.1 %collective-permute-start.11 = (bf16[512,768]{1,0:T(8,128)(2,1)S(1)}, bf16[512,768]{1,0:T(8,128)(2,1)S(1)}, u32[]{:S(2)}, u32[]{:S(2)}) collective-permute-start(bf16[512,768]{1,0:T(8,128)(2,1)S(1)} %collective-permute-done.9.refs_11_), channel_id=1, source_target_pairs={{0,2},{1,7},{2,4},{3,1},{4,6},{5,3},{6,0},{7,5},{8,10},{9,15},{10,... | collective-permute-start | bytes 2359304 | tf_op jit(solution)/shard_map/ppermute | solution.py:36
  110.1 22.5 %collective-permute-start.19 = (bf16[512,768]{1,0:T(8,128)(2,1)S(1)}, bf16[512,768]{1,0:T(8,128)(2,1)S(1)}, u32[]{:S(2)}, u32[]{:S(2)}) collective-permute-start(bf16[512,768]{1,0:T(8,128)(2,1)S(1)} %collective-permute-done.3.refs_5_), channel_id=1, source_target_pairs={{0,1},{1,0},{2,3},{3,2},{4,5},{5,4},{6,7},{7,6},{8,9},{9,8},{10,11... | collective-permute-start | bytes 2359304 | tf_op jit(solution)/shard_map/ppermute | solution.py:224
  116.9 69.8 %copy-start.61 = (bf16[768,512]{1,0:T(8,128)(2,1)}, bf16[768,512]{1,0:T(8,128)(2,1)S(1)}, u32[]{:S(2)}) copy-start(bf16[768,512]{1,0:T(8,128)(2,1)S(1)} %collective-permute-done.38.refs_42_) | copy-start | bytes 2359300
  116.9 18.7 %collective-permute-start.5 = (bf16[512,768]{1,0:T(8,128)(2,1)S(1)}, bf16[512,768]{1,0:T(8,128)(2,1)S(1)}, u32[]{:S(2)}, u32[]{:S(2)}) collective-permute-start(bf16[512,768]{1,0:T(8,128)(2,1)S(1)} %collective-permute-done.3.refs_5_), channel_id=1, source_target_pairs={{0,2},{1,7},{2,4},{3,1},{4,6},{5,3},{6,0},{7,5},{8,10},{9,15},{10,... | collective-permute-start | bytes 2359304 | tf_op jit(solution)/shard_map/ppermute | solution.py:36
  125.3 11.8 %collective-permute-start.24 = (bf16[512,768]{1,0:T(8,128)(2,1)S(1)}, bf16[512,768]{1,0:T(8,128)(2,1)S(1)}, u32[]{:S(2)}, u32[]{:S(2)}) collective-permute-start(bf16[512,768]{1,0:T(8,128)(2,1)S(1)} %collective-permute-done.8.refs_10_), channel_id=1, source_target_pairs={{0,1},{1,0},{2,3},{3,2},{4,5},{5,4},{6,7},{7,6},{8,9},{9,8},{10,11... | collective-permute-start | bytes 2359304 | tf_op jit(solution)/shard_map/ppermute | solution.py:224
  129.9 11.2 %collective-permute-start.10 = (bf16[512,768]{1,0:T(8,128)(2,1)S(1)}, bf16[512,768]{1,0:T(8,128)(2,1)S(1)}, u32[]{:S(2)}, u32[]{:S(2)}) collective-permute-start(bf16[512,768]{1,0:T(8,128)(2,1)S(1)} %collective-permute-done.8.refs_10_), channel_id=1, source_target_pairs={{0,2},{1,7},{2,4},{3,1},{4,6},{5,3},{6,0},{7,5},{8,10},{9,15},{10,... | collective-permute-start | bytes 2359304 | tf_op jit(solution)/shard_map/ppermute | solution.py:36
  132.5 10.1 %collective-permute-start.18 = (bf16[512,768]{1,0:T(8,128)(2,1)S(1)}, bf16[512,768]{1,0:T(8,128)(2,1)S(1)}, u32[]{:S(2)}, u32[]{:S(2)}) collective-permute-start(bf16[512,768]{1,0:T(8,128)(2,1)S(1)} %collective-permute-done.2.refs_4_), channel_id=1, source_target_pairs={{0,1},{1,0},{2,3},{3,2},{4,5},{5,4},{6,7},{7,6},{8,9},{9,8},{10,11... | collective-permute-start | bytes 2359304 | tf_op jit(solution)/shard_map/ppermute | solution.py:224
  133.5 16.1 %collective-permute-start.4 = (bf16[512,768]{1,0:T(8,128)(2,1)S(1)}, bf16[512,768]{1,0:T(8,128)(2,1)}, u32[]{:S(2)}, u32[]{:S(2)}) collective-permute-start(bf16[512,768]{1,0:T(8,128)(2,1)S(1)} %collective-permute-done.2.refs_4_), channel_id=1, source_target_pairs={{0,2},{1,7},{2,4},{3,1},{4,6},{5,3},{6,0},{7,5},{8,10},{9,15},{10,... | collective-permute-start | bytes 2359304 | tf_op jit(solution)/shard_map/ppermute | solution.py:36
  135.6 16.1 %collective-permute-start.41 = (bf16[768,512]{1,0:T(8,128)(2,1)S(1)}, bf16[768,512]{1,0:T(8,128)(2,1)}, u32[]{:S(2)}, u32[]{:S(2)}) collective-permute-start(bf16[768,512]{1,0:T(8,128)(2,1)S(1)} %collective-permute-done.39.refs_43_), channel_id=1, source_target_pairs={{0,16},{1,49},{16,32},{17,1},{32,48},{33,17},{48,0},{49,33},{2,18}... | collective-permute-start | bytes 2359304 | tf_op jit(solution)/shard_map/ppermute | solution.py:36
  138.0 17.2 %collective-permute-start.35 = (bf16[768,512]{1,0:T(8,128)(2,1)S(1)}, bf16[768,512]{1,0:T(8,128)(2,1)}, u32[]{:S(2)}, u32[]{:S(2)}) collective-permute-start(bf16[768,512]{1,0:T(8,128)(2,1)S(1)} %collective-permute-done.33.refs_37_), channel_id=1, source_target_pairs={{0,16},{1,49},{16,32},{17,1},{32,48},{33,17},{48,0},{49,33},{2,18}... | collective-permute-start | bytes 2359304 | tf_op jit(solution)/shard_map/ppermute | solution.py:36
  141.2 22.5 %collective-permute-start.40 = (bf16[768,512]{1,0:T(8,128)(2,1)S(1)}, bf16[768,512]{1,0:T(8,128)(2,1)}, u32[]{:S(2)}, u32[]{:S(2)}) collective-permute-start(bf16[768,512]{1,0:T(8,128)(2,1)S(1)} %collective-permute-done.38.refs_42_), channel_id=1, source_target_pairs={{0,16},{1,49},{16,32},{17,1},{32,48},{33,17},{48,0},{49,33},{2,18}... | collective-permute-start | bytes 2359304 | tf_op jit(solution)/shard_map/ppermute | solution.py:36
  143.6 28.4 %collective-permute-start.34 = (bf16[768,512]{1,0:T(8,128)(2,1)S(1)}, bf16[768,512]{1,0:T(8,128)(2,1)S(1)}, u32[]{:S(2)}, u32[]{:S(2)}) collective-permute-start(bf16[768,512]{1,0:T(8,128)(2,1)S(1)} %collective-permute-done.32.refs_36_), channel_id=1, source_target_pairs={{0,16},{1,49},{16,32},{17,1},{32,48},{33,17},{48,0},{49,33},{2,18}... | collective-permute-start | bytes 2359304 | tf_op jit(solution)/shard_map/ppermute | solution.py:36
  149.6 23.8 %collective-permute-start.27 = (bf16[512,768]{1,0:T(8,128)(2,1)S(1)}, bf16[512,768]{1,0:T(8,128)(2,1)S(1)}, u32[]{:S(2)}, u32[]{:S(2)}) collective-permute-start(bf16[512,768]{1,0:T(8,128)(2,1)S(1)} %collective-permute-done.11.refs_13_), channel_id=1, source_target_pairs={{0,1},{1,0},{2,3},{3,2},{4,5},{5,4},{6,7},{7,6},{8,9},{9,8},{10,11... | collective-permute-start | bytes 2359304 | tf_op jit(solution)/shard_map/ppermute | solution.py:224
  151.7 24.6 %collective-permute-start.13 = (bf16[512,768]{1,0:T(8,128)(2,1)S(1)}, bf16[512,768]{1,0:T(8,128)(2,1)}, u32[]{:S(2)}, u32[]{:S(2)}) collective-permute-start(bf16[512,768]{1,0:T(8,128)(2,1)S(1)} %collective-permute-done.11.refs_13_), channel_id=1, source_target_pairs={{0,2},{1,7},{2,4},{3,1},{4,6},{5,3},{6,0},{7,5},{8,10},{9,15},{10,... | collective-permute-start | bytes 2359304 | tf_op jit(solution)/shard_map/ppermute | solution.py:36
  155.2 21.5 %collective-permute-start.21 = (bf16[512,768]{1,0:T(8,128)(2,1)S(1)}, bf16[512,768]{1,0:T(8,128)(2,1)S(1)}, u32[]{:S(2)}, u32[]{:S(2)}) collective-permute-start(bf16[512,768]{1,0:T(8,128)(2,1)S(1)} %collective-permute-done.5.refs_7_), channel_id=1, source_target_pairs={{0,1},{1,0},{2,3},{3,2},{4,5},{5,4},{6,7},{7,6},{8,9},{9,8},{10,11... | collective-permute-start | bytes 2359304 | tf_op jit(solution)/shard_map/ppermute | solution.py:224
  163.7 14.3 %collective-permute-start.26 = (bf16[512,768]{1,0:T(8,128)(2,1)S(1)}, bf16[512,768]{1,0:T(8,128)(2,1)S(1)}, u32[]{:S(2)}, u32[]{:S(2)}) collective-permute-start(bf16[512,768]{1,0:T(8,128)(2,1)S(1)} %collective-permute-done.10.refs_12_), channel_id=1, source_target_pairs={{0,1},{1,0},{2,3},{3,2},{4,5},{5,4},{6,7},{7,6},{8,9},{9,8},{10,11... | collective-permute-start | bytes 2359304 | tf_op jit(solution)/shard_map/ppermute | solution.py:224
  172.0 11.2 %collective-permute-start.12 = (bf16[512,768]{1,0:T(8,128)(2,1)S(1)}, bf16[512,768]{1,0:T(8,128)(2,1)}, u32[]{:S(2)}, u32[]{:S(2)}) collective-permute-start(bf16[512,768]{1,0:T(8,128)(2,1)S(1)} %collective-permute-done.10.refs_12_), channel_id=1, source_target_pairs={{0,2},{1,7},{2,4},{3,1},{4,6},{5,3},{6,0},{7,5},{8,10},{9,15},{10,... | collective-permute-start | bytes 2359304 | tf_op jit(solution)/shard_map/ppermute | solution.py:36
  174.3 15.2 %collective-permute-start.20 = (bf16[512,768]{1,0:T(8,128)(2,1)}, bf16[512,768]{1,0:T(8,128)(2,1)}, u32[]{:S(2)}, u32[]{:S(2)}) collective-permute-start(bf16[512,768]{1,0:T(8,128)(2,1)} %collective-permute-done.4.refs_6_), channel_id=1, source_target_pairs={{0,1},{1,0},{2,3},{3,2},{4,5},{5,4},{6,7},{7,6},{8,9},{9,8},{10,11... | collective-permute-start | bytes 2359304 | tf_op jit(solution)/shard_map/ppermute | solution.py:224
  176.3 13.1 %collective-permute-start.43 = (bf16[768,512]{1,0:T(8,128)(2,1)}, bf16[768,512]{1,0:T(8,128)(2,1)}, u32[]{:S(2)}, u32[]{:S(2)}) collective-permute-start(bf16[768,512]{1,0:T(8,128)(2,1)} %collective-permute-done.41.refs_45_), channel_id=1, source_target_pairs={{0,16},{1,49},{16,32},{17,1},{32,48},{33,17},{48,0},{49,33},{2,18}... | collective-permute-start | bytes 2359304 | tf_op jit(solution)/shard_map/ppermute | solution.py:36
  177.6 18.5 %collective-permute-start.42 = (bf16[768,512]{1,0:T(8,128)(2,1)}, bf16[768,512]{1,0:T(8,128)(2,1)}, u32[]{:S(2)}, u32[]{:S(2)}) collective-permute-start(bf16[768,512]{1,0:T(8,128)(2,1)} %collective-permute-done.40.refs_44_), channel_id=1, source_target_pairs={{0,16},{1,49},{16,32},{17,1},{32,48},{33,17},{48,0},{49,33},{2,18}... | collective-permute-start | bytes 2359304 | tf_op jit(solution)/shard_map/ppermute | solution.py:36
  178.9 17.3 %collective-permute-start.29 = (bf16[512,768]{1,0:T(8,128)(2,1)}, bf16[512,768]{1,0:T(8,128)(2,1)}, u32[]{:S(2)}, u32[]{:S(2)}) collective-permute-start(bf16[512,768]{1,0:T(8,128)(2,1)} %collective-permute-done.13.refs_15_), channel_id=1, source_target_pairs={{0,1},{1,0},{2,3},{3,2},{4,5},{5,4},{6,7},{7,6},{8,9},{9,8},{10,11... | collective-permute-start | bytes 2359304 | tf_op jit(solution)/shard_map/ppermute | solution.py:224
  183.2 13.0 %collective-permute-start.28 = (bf16[512,768]{1,0:T(8,128)(2,1)}, bf16[512,768]{1,0:T(8,128)(2,1)}, u32[]{:S(2)}, u32[]{:S(2)}) collective-permute-start(bf16[512,768]{1,0:T(8,128)(2,1)} %collective-permute-done.12.refs_14_), channel_id=1, source_target_pairs={{0,1},{1,0},{2,3},{3,2},{4,5},{5,4},{6,7},{7,6},{8,9},{9,8},{10,11... | collective-permute-start | bytes 2359304 | tf_op jit(solution)/shard_map/ppermute | solution.py:224
  (59 other events, 124.4 us)

commit v2 on v1

v2 whole, which is shorter than its diff:
```python
import math

import jax
import jax.numpy as jnp
import numpy as np
from jax import lax
from jax.experimental import pallas as pl
from jax.experimental.pallas import tpu as pltpu
from jax.sharding import Mesh
from jax.sharding import PartitionSpec as P

HEAD_WIDTH = 128
QUERY_HEADS = 48
KEY_VALUE_HEADS = 8

rope_base = 1000000.0
SWAP = ((0, 1), (1, 0))


def rotary_tables(positions, head_size):
    half_size = head_size // 2
    column_ids = jnp.arange(head_size, dtype=jnp.int32)
    exponent = (column_ids % half_size).astype(jnp.float32) * (
        -2.0 * math.log(rope_base) / head_size
    )
    frequency = jnp.exp(exponent)
    angles = positions.astype(jnp.float32)[:, None] * frequency[None, :]
    sign_table = jnp.where(column_ids < half_size, -1.0, 1.0).astype(jnp.float32)
    return (jnp.cos(angles), jnp.sin(angles) * sign_table[None, :])


def ring_step(block, axis, way=1):
    pairs = [
        (i * 2 + c, ((i + (1, -1)[c] * way) % 4) * 2 + c) for i in range(4) for c in range(2)
    ]
    return lax.ppermute(block, (axis, "c"), pairs)


def piece_table():
    table = np.zeros((2, 4, 2, 4, 2, 8, 2), np.int32)
    for xh, y, xl, z, c in np.ndindex(2, 4, 2, 4, 2):
        way = (1, -1)[c]
        places = (0, -way, way, 2)
        a_blocks = {(xl ^ p, (z + d) % 4): p * 4 + i for p in range(2) for i, d in enumerate(places)}
        b_blocks = {(xh ^ p, (y + d) % 4): p * 4 + i for p in range(2) for i, d in enumerate(places)}
        pairs = [(a_blocks[f], b_blocks[f]) for f in np.ndindex(2, 4)]
        table[xh, y, xl, z, c] = sorted(pairs, key=lambda p: (7 in p, max(p), p))
    return table


TABLE = piece_table()
EARLY = 6


def product(table, core, first, count, a_blocks, b_blocks, total=None, tables=None):
    rows = sum(v.shape[0] for v in a_blocks[0][0])
    half = a_blocks[0][0][0].shape[1]
    depth, columns = 2 * half, b_blocks[0][0].shape[1]
    slots = 2
    tile = 256
    last = tables is not None
    used_a = [p for p in range(len(a_blocks)) if a_blocks[p] is not None]
    used_b = [q for q in range(len(b_blocks)) if b_blocks[q] is not None]

    def kernel(table_ref, *refs):
        refs = list(refs)
        a_refs = {p: [[refs.pop(0) for _ in part] for part in a_blocks[p]] for p in used_a}
        b_refs = {q: [refs.pop(0) for _ in b_blocks[q]] for q in used_b}
        if total is not None:
            total_ref = refs.pop(0)
        if last:
            cos_ref, sin_ref = refs.pop(0), refs.pop(0)
        out_ref, a_buf, b_buf, *rest, sems = refs
        acc = rest[0] if last else out_ref
        me = table_ref[16]

        def start(k):
            slot = lax.rem(k, slots)
            a_id = table_ref[(first + k) * 2]
            b_id = table_ref[(first + k) * 2 + 1]
            for p in used_a:

                @pl.when(a_id == p)
                def _():
                    for part in range(2):
                        own = me if part == 0 else 1 - me
                        span = pl.ds(pl.multiple_of(own * half, half), half)
                        row = 0
                        for ref in a_refs[p][part]:
                            pltpu.make_async_copy(
                                ref, a_buf.at[slot, pl.ds(row, ref.shape[0]), span], sems.at[slot]
                            ).start()
                            row += ref.shape[0]

            for q in used_b:

                @pl.when(b_id == q)
                def _():
                    row = 0
                    for ref in b_refs[q]:
                        pltpu.make_async_copy(
                            ref, b_buf.at[slot, pl.ds(row, ref.shape[0]), :], sems.at[slot]
                        ).start()
                        row += ref.shape[0]

        def wait(k):
            slot = lax.rem(k, slots)
            pltpu.make_async_copy(a_buf.at[slot], a_buf.at[slot], sems.at[slot]).wait()
            pltpu.make_async_copy(b_buf.at[slot], b_buf.at[slot], sems.at[slot]).wait()

        def spans(body):
            @pl.loop(0, rows // tile)
            def _(i):
                body(pl.ds(pl.multiple_of(i * tile, tile), tile))

        start(0)
        if total is None:
            acc[...] = jnp.zeros(acc.shape, jnp.float32)
        elif last:
            acc[...] = total_ref[...]

        @pl.loop(0, count)
        def _(k):
            @pl.when(k + 1 < count)
            def _():
                start(k + 1)

            wait(k)
            slot = lax.rem(k, slots)
            acc[...] += jnp.dot(a_buf[slot], b_buf[slot], preferred_element_type=jnp.float32)

        def turn(span):
            cosine, sine = cos_ref[span, :], sin_ref[span, :]
            for h in range(columns // HEAD_WIDTH):
                head = acc[span, h * HEAD_WIDTH : (h + 1) * HEAD_WIDTH]
                swapped = pltpu.roll(head, HEAD_WIDTH // 2, 1)
                out_ref[span, h * HEAD_WIDTH : (h + 1) * HEAD_WIDTH] = (
                    head * cosine + swapped * sine
                ).astype(jnp.bfloat16)

        if last:
            spans(turn)

    anywhere = pl.BlockSpec(memory_space=pl.ANY)
    vmem = pl.BlockSpec(memory_space=pltpu.VMEM)
    pieces = [v for p in used_a for part in a_blocks[p] for v in part]
    pieces += [v for q in used_b for v in b_blocks[q]]
    operands = [jnp.concatenate([table.reshape(-1), core.reshape(1)])]
    operands += [pltpu.with_memory_space_constraint(v, pltpu.HBM) for v in pieces]
    in_specs = [pl.BlockSpec(memory_space=pltpu.SMEM)] + [anywhere] * len(pieces)
    if total is not None:
        operands.append(total)
        in_specs.append(vmem)
    if last:
        operands += tables
        in_specs += [vmem] * 2
    scratch = [
        pltpu.VMEM((slots, rows, depth), pieces[0].dtype),
        pltpu.VMEM((slots, depth, columns), pieces[0].dtype),
    ]
    if last:
        scratch.append(pltpu.VMEM((rows, columns), jnp.float32))
    return pl.pallas_call(
        kernel,
        out_shape=jax.ShapeDtypeStruct((rows, columns), jnp.bfloat16 if last else jnp.float32),
        in_specs=in_specs,
        out_specs=vmem,
        scratch_shapes=scratch + [pltpu.SemaphoreType.DMA((slots,))],
        compiler_params=pltpu.CompilerParams(vmem_limit_bytes=28 * 1024 * 1024),
        cost_estimate=pl.CostEstimate(
            flops=2 * rows * columns * depth * count,
            bytes_accessed=(rows + columns) * depth * 2 * count,
            transcendentals=0,
        ),
    )(*operands)


def after(block, *before):
    return lax.optimization_barrier((block,) + before)[0]


def swap(block, axis):
    return lax.ppermute(block, axis, SWAP)


def gathers(a, b):
    a_part, b_part = a.shape[0] // 2, b.shape[0] // 2
    a_0, a_1, b_0, b_1 = a[:a_part], a[a_part:], b[:b_part], b[b_part:]

    z_near, z_other = ring_step(a, "z"), ring_step(a, "z", -1)
    y_near, y_other = ring_step(b, "y"), ring_step(b, "y", -1)
    p_0 = swap(a_0, "xl")
    r_0 = swap(after(b_0, p_0), "xh")

    p_0_in = after(p_0, z_near, z_other, r_0)
    r_0_in = after(r_0, y_near, y_other)
    p_0_near, p_0_other = ring_step(p_0_in, "z"), ring_step(p_0_in, "z", -1)
    r_0_near, r_0_other = ring_step(r_0_in, "y"), ring_step(r_0_in, "y", -1)
    p_1 = swap(after(a_1, z_near, z_other, y_near, y_other), "xl")
    r_1 = swap(after(b_1, p_1), "xh")

    z_far = ring_step(after(z_near, p_0_near, p_0_other), "z")
    y_far = ring_step(after(y_near, r_0_near, r_0_other), "y")
    a_c = swap(after(a, p_0_near, p_0_other, r_0_near, r_0_other), "c")
    z_near_c = swap(after(z_near, a_c), "c")
    z_other_c = swap(after(z_other, z_near_c), "c")

    p_1_in = after(p_1, z_far, r_1)
    r_1_in = after(r_1, y_far)
    p_1_near, p_1_other = ring_step(p_1_in, "z"), ring_step(p_1_in, "z", -1)
    r_1_near, r_1_other = ring_step(r_1_in, "y"), ring_step(r_1_in, "y", -1)
    p_0_c = swap(after(p_0, z_far, y_far), "c")
    p_0_near_c = swap(after(p_0_near, p_0_c), "c")
    p_0_other_c = swap(after(p_0_other, p_0_near_c), "c")
    z_far_c = swap(after(z_far, p_0_other_c), "c")

    p_0_far = ring_step(after(p_0_near, p_1_near, p_1_other), "z")
    r_0_far = ring_step(after(r_0_near, r_1_near, r_1_other), "y")
    p_1_far = ring_step(p_1_near, "z")
    r_1_far = ring_step(r_1_near, "y")
    p_1_c = swap(after(p_1, p_1_near, p_1_other, r_1_near, r_1_other), "c")
    p_1_near_c = swap(after(p_1_near, p_1_c), "c")
    p_1_other_c = swap(after(p_1_other, p_1_near_c), "c")
    p_0_far_c = swap(p_0_far, "c")
    p_1_far_c = swap(p_1_far, "c")

    a_blocks = [
        ([a], [a_c]),
        ([z_near], [z_other_c]),
        ([z_other], [z_near_c]),
        ([z_far], [z_far_c]),
        ([p_0, p_1], [p_0_c, p_1_c]),
        ([p_0_near, p_1_near], [p_0_other_c, p_1_other_c]),
        ([p_0_other, p_1_other], [p_0_near_c, p_1_near_c]),
        ([p_0_far, p_1_far], [p_0_far_c, p_1_far_c]),
    ]
    b_blocks = [
        [b],
        [y_near],
        [y_other],
        [y_far],
        [r_0, r_1],
        [r_0_near, r_1_near],
        [r_0_other, r_1_other],
        [r_0_far, r_1_far],
    ]
    return a_blocks, b_blocks


def shards(tokens, joined_weight, positions):
    rows, depth = tokens.shape
    columns = joined_weight.shape[1]
    place = [lax.axis_index(a) for a in ("xh", "y", "xl", "z", "c")]
    table = jnp.asarray(TABLE)[tuple(place)]

    a_blocks, b_blocks = gathers(tokens, joined_weight)

    column_block = (place[2] * 4 + place[3]) * 2 + place[4]
    rotated = column_block * columns < (QUERY_HEADS + KEY_VALUE_HEADS) * HEAD_WIDTH
    cosine, sine = rotary_tables(positions, HEAD_WIDTH)
    tables = [jnp.where(rotated, cosine, 1.0), jnp.where(rotated, sine, 0.0)]

    early = product(table, place[4], 0, EARLY, a_blocks[:7] + [None], b_blocks[:7] + [None])
    turned = product(table, place[4], EARLY, 8 - EARLY, a_blocks, b_blocks, early, tables)
    received = lax.all_to_all(turned, ("xl", "z", "c"), split_axis=0, concat_axis=1, tiled=True)
    query_columns = QUERY_HEADS * HEAD_WIDTH
    rotated_columns = (QUERY_HEADS + KEY_VALUE_HEADS) * HEAD_WIDTH
    return (
        received[:, :query_columns],
        received[:, query_columns:rotated_columns],
        received[:, rotated_columns:],
    )


def solution(mesh):
    fine = Mesh(mesh.devices.reshape(2, 4, 2, 4, 2), ("xh", "y", "xl", "z", "c"))
    row, col = ("xh", "y"), ("xl", "z", "c")
    in_specs = (P(row, col), P(row, col), P(row))
    out_specs = (P(row + col, None),) * 3
    return jax.shard_map(shards, mesh=fine, in_specs=in_specs, out_specs=out_specs, check_vma=False)
```

time: 284 us -> 200 us (0.70)
  local copies, waits for them, and re-layouts: 61.2 us -> 6.52 us
  starting transfers between devices: 65.6 us -> 43.3 us
  Pallas kernels: 30.2 us -> 22.5 us
  waiting for transfers between devices: 100 us -> 106 us
  blocking collectives: 22.6 us -> 18.8 us
    unnamed x126 -> x52, local copies, waits for them, and re-layouts: 57 us -> 2.29 us
    ppermute x24 -> x18, starting transfers between devices: 41 us -> 24.1 us  [ring_step(): return lax.ppermute(block, (axis, 'c'), pairs)]
    ppermute x20 -> x16, waiting for transfers between devices: 51 us -> 61 us  [swap(): return lax.ppermute(block, axis, SWAP)]
    pallas_call x1 -> x2, Pallas kernels: 30.2 us -> 22.5 us  [product(): pl.pallas_call(kernel, out_shape=jax.ShapeDtypeStruct((rows, columns), jn...]
    ppermute x20 -> x16, starting transfers between devices: 24.6 us -> 19.1 us  [swap(): return lax.ppermute(block, axis, SWAP)]
    ppermute x24 -> x18, waiting for transfers between devices: 49.2 us -> 44.6 us  [ring_step(): return lax.ppermute(block, (axis, 'c'), pairs)]
    all_to_all x1, blocking collectives: 22.6 us -> 18.8 us  [shards(): lax.all_to_all(turned, ('xl', 'z', 'c'), split_axis=0, concat_axis=1, til...]
  transfers between devices with their start and end apart: 44 -> 34, of which waited for: 16 -> 15; matrix products, arithmetic and copies ran while one was open for 1% -> 1% of each run, Pallas kernels for 0% -> 8%
where the time goes in v2:
time: 200 us
  waiting for transfers between devices  106 us (53%)
  starting transfers between devices  43.3 us (22%)
  Pallas kernels  22.5 us (11%)
  blocking collectives  18.8 us (9%)
  local copies, waits for them, and re-layouts  6.52 us (3%)
  other arithmetic  2.03 us (1%)
    ppermute x16, waiting for transfers between devices, swap(): return lax.ppermute(block, axis, SWAP)  61 us
    ppermute x18, waiting for transfers between devices, ring_step(): return lax.ppermute(block, (axis, 'c'), pairs)  44.6 us
    ppermute x18, starting transfers between devices, ring_step(): return lax.ppermute(block, (axis, 'c'), pairs)  24.1 us
    pallas_call x2, Pallas kernels, product(): pl.pallas_call(kernel, out_shape=jax.ShapeDtypeStruct((rows, columns), jn...  22.5 us
    ppermute x16, starting transfers between devices, swap(): return lax.ppermute(block, axis, SWAP)  19.1 us
    all_to_all x1, blocking collectives, shards(): lax.all_to_all(turned, ('xl', 'z', 'c'), split_axis=0, concat_axis=1, til...  18.8 us
  transfers between devices with their start and end apart: 34, of which 15 were waited for; matrix products, arithmetic and copies ran while one was open for 1% of the time, Pallas kernels for 8%

profile of v2, /device:TPU:1, one launch (start us, length us, event | category | flops | bytes accessed | tf_op | source)
XLA Modules:
  0.0 199.6 jit_solution(12143222917718417506)
XLA Ops:
  0.7 1.6 fusion.7
  2.3 2.1 %collective-permute-start = (bf16[512,768]{1,0:T(8,128)(2,1)S(1)}, bf16[512,768]{1,0:T(8,128)(2,1)S(1)}, u32[]{:S(2)}, u32[]{:S(2)}) collective-permute-start(bf16[512,768]{1,0:T(8,128)(2,1)S(1)} %get-tuple-element.48), channel_id=1, source_target_pairs={{0,8},{8,0},{1,9},{9,1},{2,10},{10,2},{3,11},{11,3},{4,12},{12,4},... | collective-permute-start | bytes 2359304 | tf_op jit(solution)/shard_map/ppermute | solution.py:183
  4.4 1.3 collective-permute-start.7
  5.7 1.4 collective-permute-start.6
  7.2 1.6 collective-permute-start.2
  8.8 2.1 %collective-permute-start.1 = (bf16[1024,768]{1,0:T(8,128)(2,1)S(1)}, bf16[1024,768]{1,0:T(8,128)(2,1)S(1)}, u32[]{:S(2)}, u32[]{:S(2)}) collective-permute-start(bf16[1024,768]{1,0:T(8,128)(2,1)S(1)} %copy-done), channel_id=1, source_target_pairs={{0,2},{1,7},{2,4},{3,1},{4,6},{5,3},{6,0},{7,5},{8,10},{9,15},{10,... | collective-permute-start | bytes 4718600 | tf_op jit(solution)/shard_map/ppermute | solution.py:36
  11.0 10.2 %collective-permute-done.refs_8_ = bf16[512,768]{1,0:T(8,128)(2,1)S(1)} collective-permute-done((bf16[512,768]{1,0:T(8,128)(2,1)S(1)}, bf16[512,768]{1,0:T(8,128)(2,1)S(1)}, u32[]{:S(2)}, u32[]{:S(2)}) %collective-permute-start) | collective-permute-done | bytes 786464 | tf_op jit(solution)/shard_map/ppermute | solution.py:183
  21.3 3.2 %collective-permute-start.3 = (bf16[768,512]{1,0:T(8,128)(2,1)S(1)}, bf16[768,512]{1,0:T(8,128)(2,1)S(1)}, u32[]{:S(2)}, u32[]{:S(2)}) collective-permute-start(bf16[768,512]{1,0:T(8,128)(2,1)S(1)} %get-tuple-element.24), channel_id=1, source_target_pairs={{0,64},{64,0},{1,65},{65,1},{2,66},{66,2},{3,67},{67,3},{4,68},{68... | collective-permute-start | bytes 2359304 | tf_op jit(solution)/shard_map/ppermute | solution.py:183
  24.5 16.2 %collective-permute-done.3.refs_24_.refs_28_ = bf16[768,512]{1,0:T(8,128)(2,1)S(1)} collective-permute-done((bf16[768,512]{1,0:T(8,128)(2,1)S(1)}, bf16[768,512]{1,0:T(8,128)(2,1)S(1)}, u32[]{:S(2)}, u32[]{:S(2)}) %collective-permute-start.3) | collective-permute-done | bytes 786464 | tf_op jit(solution)/shard_map/ppermute | solution.py:183
  40.6 1.5 collective-permute-done.6.refs_21_.refs_25_
  42.1 1.3 collective-permute-start.9
  43.4 1.4 collective-permute-start.8
  45.3 1.6 collective-permute-start.5
  46.9 1.8 collective-permute-start.4
  48.7 9.6 %collective-permute-done.9.refs_28_.refs_32_ = bf16[768,512]{1,0:T(8,128)(2,1)S(1)} collective-permute-done((bf16[768,512]{1,0:T(8,128)(2,1)S(1)}, bf16[768,512]{1,0:T(8,128)(2,1)S(1)}, u32[]{:S(2)}, u32[]{:S(2)}) %collective-permute-start.9) | collective-permute-done | bytes 786464 | tf_op jit(solution)/shard_map/ppermute | solution.py:36
  58.3 4.7 %collective-permute-done.8.refs_26_.refs_30_ = bf16[768,512]{1,0:T(8,128)(2,1)} collective-permute-done((bf16[768,512]{1,0:T(8,128)(2,1)S(1)}, bf16[768,512]{1,0:T(8,128)(2,1)}, u32[]{:S(2)}, u32[]{:S(2)}) %collective-permute-start.8) | collective-permute-done | bytes 786464 | tf_op jit(solution)/shard_map/ppermute | solution.py:36
  63.0 0.9 collective-permute-start.14
  63.9 2.6 %collective-permute-done.4.refs_12_ = bf16[512,768]{1,0:T(8,128)(2,1)} collective-permute-done((bf16[512,768]{1,0:T(8,128)(2,1)S(1)}, bf16[512,768]{1,0:T(8,128)(2,1)}, u32[]{:S(2)}, u32[]{:S(2)}) %collective-permute-start.4) | collective-permute-done | bytes 786464 | tf_op jit(solution)/shard_map/ppermute | solution.py:36
  66.5 1.2 collective-permute-start.13
  67.7 1.3 collective-permute-start.10
  69.0 17.2 %collective-permute-done.19.refs_9_ = bf16[512,768]{1,0:T(8,128)(2,1)S(1)} collective-permute-done((bf16[512,768]{1,0:T(8,128)(2,1)S(1)}, bf16[512,768]{1,0:T(8,128)(2,1)S(1)}, u32[]{:S(2)}, u32[]{:S(2)}) %collective-permute-start.19) | collective-permute-done | bytes 786464 | tf_op jit(solution)/shard_map/ppermute | solution.py:183
  86.1 1.8 collective-permute-start.20
  87.9 2.2 %collective-permute-start.15 = (bf16[512,768]{1,0:T(8,128)(2,1)S(1)}, bf16[512,768]{1,0:T(8,128)(2,1)S(1)}, u32[]{:S(2)}, u32[]{:S(2)}) collective-permute-start(bf16[512,768]{1,0:T(8,128)(2,1)S(1)} %collective-permute-done.refs_8_), channel_id=1, source_target_pairs={{0,1},{1,0},{2,3},{3,2},{4,5},{5,4},{6,7},{7,6},{8,9},{9,8},{10,11... | collective-permute-start | bytes 2359304 | tf_op jit(solution)/shard_map/ppermute | solution.py:183
  90.1 15.0 %collective-permute-done.20.refs_25_.refs_29_ = bf16[768,512]{1,0:T(8,128)(2,1)S(1)} collective-permute-done((bf16[768,512]{1,0:T(8,128)(2,1)S(1)}, bf16[768,512]{1,0:T(8,128)(2,1)S(1)}, u32[]{:S(2)}, u32[]{:S(2)}) %collective-permute-start.20) | collective-permute-done | bytes 786464 | tf_op jit(solution)/shard_map/ppermute | solution.py:183
  105.1 1.1 collective-permute-start.24
  106.2 1.6 collective-permute-start.23
  107.8 2.7 %collective-permute-start.21 = (bf16[512,768]{1,0:T(8,128)(2,1)S(1)}, bf16[512,768]{1,0:T(8,128)(2,1)}, u32[]{:S(2)}, u32[]{:S(2)}) collective-permute-start(bf16[512,768]{1,0:T(8,128)(2,1)S(1)} %collective-permute-done.19.refs_9_), channel_id=1, source_target_pairs={{0,2},{1,7},{2,4},{3,1},{4,6},{5,3},{6,0},{7,5},{8,10},{9,15},{10,... | collective-permute-start | bytes 2359304 | tf_op jit(solution)/shard_map/ppermute | solution.py:36
  110.6 1.2 collective-permute-start.11
  111.8 11.2 %collective-permute-done.24.refs_29_.refs_33_ = bf16[768,512]{1,0:T(8,128)(2,1)S(1)} collective-permute-done((bf16[768,512]{1,0:T(8,128)(2,1)S(1)}, bf16[768,512]{1,0:T(8,128)(2,1)S(1)}, u32[]{:S(2)}, u32[]{:S(2)}) %collective-permute-start.24) | collective-permute-done | bytes 786464 | tf_op jit(solution)/shard_map/ppermute | solution.py:36
  123.0 3.1 %collective-permute-start.16 = (bf16[512,768]{1,0:T(8,128)(2,1)}, bf16[512,768]{1,0:T(8,128)(2,1)S(1)}, u32[]{:S(2)}, u32[]{:S(2)}) collective-permute-start(bf16[512,768]{1,0:T(8,128)(2,1)} %collective-permute-done.4.refs_12_), channel_id=1, source_target_pairs={{0,1},{1,0},{2,3},{3,2},{4,5},{5,4},{6,7},{7,6},{8,9},{9,8},{10,11... | collective-permute-start | bytes 2359304 | tf_op jit(solution)/shard_map/ppermute | solution.py:183
  126.2 1.3 collective-permute-done.21.refs_13_
  127.5 1.6 collective-permute-start.25
  129.2 1.8 collective-permute-done.25.refs_11_
  131.5 0.6 collective-permute-done.17.refs_14_
  132.5 2.8 %collective-permute-start.28 = (bf16[512,768]{1,0:T(8,128)(2,1)}, bf16[512,768]{1,0:T(8,128)(2,1)}, u32[]{:S(2)}, u32[]{:S(2)}) collective-permute-start(bf16[512,768]{1,0:T(8,128)(2,1)} %collective-permute-done.4.refs_12_), channel_id=1, source_target_pairs={{0,2},{1,7},{2,4},{3,1},{4,6},{5,3},{6,0},{7,5},{8,10},{9,15},{10,... | collective-permute-start | bytes 2359304 | tf_op jit(solution)/shard_map/ppermute | solution.py:36
  135.7 0.6 copy-done.20
  136.3 0.7 constant_dynamic-slice_fusion
  137.2 1.9 fusion.2
  139.1 5.4 %collective-permute-done.28.refs_20_ = bf16[512,768]{1,0:T(8,128)(2,1)} collective-permute-done((bf16[512,768]{1,0:T(8,128)(2,1)}, bf16[512,768]{1,0:T(8,128)(2,1)}, u32[]{:S(2)}, u32[]{:S(2)}) %collective-permute-start.28) | collective-permute-done | bytes 786464 | tf_op jit(solution)/shard_map/ppermute | solution.py:36
  145.1 7.8 %collective-permute-done.29.refs_21_ = bf16[512,768]{1,0:T(8,128)(2,1)} collective-permute-done((bf16[512,768]{1,0:T(8,128)(2,1)}, bf16[512,768]{1,0:T(8,128)(2,1)}, u32[]{:S(2)}, u32[]{:S(2)}) %collective-permute-start.29) | collective-permute-done | bytes 786464 | tf_op jit(solution)/shard_map/ppermute | solution.py:36
  152.9 0.6 collective-permute-start.33
  153.5 1.2 collective-permute-start.30
  154.8 15.2 %shard_map.67.refs_36_ = f32[1024,512]{1,0:T(8,128)S(1)} custom-call(s32[17]{0:T(128)S(1)} %pad_add_fusion.table_ref, bf16[1024,768]{1,0:T(8,128)(2,1)} %refs_0_.3, bf16[1024,768]{1,0:T(8,128)(2,1)} %copy-done.6, bf16[1024,768]{1,0:T(8,128)(2,1)} %copy-done.4, bf16[1024,768]{1,0:T(8,128)(2,1)} %collective-permute-done.12.refs_3_, ...), custom_call_target="tpu_custom_call" | custom-call | flops 9663676416 | bytes 28311552 | tf_op jit(solution)/shard_map/pallas_call | solution.py:163
  170.1 0.8 copy-done.21
  171.7 7.3 %shard_map.68 = bf16[1024,512]{1,0:T(8,128)(2,1)S(1)} custom-call(s32[17]{0:T(128)S(1)} %pad_add_fusion.table_ref, bf16[1024,768]{1,0:T(8,128)(2,1)} %refs_0_.3, bf16[1024,768]{1,0:T(8,128)(2,1)} %copy-done.6, bf16[1024,768]{1,0:T(8,128)(2,1)} %copy-done.4, bf16[1024,768]{1,0:T(8,128)(2,1)} %collective-permute-done.12.refs_3_, ...), custom_call_target="tpu_custom_call" | custom-call | flops 3221225472 | bytes 9437184 | tf_op jit(solution)/shard_map/pallas_call | solution.py:163
  179.0 18.8 %all_to_all.19 = bf16[16,64,512]{2,1,0:T(8,128)(2,1)S(1)} all-to-all(bf16[16,64,512]{2,1,0:T(8,128)(2,1)S(1)} %bitcast.7), channel_id=1, replica_groups=mesh['xh'=2,'y'=4,'xl'=2,'z'=4,'c'=2] {'xl','z','c'}, dimensions={0} | all-to-all | bytes 2097152 | tf_op jit(solution)/shard_map/all_to_all | solution.py:265
  197.9 0.7 fusion.8
  198.6 0.9 slice.28
  (86 shorter events, 3.7 us)
Async XLA Ops:
  2.3 134.8 %copy-start.25 = (s32[1024]{0:T(1024)S(1)}, s32[1024]{0:T(1024)}, u32[]{:S(2)}) copy-start(s32[1024]{0:T(1024)} %param.6) | copy-start | bytes 12292
  2.3 19.0 %collective-permute-start = (bf16[512,768]{1,0:T(8,128)(2,1)S(1)}, bf16[512,768]{1,0:T(8,128)(2,1)S(1)}, u32[]{:S(2)}, u32[]{:S(2)}) collective-permute-start(bf16[512,768]{1,0:T(8,128)(2,1)S(1)} %get-tuple-element.48), channel_id=1, source_target_pairs={{0,8},{8,0},{1,9},{9,1},{2,10},{10,2},{3,11},{11,3},{4,12},{12,4},... | collective-permute-start | bytes 2359304 | tf_op jit(solution)/shard_map/ppermute | solution.py:183
  4.4 36.2 %collective-permute-start.7 = (bf16[1536,512]{1,0:T(8,128)(2,1)S(1)}, bf16[1536,512]{1,0:T(8,128)(2,1)S(1)}, u32[]{:S(2)}, u32[]{:S(2)}) collective-permute-start(bf16[1536,512]{1,0:T(8,128)(2,1)S(1)} %copy-done.1), channel_id=1, source_target_pairs={{0,48},{1,17},{16,0},{17,33},{32,16},{33,49},{48,32},{49,1},{2,50}... | collective-permute-start | bytes 4718600 | tf_op jit(solution)/shard_map/ppermute | solution.py:36
  5.7 36.4 %collective-permute-start.6 = (bf16[1536,512]{1,0:T(8,128)(2,1)S(1)}, bf16[1536,512]{1,0:T(8,128)(2,1)S(1)}, u32[]{:S(2)}, u32[]{:S(2)}) collective-permute-start(bf16[1536,512]{1,0:T(8,128)(2,1)S(1)} %copy-done.1), channel_id=1, source_target_pairs={{0,16},{1,49},{16,32},{17,1},{32,48},{33,17},{48,0},{49,33},{2,18}... | collective-permute-start | bytes 4718600 | tf_op jit(solution)/shard_map/ppermute | solution.py:36
  7.2 37.6 %collective-permute-start.2 = (bf16[1024,768]{1,0:T(8,128)(2,1)S(1)}, bf16[1024,768]{1,0:T(8,128)(2,1)}, u32[]{:S(2)}, u32[]{:S(2)}) collective-permute-start(bf16[1024,768]{1,0:T(8,128)(2,1)S(1)} %copy-done), channel_id=1, source_target_pairs={{0,6},{1,3},{2,0},{3,5},{4,2},{5,7},{6,4},{7,1},{8,14},{9,11},{10,... | collective-permute-start | bytes 4718600 | tf_op jit(solution)/shard_map/ppermute | solution.py:36
  8.8 36.5 %collective-permute-start.1 = (bf16[1024,768]{1,0:T(8,128)(2,1)S(1)}, bf16[1024,768]{1,0:T(8,128)(2,1)S(1)}, u32[]{:S(2)}, u32[]{:S(2)}) collective-permute-start(bf16[1024,768]{1,0:T(8,128)(2,1)S(1)} %copy-done), channel_id=1, source_target_pairs={{0,2},{1,7},{2,4},{3,1},{4,6},{5,3},{6,0},{7,5},{8,10},{9,15},{10,... | collective-permute-start | bytes 4718600 | tf_op jit(solution)/shard_map/ppermute | solution.py:36
  21.3 109.7 %copy-start.8 = (bf16[512,768]{1,0:T(8,128)(2,1)}, bf16[512,768]{1,0:T(8,128)(2,1)S(1)}, u32[]{:S(2)}) copy-start(bf16[512,768]{1,0:T(8,128)(2,1)S(1)} %collective-permute-done.refs_8_) | copy-start | bytes 2359300
  21.3 19.3 %collective-permute-start.3 = (bf16[768,512]{1,0:T(8,128)(2,1)S(1)}, bf16[768,512]{1,0:T(8,128)(2,1)S(1)}, u32[]{:S(2)}, u32[]{:S(2)}) collective-permute-start(bf16[768,512]{1,0:T(8,128)(2,1)S(1)} %get-tuple-element.24), channel_id=1, source_target_pairs={{0,64},{64,0},{1,65},{65,1},{2,66},{66,2},{3,67},{67,3},{4,68},{68... | collective-permute-start | bytes 2359304 | tf_op jit(solution)/shard_map/ppermute | solution.py:183
  40.6 90.8 %copy-start.9 = (bf16[768,512]{1,0:T(8,128)(2,1)}, bf16[768,512]{1,0:T(8,128)(2,1)S(1)}, u32[]{:S(2)}) copy-start(bf16[768,512]{1,0:T(8,128)(2,1)S(1)} %collective-permute-done.3.refs_24_.refs_28_) | copy-start | bytes 2359300
  40.6 67.2 %copy-start.2 = (bf16[1536,512]{1,0:T(8,128)(2,1)}, bf16[1536,512]{1,0:T(8,128)(2,1)S(1)}, u32[]{:S(2)}) copy-start(bf16[1536,512]{1,0:T(8,128)(2,1)S(1)} %collective-permute-done.7.refs_22_.refs_26_) | copy-start | bytes 4718596
  42.1 68.4 %copy-start.3 = (bf16[1536,512]{1,0:T(8,128)(2,1)}, bf16[1536,512]{1,0:T(8,128)(2,1)S(1)}, u32[]{:S(2)}) copy-start(bf16[1536,512]{1,0:T(8,128)(2,1)S(1)} %collective-permute-done.6.refs_21_.refs_25_) | copy-start | bytes 4718596
  42.1 16.2 %collective-permute-start.9 = (bf16[768,512]{1,0:T(8,128)(2,1)S(1)}, bf16[768,512]{1,0:T(8,128)(2,1)S(1)}, u32[]{:S(2)}, u32[]{:S(2)}) collective-permute-start(bf16[768,512]{1,0:T(8,128)(2,1)S(1)} %collective-permute-done.3.refs_24_.refs_28_), channel_id=1, source_target_pairs={{0,48},{1,17},{16,0},{17,33},{32,16},{33,49},{48,32},{49,1},{2,50}... | collective-permute-start | bytes 2359304 | tf_op jit(solution)/shard_map/ppermute | solution.py:36
  43.4 19.6 %collective-permute-start.8 = (bf16[768,512]{1,0:T(8,128)(2,1)S(1)}, bf16[768,512]{1,0:T(8,128)(2,1)}, u32[]{:S(2)}, u32[]{:S(2)}) collective-permute-start(bf16[768,512]{1,0:T(8,128)(2,1)S(1)} %collective-permute-done.3.refs_24_.refs_28_), channel_id=1, source_target_pairs={{0,16},{1,49},{16,32},{17,1},{32,48},{33,17},{48,0},{49,33},{2,18}... | collective-permute-start | bytes 2359304 | tf_op jit(solution)/shard_map/ppermute | solution.py:36
  45.3 65.3 %copy-start.4 = (bf16[1024,768]{1,0:T(8,128)(2,1)}, bf16[1024,768]{1,0:T(8,128)(2,1)S(1)}, u32[]{:S(2)}) copy-start(bf16[1024,768]{1,0:T(8,128)(2,1)S(1)} %collective-permute-done.1.refs_2_) | copy-start | bytes 4718596
  45.3 18.7 %collective-permute-start.5 = (bf16[512,768]{1,0:T(8,128)(2,1)S(1)}, bf16[512,768]{1,0:T(8,128)(2,1)S(1)}, u32[]{:S(2)}, u32[]{:S(2)}) collective-permute-start(bf16[512,768]{1,0:T(8,128)(2,1)S(1)} %collective-permute-done.refs_8_), channel_id=1, source_target_pairs={{0,6},{1,3},{2,0},{3,5},{4,2},{5,7},{6,4},{7,1},{8,14},{9,11},{10,... | collective-permute-start | bytes 2359304 | tf_op jit(solution)/shard_map/ppermute | solution.py:36
  46.9 19.6 %collective-permute-start.4 = (bf16[512,768]{1,0:T(8,128)(2,1)S(1)}, bf16[512,768]{1,0:T(8,128)(2,1)}, u32[]{:S(2)}, u32[]{:S(2)}) collective-permute-start(bf16[512,768]{1,0:T(8,128)(2,1)S(1)} %collective-permute-done.refs_8_), channel_id=1, source_target_pairs={{0,2},{1,7},{2,4},{3,1},{4,6},{5,3},{6,0},{7,5},{8,10},{9,15},{10,... | collective-permute-start | bytes 2359304 | tf_op jit(solution)/shard_map/ppermute | solution.py:36
  58.3 73.2 %copy-start.10 = (bf16[768,512]{1,0:T(8,128)(2,1)}, bf16[768,512]{1,0:T(8,128)(2,1)S(1)}, u32[]{:S(2)}) copy-start(bf16[768,512]{1,0:T(8,128)(2,1)S(1)} %collective-permute-done.9.refs_28_.refs_32_) | copy-start | bytes 2359300
  63.0 25.0 %collective-permute-start.14 = (bf16[1536,512]{1,0:T(8,128)(2,1)S(1)}, bf16[1536,512]{1,0:T(8,128)(2,1)S(1)}, u32[]{:S(2)}, u32[]{:S(2)}) collective-permute-start(bf16[1536,512]{1,0:T(8,128)(2,1)S(1)} %collective-permute-done.6.refs_21_.refs_25_), channel_id=1, source_target_pairs={{0,16},{1,49},{16,32},{17,1},{32,48},{33,17},{48,0},{49,33},{2,18}... | collective-permute-start | bytes 4718600 | tf_op jit(solution)/shard_map/ppermute | solution.py:36
  63.9 68.2 %copy-start.11 = (bf16[512,768]{1,0:T(8,128)(2,1)}, bf16[512,768]{1,0:T(8,128)(2,1)S(1)}, u32[]{:S(2)}) copy-start(bf16[512,768]{1,0:T(8,128)(2,1)S(1)} %collective-permute-done.5.refs_16_) | copy-start | bytes 2359300
  66.5 21.4 %collective-permute-start.13 = (bf16[1024,768]{1,0:T(8,128)(2,1)S(1)}, bf16[1024,768]{1,0:T(8,128)(2,1)}, u32[]{:S(2)}, u32[]{:S(2)}) collective-permute-start(bf16[1024,768]{1,0:T(8,128)(2,1)S(1)} %collective-permute-done.1.refs_2_), channel_id=1, source_target_pairs={{0,2},{1,7},{2,4},{3,1},{4,6},{5,3},{6,0},{7,5},{8,10},{9,15},{10,... | collective-permute-start | bytes 4718600 | tf_op jit(solution)/shard_map/ppermute | solution.py:36
  67.7 18.4 %collective-permute-start.19 = (bf16[512,768]{1,0:T(8,128)(2,1)S(1)}, bf16[512,768]{1,0:T(8,128)(2,1)S(1)}, u32[]{:S(2)}, u32[]{:S(2)}) collective-permute-start(bf16[512,768]{1,0:T(8,128)(2,1)S(1)} %get-tuple-element.36), channel_id=1, source_target_pairs={{0,8},{8,0},{1,9},{9,1},{2,10},{10,2},{3,11},{11,3},{4,12},{12,4},... | collective-permute-start | bytes 2359304 | tf_op jit(solution)/shard_map/ppermute | solution.py:183
  67.7 40.2 %collective-permute-start.10 = (bf16[1024,768]{1,0:T(8,128)(2,1)S(1)}, bf16[1024,768]{1,0:T(8,128)(2,1)S(1)}, u32[]{:S(2)}, u32[]{:S(2)}) collective-permute-start(bf16[1024,768]{1,0:T(8,128)(2,1)S(1)} %copy-done), channel_id=1, source_target_pairs={{0,1},{1,0},{2,3},{3,2},{4,5},{5,4},{6,7},{7,6},{8,9},{9,8},{10,11... | collective-permute-start | bytes 4718600 | tf_op jit(solution)/shard_map/ppermute | solution.py:183
  86.1 46.4 %copy-start.12 = (bf16[512,768]{1,0:T(8,128)(2,1)}, bf16[512,768]{1,0:T(8,128)(2,1)S(1)}, u32[]{:S(2)}) copy-start(bf16[512,768]{1,0:T(8,128)(2,1)S(1)} %collective-permute-done.19.refs_9_) | copy-start | bytes 2359300
  86.1 19.0 %collective-permute-start.20 = (bf16[768,512]{1,0:T(8,128)(2,1)S(1)}, bf16[768,512]{1,0:T(8,128)(2,1)S(1)}, u32[]{:S(2)}, u32[]{:S(2)}) collective-permute-start(bf16[768,512]{1,0:T(8,128)(2,1)S(1)} %get-tuple-element.37), channel_id=1, source_target_pairs={{0,64},{64,0},{1,65},{65,1},{2,66},{66,2},{3,67},{67,3},{4,68},{68... | collective-permute-start | bytes 2359304 | tf_op jit(solution)/shard_map/ppermute | solution.py:183
  87.9 66.9 %copy-start.5 = (bf16[1536,512]{1,0:T(8,128)(2,1)}, bf16[1536,512]{1,0:T(8,128)(2,1)S(1)}, u32[]{:S(2)}) copy-start(bf16[1536,512]{1,0:T(8,128)(2,1)S(1)} %collective-permute-done.14.refs_23_.refs_27_) | copy-start | bytes 4718596
  87.9 22.6 %collective-permute-start.15 = (bf16[512,768]{1,0:T(8,128)(2,1)S(1)}, bf16[512,768]{1,0:T(8,128)(2,1)S(1)}, u32[]{:S(2)}, u32[]{:S(2)}) collective-permute-start(bf16[512,768]{1,0:T(8,128)(2,1)S(1)} %collective-permute-done.refs_8_), channel_id=1, source_target_pairs={{0,1},{1,0},{2,3},{3,2},{4,5},{5,4},{6,7},{7,6},{8,9},{9,8},{10,11... | collective-permute-start | bytes 2359304 | tf_op jit(solution)/shard_map/ppermute | solution.py:183
  105.1 30.1 %copy-start.13 = (bf16[768,512]{1,0:T(8,128)(2,1)}, bf16[768,512]{1,0:T(8,128)(2,1)S(1)}, u32[]{:S(2)}) copy-start(bf16[768,512]{1,0:T(8,128)(2,1)S(1)} %collective-permute-done.20.refs_25_.refs_29_) | copy-start | bytes 2359300
  105.1 17.9 %collective-permute-start.24 = (bf16[768,512]{1,0:T(8,128)(2,1)S(1)}, bf16[768,512]{1,0:T(8,128)(2,1)S(1)}, u32[]{:S(2)}, u32[]{:S(2)}) collective-permute-start(bf16[768,512]{1,0:T(8,128)(2,1)S(1)} %collective-permute-done.20.refs_25_.refs_29_), channel_id=1, source_target_pairs={{0,48},{1,17},{16,0},{17,33},{32,16},{33,49},{48,32},{49,1},{2,50}... | collective-permute-start | bytes 2359304 | tf_op jit(solution)/shard_map/ppermute | solution.py:36
  106.2 20.0 %collective-permute-start.23 = (bf16[768,512]{1,0:T(8,128)(2,1)S(1)}, bf16[768,512]{1,0:T(8,128)(2,1)S(1)}, u32[]{:S(2)}, u32[]{:S(2)}) collective-permute-start(bf16[768,512]{1,0:T(8,128)(2,1)S(1)} %collective-permute-done.20.refs_25_.refs_29_), channel_id=1, source_target_pairs={{0,16},{1,49},{16,32},{17,1},{32,48},{33,17},{48,0},{49,33},{2,18}... | collective-permute-start | bytes 2359304 | tf_op jit(solution)/shard_map/ppermute | solution.py:36
  107.8 18.4 %collective-permute-start.22 = (bf16[512,768]{1,0:T(8,128)(2,1)S(1)}, bf16[512,768]{1,0:T(8,128)(2,1)}, u32[]{:S(2)}, u32[]{:S(2)}) collective-permute-start(bf16[512,768]{1,0:T(8,128)(2,1)S(1)} %collective-permute-done.19.refs_9_), channel_id=1, source_target_pairs={{0,6},{1,3},{2,0},{3,5},{4,2},{5,7},{6,4},{7,1},{8,14},{9,11},{10,... | collective-permute-start | bytes 2359304 | tf_op jit(solution)/shard_map/ppermute | solution.py:36
  107.8 21.4 %copy-start.6 = (bf16[1024,768]{1,0:T(8,128)(2,1)}, bf16[1024,768]{1,0:T(8,128)(2,1)S(1)}, u32[]{:S(2)}) copy-start(bf16[1024,768]{1,0:T(8,128)(2,1)S(1)} %collective-permute-done.10.refs_1_) | copy-start | bytes 4718596
  107.8 19.6 %collective-permute-start.21 = (bf16[512,768]{1,0:T(8,128)(2,1)S(1)}, bf16[512,768]{1,0:T(8,128)(2,1)}, u32[]{:S(2)}, u32[]{:S(2)}) collective-permute-start(bf16[512,768]{1,0:T(8,128)(2,1)S(1)} %collective-permute-done.19.refs_9_), channel_id=1, source_target_pairs={{0,2},{1,7},{2,4},{3,1},{4,6},{5,3},{6,0},{7,5},{8,10},{9,15},{10,... | collective-permute-start | bytes 2359304 | tf_op jit(solution)/shard_map/ppermute | solution.py:36
  110.6 24.8 %copy-start.14 = (bf16[512,768]{1,0:T(8,128)(2,1)}, bf16[512,768]{1,0:T(8,128)(2,1)S(1)}, u32[]{:S(2)}) copy-start(bf16[512,768]{1,0:T(8,128)(2,1)S(1)} %collective-permute-done.15.refs_10_) | copy-start | bytes 2359300
  110.6 18.6 %collective-permute-start.11 = (bf16[1024,768]{1,0:T(8,128)(2,1)S(1)}, bf16[1024,768]{1,0:T(8,128)(2,1)S(1)}, u32[]{:S(2)}, u32[]{:S(2)}) collective-permute-start(bf16[1024,768]{1,0:T(8,128)(2,1)S(1)} %collective-permute-done.1.refs_2_), channel_id=1, source_target_pairs={{0,1},{1,0},{2,3},{3,2},{4,5},{5,4},{6,7},{7,6},{8,9},{9,8},{10,11... | collective-permute-start | bytes 4718600 | tf_op jit(solution)/shard_map/ppermute | solution.py:183
  123.0 6.0 %collective-permute-start.16 = (bf16[512,768]{1,0:T(8,128)(2,1)}, bf16[512,768]{1,0:T(8,128)(2,1)S(1)}, u32[]{:S(2)}, u32[]{:S(2)}) collective-permute-start(bf16[512,768]{1,0:T(8,128)(2,1)} %collective-permute-done.4.refs_12_), channel_id=1, source_target_pairs={{0,1},{1,0},{2,3},{3,2},{4,5},{5,4},{6,7},{7,6},{8,9},{9,8},{10,11... | collective-permute-start | bytes 2359304 | tf_op jit(solution)/shard_map/ppermute | solution.py:183
  127.5 3.5 %collective-permute-start.25 = (bf16[512,768]{1,0:T(8,128)(2,1)S(1)}, bf16[512,768]{1,0:T(8,128)(2,1)S(1)}, u32[]{:S(2)}, u32[]{:S(2)}) collective-permute-start(bf16[512,768]{1,0:T(8,128)(2,1)S(1)} %collective-permute-done.19.refs_9_), channel_id=1, source_target_pairs={{0,1},{1,0},{2,3},{3,2},{4,5},{5,4},{6,7},{7,6},{8,9},{9,8},{10,11... | collective-permute-start | bytes 2359304 | tf_op jit(solution)/shard_map/ppermute | solution.py:183
  129.1 3.0 %collective-permute-start.17 = (bf16[512,768]{1,0:T(8,128)(2,1)S(1)}, bf16[512,768]{1,0:T(8,128)(2,1)S(1)}, u32[]{:S(2)}, u32[]{:S(2)}) collective-permute-start(bf16[512,768]{1,0:T(8,128)(2,1)S(1)} %collective-permute-done.5.refs_16_), channel_id=1, source_target_pairs={{0,1},{1,0},{2,3},{3,2},{4,5},{5,4},{6,7},{7,6},{8,9},{9,8},{10,11... | collective-permute-start | bytes 2359304 | tf_op jit(solution)/shard_map/ppermute | solution.py:183
  129.2 25.7 %copy-start.7 = (bf16[1024,768]{1,0:T(8,128)(2,1)}, bf16[1024,768]{1,0:T(8,128)(2,1)S(1)}, u32[]{:S(2)}) copy-start(bf16[1024,768]{1,0:T(8,128)(2,1)S(1)} %collective-permute-done.11.refs_5_) | copy-start | bytes 4718596
  131.0 4.3 %collective-permute-start.26 = (bf16[512,768]{1,0:T(8,128)(2,1)}, bf16[512,768]{1,0:T(8,128)(2,1)S(1)}, u32[]{:S(2)}, u32[]{:S(2)}) collective-permute-start(bf16[512,768]{1,0:T(8,128)(2,1)} %collective-permute-done.21.refs_13_), channel_id=1, source_target_pairs={{0,1},{1,0},{2,3},{3,2},{4,5},{5,4},{6,7},{7,6},{8,9},{9,8},{10,11... | collective-permute-start | bytes 2359304 | tf_op jit(solution)/shard_map/ppermute | solution.py:183
  131.4 22.2 %collective-permute-start.12 = (bf16[1024,768]{1,0:T(8,128)(2,1)}, bf16[1024,768]{1,0:T(8,128)(2,1)}, u32[]{:S(2)}, u32[]{:S(2)}) collective-permute-start(bf16[1024,768]{1,0:T(8,128)(2,1)} %collective-permute-done.2.refs_4_), channel_id=1, source_target_pairs={{0,1},{1,0},{2,3},{3,2},{4,5},{5,4},{6,7},{7,6},{8,9},{9,8},{10,11... | collective-permute-start | bytes 4718600 | tf_op jit(solution)/shard_map/ppermute | solution.py:183
  132.1 22.7 %collective-permute-start.18 = (bf16[1024,768]{1,0:T(8,128)(2,1)}, bf16[1024,768]{1,0:T(8,128)(2,1)}, u32[]{:S(2)}, u32[]{:S(2)}) collective-permute-start(bf16[1024,768]{1,0:T(8,128)(2,1)} %collective-permute-done.13.refs_6_), channel_id=1, source_target_pairs={{0,1},{1,0},{2,3},{3,2},{4,5},{5,4},{6,7},{7,6},{8,9},{9,8},{10,11... | collective-permute-start | bytes 4718600 | tf_op jit(solution)/shard_map/ppermute | solution.py:183
  132.5 12.0 %collective-permute-start.28 = (bf16[512,768]{1,0:T(8,128)(2,1)}, bf16[512,768]{1,0:T(8,128)(2,1)}, u32[]{:S(2)}, u32[]{:S(2)}) collective-permute-start(bf16[512,768]{1,0:T(8,128)(2,1)} %collective-permute-done.4.refs_12_), channel_id=1, source_target_pairs={{0,2},{1,7},{2,4},{3,1},{4,6},{5,3},{6,0},{7,5},{8,10},{9,15},{10,... | collective-permute-start | bytes 2359304 | tf_op jit(solution)/shard_map/ppermute | solution.py:36
  135.3 17.7 %collective-permute-start.29 = (bf16[512,768]{1,0:T(8,128)(2,1)}, bf16[512,768]{1,0:T(8,128)(2,1)}, u32[]{:S(2)}, u32[]{:S(2)}) collective-permute-start(bf16[512,768]{1,0:T(8,128)(2,1)} %collective-permute-done.21.refs_13_), channel_id=1, source_target_pairs={{0,2},{1,7},{2,4},{3,1},{4,6},{5,3},{6,0},{7,5},{8,10},{9,15},{10,... | collective-permute-start | bytes 2359304 | tf_op jit(solution)/shard_map/ppermute | solution.py:36
  135.4 19.4 %collective-permute-start.27 = (bf16[512,768]{1,0:T(8,128)(2,1)}, bf16[512,768]{1,0:T(8,128)(2,1)}, u32[]{:S(2)}, u32[]{:S(2)}) collective-permute-start(bf16[512,768]{1,0:T(8,128)(2,1)} %collective-permute-done.22.refs_17_), channel_id=1, source_target_pairs={{0,1},{1,0},{2,3},{3,2},{4,5},{5,4},{6,7},{7,6},{8,9},{9,8},{10,11... | collective-permute-start | bytes 2359304 | tf_op jit(solution)/shard_map/ppermute | solution.py:183
  144.5 25.5 %collective-permute-start.32 = (bf16[768,512]{1,0:T(8,128)(2,1)}, bf16[768,512]{1,0:T(8,128)(2,1)S(1)}, u32[]{:S(2)}, u32[]{:S(2)}) collective-permute-start(bf16[768,512]{1,0:T(8,128)(2,1)} %collective-permute-done.8.refs_26_.refs_30_), channel_id=1, source_target_pairs={{0,16},{1,49},{16,32},{17,1},{32,48},{33,17},{48,0},{49,33},{2,18}... | collective-permute-start | bytes 2359304 | tf_op jit(solution)/shard_map/ppermute | solution.py:36
  152.9 17.1 %collective-permute-start.33 = (bf16[768,512]{1,0:T(8,128)(2,1)}, bf16[768,512]{1,0:T(8,128)(2,1)S(1)}, u32[]{:S(2)}, u32[]{:S(2)}) collective-permute-start(bf16[768,512]{1,0:T(8,128)(2,1)} %copy-done.16), channel_id=1, source_target_pairs={{0,16},{1,49},{16,32},{17,1},{32,48},{33,17},{48,0},{49,33},{2,18}... | collective-permute-start | bytes 2359304 | tf_op jit(solution)/shard_map/ppermute | solution.py:36
  153.5 16.5 %collective-permute-start.30 = (bf16[512,768]{1,0:T(8,128)(2,1)}, bf16[512,768]{1,0:T(8,128)(2,1)S(1)}, u32[]{:S(2)}, u32[]{:S(2)}) collective-permute-start(bf16[512,768]{1,0:T(8,128)(2,1)} %collective-permute-done.28.refs_20_), channel_id=1, source_target_pairs={{0,1},{1,0},{2,3},{3,2},{4,5},{5,4},{6,7},{7,6},{8,9},{9,8},{10,11... | collective-permute-start | bytes 2359304 | tf_op jit(solution)/shard_map/ppermute | solution.py:183
  154.8 15.3 %collective-permute-start.31 = (bf16[512,768]{1,0:T(8,128)(2,1)}, bf16[512,768]{1,0:T(8,128)(2,1)S(1)}, u32[]{:S(2)}, u32[]{:S(2)}) collective-permute-start(bf16[512,768]{1,0:T(8,128)(2,1)} %collective-permute-done.29.refs_21_), channel_id=1, source_target_pairs={{0,1},{1,0},{2,3},{3,2},{4,5},{5,4},{6,7},{7,6},{8,9},{9,8},{10,11... | collective-permute-start | bytes 2359304 | tf_op jit(solution)/shard_map/ppermute | solution.py:183
  (12 other events, 52.7 us)

commit v3 on v0

v3 whole, which is shorter than its diff:
```python
import math

import jax
import jax.numpy as jnp
import numpy as np
from jax import lax
from jax.experimental import pallas as pl
from jax.experimental.pallas import tpu as pltpu
from jax.sharding import Mesh
from jax.sharding import PartitionSpec as P

HEAD_WIDTH = 128
QUERY_HEADS = 48
KEY_VALUE_HEADS = 8

rope_base = 1000000.0
SWAP = ((0, 1), (1, 0))


def rotary_tables(positions, head_size):
    half_size = head_size // 2
    column_ids = jnp.arange(head_size, dtype=jnp.int32)
    exponent = (column_ids % half_size).astype(jnp.float32) * (
        -2.0 * math.log(rope_base) / head_size
    )
    frequency = jnp.exp(exponent)
    angles = positions.astype(jnp.float32)[:, None] * frequency[None, :]
    sign_table = jnp.where(column_ids < half_size, -1.0, 1.0).astype(jnp.float32)
    return (jnp.cos(angles), jnp.sin(angles) * sign_table[None, :])


def ring_step(block, axis, way=1):
    pairs = [
        (i * 2 + c, ((i + (1, -1)[c] * way) % 4) * 2 + c) for i in range(4) for c in range(2)
    ]
    return lax.ppermute(block, (axis, "c"), pairs)


def piece_table():
    table = np.zeros((2, 4, 2, 4, 2, 8, 2), np.int32)
    for xh, y, xl, z, c in np.ndindex(2, 4, 2, 4, 2):
        way = (1, -1)[c]
        places = (0, -way, way, 2)
        a_blocks = {(xl ^ p, (z + d) % 4): p * 4 + i for p in range(2) for i, d in enumerate(places)}
        b_blocks = {(xh ^ p, (y + d) % 4): p * 4 + i for p in range(2) for i, d in enumerate(places)}
        pairs = [(a_blocks[f], b_blocks[f]) for f in np.ndindex(2, 4)]
        table[xh, y, xl, z, c] = sorted(pairs, key=lambda p: (7 in p, max(p), p))
    return table


TABLE = piece_table()
EARLY = 6


def product(table, first, count, a_blocks, b_blocks, parts, totals=()):
    depth = a_blocks[0][0].shape[1]
    rows = sum(v.shape[0] for v in a_blocks[0])
    width = b_blocks[0].shape[1] // 2
    slots = 2
    used_a = [p for p in range(len(a_blocks)) if a_blocks[p] is not None]
    used_b = [q for q in range(len(b_blocks)) if b_blocks[q] is not None]
    low, high = parts[0] * width, (parts[-1] + 1) * width

    def kernel(table_ref, *refs):
        refs = list(refs)
        a_refs = {p: [refs.pop(0) for _ in a_blocks[p]] for p in used_a}
        b_refs = {q: refs.pop(0) for q in used_b}
        total_refs = [refs.pop(0) for _ in totals]
        out_refs = [refs.pop(0) for _ in parts]
        a_buf, b_buf, sems = refs

        def start(k):
            slot = lax.rem(k, slots)
            a_id = table_ref[(first + k) * 2]
            b_id = table_ref[(first + k) * 2 + 1]
            for p in used_a:

                @pl.when(a_id == p)
                def _():
                    row = 0
                    for ref in a_refs[p]:
                        pltpu.make_async_copy(
                            ref, a_buf.at[slot, pl.ds(row, ref.shape[0]), :], sems.at[slot]
                        ).start()
                        row += ref.shape[0]

            for q in used_b:

                @pl.when(b_id == q)
                def _():
                    pltpu.make_async_copy(
                        b_refs[q].at[:, pl.ds(low, high - low)], b_buf.at[slot], sems.at[slot]
                    ).start()

        def wait(k):
            slot = lax.rem(k, slots)
            pltpu.make_async_copy(a_buf.at[slot], a_buf.at[slot], sems.at[slot]).wait()
            pltpu.make_async_copy(b_buf.at[slot], b_buf.at[slot], sems.at[slot]).wait()

        start(0)
        if totals:
            out_refs[0][...] = sum(ref[...] for ref in total_refs)
        else:
            for ref in out_refs:
                ref[...] = jnp.zeros(ref.shape, jnp.float32)

        @pl.loop(0, count)
        def _(k):
            @pl.when(k + 1 < count)
            def _():
                start(k + 1)

            wait(k)
            slot = lax.rem(k, slots)
            for i, ref in enumerate(out_refs):
                ref[...] += jnp.dot(
                    a_buf[slot],
                    b_buf[slot, :, i * width : (i + 1) * width],
                    preferred_element_type=jnp.float32,
                )

    anywhere = pl.BlockSpec(memory_space=pl.ANY)
    vmem = pl.BlockSpec(memory_space=pltpu.VMEM)
    pieces = [v for p in used_a for v in a_blocks[p]] + [b_blocks[q] for q in used_b]
    late = [7 in used_a and p == 7 for p in used_a for _ in a_blocks[p]] + [q == 7 for q in used_b]
    operands = [table.reshape(-1)]
    operands += [
        pltpu.with_memory_space_constraint(v, pltpu.VMEM if near else pltpu.HBM)
        for v, near in zip(pieces, late)
    ]
    return pl.pallas_call(
        kernel,
        out_shape=[jax.ShapeDtypeStruct((rows, width), jnp.float32) for _ in parts],
        in_specs=[pl.BlockSpec(memory_space=pltpu.SMEM)] + [anywhere] * len(pieces) + [vmem] * len(totals),
        out_specs=[vmem] * len(parts),
        scratch_shapes=[
            pltpu.VMEM((slots, rows, depth), pieces[0].dtype),
            pltpu.VMEM((slots, depth, high - low), pieces[0].dtype),
            pltpu.SemaphoreType.DMA((slots,)),
        ],
        compiler_params=pltpu.CompilerParams(vmem_limit_bytes=24 * 1024 * 1024),
        cost_estimate=pl.CostEstimate(
            flops=2 * rows * (high - low) * depth * count,
            bytes_accessed=(rows + high - low) * depth * 2 * count,
            transcendentals=0,
        ),
    )(*operands, *totals)


def turn(total, received, cosine, sine):
    rows, columns = total.shape
    tile = 256

    def kernel(total_ref, received_ref, cos_ref, sin_ref, out_ref):
        @pl.loop(0, rows // tile)
        def _(i):
            span = pl.ds(pl.multiple_of(i * tile, tile), tile)
            for h in range(columns // HEAD_WIDTH):
                lanes = slice(h * HEAD_WIDTH, (h + 1) * HEAD_WIDTH)
                head = total_ref[span, lanes] + received_ref[span, lanes]
                swapped = pltpu.roll(head, HEAD_WIDTH // 2, 1)
                out_ref[span, lanes] = (head * cos_ref[span, :] + swapped * sin_ref[span, :]).astype(
                    jnp.bfloat16
                )

    return pl.pallas_call(
        kernel,
        out_shape=jax.ShapeDtypeStruct((rows, columns), jnp.bfloat16),
        compiler_params=pltpu.CompilerParams(vmem_limit_bytes=24 * 1024 * 1024),
        cost_estimate=pl.CostEstimate(flops=rows * columns * 4, bytes_accessed=rows * columns * 12, transcendentals=0),
    )(total, received, cosine, sine)


def after(block, *before):
    return lax.optimization_barrier((block,) + before)[0]


def swap(block, axis):
    return lax.ppermute(block, axis, SWAP)


def gathers(a, b):
    part = a.shape[0] // 2

    z_near, z_other = ring_step(a, "z"), ring_step(a, "z", -1)
    y_near, y_other = ring_step(b, "y"), ring_step(b, "y", -1)
    r = swap(b, "xh")

    p_0 = swap(after(a[:part], r), "xl")
    r_in = after(r, y_near, y_other)
    r_near, r_other = ring_step(r_in, "y"), ring_step(r_in, "y", -1)
    z_far = ring_step(after(z_near, z_other, r), "z")

    p_0_in = after(p_0, z_far)
    p_0_near, p_0_other = ring_step(p_0_in, "z"), ring_step(p_0_in, "z", -1)
    p_1 = swap(after(a[part:], p_0, z_far), "xl")

    y_far = ring_step(after(y_near, r_near, r_other, p_1, p_0_near, p_0_other), "y")
    p_1_in = after(p_1, p_0_near, p_0_other)
    p_1_near, p_1_other = ring_step(p_1_in, "z"), ring_step(p_1_in, "z", -1)

    r_far = ring_step(after(r_near, y_far), "y")
    p_0_far = ring_step(after(p_0_near, p_1_near, p_1_other), "z")
    p_1_far = ring_step(after(p_1_near, p_1_other), "z")

    a_blocks = [
        [a],
        [z_near],
        [z_other],
        [z_far],
        [p_0, p_1],
        [p_0_near, p_1_near],
        [p_0_other, p_1_other],
        [p_0_far, p_1_far],
    ]
    return a_blocks, [b, y_near, y_other, y_far, r, r_near, r_other, r_far]


def shards(tokens, joined_weight, positions):
    rows, depth = tokens.shape
    columns = joined_weight.shape[1]
    place = [lax.axis_index(a) for a in ("xh", "y", "xl", "z", "c")]
    table = jnp.asarray(TABLE)[tuple(place)]

    core = place[4]
    mine = lax.dynamic_slice_in_dim(joined_weight, core * depth, depth, 0)
    sent = lax.dynamic_slice_in_dim(joined_weight, (1 - core) * depth, depth, 0)
    weight = jnp.concatenate([mine, swap(sent, "c")], axis=1)
    a_blocks, b_blocks = gathers(tokens, weight)

    column_block = (place[2] * 4 + place[3]) * 2 + place[4]
    rotated = column_block * columns < (QUERY_HEADS + KEY_VALUE_HEADS) * HEAD_WIDTH
    cosine, sine = rotary_tables(positions, HEAD_WIDTH)
    cosine, sine = jnp.where(rotated, cosine, 1.0), jnp.where(rotated, sine, 0.0)

    early_a, early_b = a_blocks[:7] + [None], b_blocks[:7] + [None]
    early, early_sent = product(table, 0, EARLY, early_a, early_b, (0, 1))
    early_received = swap(early_sent, "c")
    (late_sent,) = product(table, EARLY, 8 - EARLY, a_blocks, b_blocks, (1,))
    late_received = swap(late_sent, "c")
    (total,) = product(table, EARLY, 8 - EARLY, a_blocks, b_blocks, (0,), (early, early_received))
    turned = turn(total, late_received, cosine, sine)
    received = lax.all_to_all(turned, ("xl", "z", "c"), split_axis=0, concat_axis=1, tiled=True)
    query_columns = QUERY_HEADS * HEAD_WIDTH
    rotated_columns = (QUERY_HEADS + KEY_VALUE_HEADS) * HEAD_WIDTH
    return (
        received[:, :query_columns],
        received[:, query_columns:rotated_columns],
        received[:, rotated_columns:],
    )


def solution(mesh):
    fine = Mesh(mesh.devices.reshape(2, 4, 2, 4, 2), ("xh", "y", "xl", "z", "c"))
    row, col = ("xh", "y"), ("xl", "z", "c")
    in_specs = (P(row, col), P(row, col), P(row))
    out_specs = (P(row + col, None),) * 3
    return jax.shard_map(shards, mesh=fine, in_specs=in_specs, out_specs=out_specs, check_vma=False)
```

time: 356 us -> 175 us (0.49)
  waiting for transfers between devices: 309 us -> 86 us
  Pallas kernels: 0 us -> 28 us
  starting transfers between devices: 5.15 us -> 31.3 us
  matrix products: 21.4 us -> 0 us
  blocking collectives: 0 us -> 18 us
  between operations: 14.1 us -> 0.89 us
  local copies, waits for them, and re-layouts: 3.61 us -> 7.83 us
    all_gather x2 -> x0, waiting for transfers between devices: 281 us -> none  [the longest x1 149 us: shards(): lax.all_gather(joined_weight, 'row', axis=0, tiled=True)]
    ppermute x0 -> x21, waiting for transfers between devices: none -> 86 us  [the longest x15 70 us: ring_step(): return lax.ppermute(block, (axis, 'c'), pairs)]
    ppermute x0 -> x21, starting transfers between devices: none -> 31.3 us  [the longest x15 23.2 us: ring_step(): return lax.ppermute(block, (axis, 'c'), pairs)]
    pallas_call x0 -> x4, Pallas kernels: none -> 28 us  [the longest x3 25.5 us: product(): pl.pallas_call(kernel, out_shape=[jax.ShapeDtypeStruct((rows, width), jnp...]
    all_to_all x1 -> x0, waiting for transfers between devices: 27 us -> none  [shards(): lax.all_to_all(projected_rows, 'col', split_axis=0, concat_axis=1, tiled=...]
    dot_general x1 -> x0, matrix products: 21.4 us -> none  [shards(): jnp.dot(whole_rows, lax.all_gather(joined_weight, 'row', axis=0, tiled=Tr...]
    all_to_all x0 -> x1, blocking collectives: none -> 18 us  [shards(): lax.all_to_all(turned, ('xl', 'z', 'c'), split_axis=0, concat_axis=1, til...]
    all_to_all x1 -> x0, starting transfers between devices: 5.07 us -> none  [shards(): lax.all_to_all(projected_rows, 'col', split_axis=0, concat_axis=1, tiled=...]
  transfers between devices with their start and end apart: 3 -> 21, of which waited for: 3 -> 9; matrix products, arithmetic and copies ran while one was open for 0% -> 2% of each run, Pallas kernels for 0% -> 15%
where the time goes in v3:
time: 175 us; the launch traced here: 174 us
  waiting for transfers between devices  86 us (49%)
  starting transfers between devices  31.3 us (18%)
  Pallas kernels  28 us (16%)
  blocking collectives  18 us (10%)
  local copies, waits for them, and re-layouts  7.83 us (4%)
  other arithmetic  2.17 us (1%)
    ppermute x15, waiting for transfers between devices, ring_step(): return lax.ppermute(block, (axis, 'c'), pairs)  70 us
    pallas_call x3, Pallas kernels, product(): pl.pallas_call(kernel, out_shape=[jax.ShapeDtypeStruct((rows, width), jnp...  25.5 us
    ppermute x15, starting transfers between devices, ring_step(): return lax.ppermute(block, (axis, 'c'), pairs)  23.2 us
    all_to_all x1, blocking collectives, shards(): lax.all_to_all(turned, ('xl', 'z', 'c'), split_axis=0, concat_axis=1, til...  18 us
    ppermute x6, waiting for transfers between devices, swap(): return lax.ppermute(block, axis, SWAP)  15.9 us
    ppermute x6, starting transfers between devices, swap(): return lax.ppermute(block, axis, SWAP)  8.16 us
    unnamed x32, local copies, waits for them, and re-layouts  3.62 us
  transfers between devices with their start and end apart: 21, of which 9 were waited for; matrix products, arithmetic and copies ran while one was open for 2% of the time, Pallas kernels for 15%

profile of v3, /device:TPU:1, one launch (start us, length us, event | category | flops | bytes accessed | tf_op | source)
XLA Modules:
  0.0 174.1 jit_solution(15505256061900162383)
XLA Ops:
  0.6 0.0 copy-start.2
  0.6 1.6 constant_dynamic-slice_fusion.1
  2.2 1.5 collective-permute-start.2
  3.8 3.8 %collective-permute-start = (bf16[1024,768]{1,0:T(8,128)(2,1)S(1)}, bf16[1024,768]{1,0:T(8,128)(2,1)S(1)}, u32[]{:S(2)}, u32[]{:S(2)}) collective-permute-start(bf16[1024,768]{1,0:T(8,128)(2,1)S(1)} %copy-done.2), channel_id=1, source_target_pairs={{0,2},{1,7},{2,4},{3,1},{4,6},{5,3},{6,0},{7,5},{8,10},{9,15},{10,... | collective-permute-start | bytes 4718600 | tf_op jit(solution)/shard_map/ppermute | solution.py:36
  7.6 0.0 collective-permute-start.1
  7.6 0.0 collective-permute-done.2
  7.6 0.2 pad_maximum_fusion.refs_10_.refs_12_
  7.8 2.8 %collective-permute-start.3 = (bf16[768,1024]{1,0:T(8,128)(2,1)S(1)}, bf16[768,1024]{1,0:T(8,128)(2,1)S(1)}, u32[]{:S(2)}, u32[]{:S(2)}) collective-permute-start(bf16[768,1024]{1,0:T(8,128)(2,1)S(1)} %pad_maximum_fusion.refs_10_.refs_12_), channel_id=1, source_target_pairs={{0,64},{64,0},{1,65},{65,1},{2,66},{66,2},{3,67},{67,3},{4,68},{68... | collective-permute-start | bytes 4718600 | tf_op jit(solution)/shard_map/ppermute | solution.py:179
  10.7 2.7 %collective-permute-start.13 = (bf16[768,1024]{1,0:T(8,128)(2,1)S(1)}, bf16[768,1024]{1,0:T(8,128)(2,1)S(1)}, u32[]{:S(2)}, u32[]{:S(2)}) collective-permute-start(bf16[768,1024]{1,0:T(8,128)(2,1)S(1)} %pad_maximum_fusion.refs_10_.refs_12_), channel_id=1, source_target_pairs={{0,16},{1,49},{16,32},{17,1},{32,48},{33,17},{48,0},{49,33},{2,18}... | collective-permute-start | bytes 4718600 | tf_op jit(solution)/shard_map/ppermute | solution.py:36
  13.4 0.0 collective-permute-start.14
  13.4 27.8 %collective-permute-done.refs_1_ = bf16[1024,768]{1,0:T(8,128)(2,1)S(1)} collective-permute-done((bf16[1024,768]{1,0:T(8,128)(2,1)S(1)}, bf16[1024,768]{1,0:T(8,128)(2,1)S(1)}, u32[]{:S(2)}, u32[]{:S(2)}) %collective-permute-start) | collective-permute-done | bytes 1572896 | tf_op jit(solution)/shard_map/ppermute | solution.py:36
  41.2 1.7 collective-permute-done.1.refs_2_
  42.9 2.0 %collective-permute-done.3.refs_14_.refs_16_ = bf16[768,1024]{1,0:T(8,128)(2,1)S(1)} collective-permute-done((bf16[768,1024]{1,0:T(8,128)(2,1)S(1)}, bf16[768,1024]{1,0:T(8,128)(2,1)S(1)}, u32[]{:S(2)}, u32[]{:S(2)}) %collective-permute-start.3) | collective-permute-done | bytes 1572896 | tf_op jit(solution)/shard_map/ppermute | solution.py:179
  44.9 3.5 %collective-permute-start.4 = (bf16[1024,768]{1,0:T(8,128)(2,1)S(1)}, bf16[1024,768]{1,0:T(8,128)(2,1)S(1)}, u32[]{:S(2)}, u32[]{:S(2)}) collective-permute-start(bf16[1024,768]{1,0:T(8,128)(2,1)S(1)} %collective-permute-done.refs_1_), channel_id=1, source_target_pairs={{0,2},{1,7},{2,4},{3,1},{4,6},{5,3},{6,0},{7,5},{8,10},{9,15},{10,... | collective-permute-start | bytes 4718600 | tf_op jit(solution)/shard_map/ppermute | solution.py:36
  48.4 0.1 fusion.6
  48.6 1.3 collective-permute-start.5
  49.9 0.0 collective-permute-done.13.refs_11_.refs_13_
  49.9 2.8 %collective-permute-start.15 = (bf16[768,1024]{1,0:T(8,128)(2,1)S(1)}, bf16[768,1024]{1,0:T(8,128)(2,1)}, u32[]{:S(2)}, u32[]{:S(2)}) collective-permute-start(bf16[768,1024]{1,0:T(8,128)(2,1)S(1)} %collective-permute-done.3.refs_14_.refs_16_), channel_id=1, source_target_pairs={{0,16},{1,49},{16,32},{17,1},{32,48},{33,17},{48,0},{49,33},{2,18}... | collective-permute-start | bytes 4718600 | tf_op jit(solution)/shard_map/ppermute | solution.py:36
  52.7 0.0 collective-permute-start.16
  52.7 13.9 %collective-permute-done.5.refs_4_ = bf16[512,768]{1,0:T(8,128)(2,1)S(1)} collective-permute-done((bf16[512,768]{1,0:T(8,128)(2,1)S(1)}, bf16[512,768]{1,0:T(8,128)(2,1)S(1)}, u32[]{:S(2)}, u32[]{:S(2)}) %collective-permute-start.5) | collective-permute-done | bytes 786464 | tf_op jit(solution)/shard_map/ppermute | solution.py:179
  66.6 0.0 collective-permute-done.4.refs_3_
  66.6 1.3 collective-permute-start.6
  67.9 2.6 %collective-permute-start.7 = (bf16[512,768]{1,0:T(8,128)(2,1)S(1)}, bf16[512,768]{1,0:T(8,128)(2,1)}, u32[]{:S(2)}, u32[]{:S(2)}) collective-permute-start(bf16[512,768]{1,0:T(8,128)(2,1)S(1)} %collective-permute-done.5.refs_4_), channel_id=1, source_target_pairs={{0,2},{1,7},{2,4},{3,1},{4,6},{5,3},{6,0},{7,5},{8,10},{9,15},{10,... | collective-permute-start | bytes 2359304 | tf_op jit(solution)/shard_map/ppermute | solution.py:36
  70.5 15.6 %collective-permute-done.15.refs_15_.refs_17_ = bf16[768,1024]{1,0:T(8,128)(2,1)} collective-permute-done((bf16[768,1024]{1,0:T(8,128)(2,1)S(1)}, bf16[768,1024]{1,0:T(8,128)(2,1)}, u32[]{:S(2)}, u32[]{:S(2)}) %collective-permute-start.15) | collective-permute-done | bytes 1572896 | tf_op jit(solution)/shard_map/ppermute | solution.py:36
  86.1 0.6 collective-permute-done.16.refs_16_.refs_18_
  86.7 3.7 %collective-permute-done.8.refs_8_ = bf16[512,768]{1,0:T(8,128)(2,1)} collective-permute-done((bf16[512,768]{1,0:T(8,128)(2,1)S(1)}, bf16[512,768]{1,0:T(8,128)(2,1)}, u32[]{:S(2)}, u32[]{:S(2)}) %collective-permute-start.8) | collective-permute-done | bytes 786464 | tf_op jit(solution)/shard_map/ppermute | solution.py:36
  90.4 2.7 %collective-permute-start.17 = (bf16[768,1024]{1,0:T(8,128)(2,1)S(1)}, bf16[768,1024]{1,0:T(8,128)(2,1)S(1)}, u32[]{:S(2)}, u32[]{:S(2)}) collective-permute-start(bf16[768,1024]{1,0:T(8,128)(2,1)S(1)} %collective-permute-done.13.refs_11_.refs_13_), channel_id=1, source_target_pairs={{0,16},{1,49},{16,32},{17,1},{32,48},{33,17},{48,0},{49,33},{2,18}... | collective-permute-start | bytes 4718600 | tf_op jit(solution)/shard_map/ppermute | solution.py:36
  93.1 1.5 collective-permute-start.10
  94.6 15.9 %collective-permute-done.17.refs_13_.refs_15_ = bf16[768,1024]{1,0:T(8,128)(2,1)S(1)} collective-permute-done((bf16[768,1024]{1,0:T(8,128)(2,1)S(1)}, bf16[768,1024]{1,0:T(8,128)(2,1)S(1)}, u32[]{:S(2)}, u32[]{:S(2)}) %collective-permute-start.17) | collective-permute-done | bytes 1572896 | tf_op jit(solution)/shard_map/ppermute | solution.py:36
  110.5 1.1 copy-done.11
  111.7 3.4 %collective-permute-start.18 = (bf16[768,1024]{1,0:T(8,128)(2,1)}, bf16[768,1024]{1,0:T(8,128)(2,1)S(1)}, u32[]{:S(2)}, u32[]{:S(2)}) collective-permute-start(bf16[768,1024]{1,0:T(8,128)(2,1)} %collective-permute-done.15.refs_15_.refs_17_), channel_id=1, source_target_pairs={{0,16},{1,49},{16,32},{17,1},{32,48},{33,17},{48,0},{49,33},{2,18}... | collective-permute-start | bytes 4718600 | tf_op jit(solution)/shard_map/ppermute | solution.py:36
  115.1 0.7 constant_dynamic-slice_fusion.2
  115.8 0.1 reshape_squeeze.2.table_ref
  115.9 0.9 copy-done.14
  116.7 14.9 %shard_map.67 = (f32[1024,512]{1,0:T(8,128)S(1)}, f32[1024,512]{1,0:T(8,128)}) custom-call(s32[16]{0:T(128)S(1)} %reshape_squeeze.2.table_ref, bf16[1024,768]{1,0:T(8,128)(2,1)} %refs_0_.5, bf16[1024,768]{1,0:T(8,128)(2,1)} %copy-done.4, bf16[1024,768]{1,0:T(8,128)(2,1)} %copy-done.5, bf16[1024,768]{1,0:T(8,128)(2,1)} %copy-done.9, ...), custom_call_target="tpu_custom_call" | custom-call | flops 9663676416 | bytes 18874368 | tf_op jit(solution)/shard_map/pallas_call | solution.py:131
  131.6 0.0 copy-start.15
  131.6 0.1 collective-permute-start.19
  131.7 4.8 %collective-permute-done.12.refs_11_ = bf16[512,768]{1,0:T(8,128)(2,1)S(1)} collective-permute-done((bf16[512,768]{1,0:T(8,128)(2,1)}, bf16[512,768]{1,0:T(8,128)(2,1)S(1)}, u32[]{:S(2)}, u32[]{:S(2)}) %collective-permute-start.12) | collective-permute-done | bytes 786464 | tf_op jit(solution)/shard_map/ppermute | solution.py:36
  136.5 5.5 %shard_map.69 = f32[1024,512]{1,0:T(8,128)} custom-call(s32[16]{0:T(128)S(1)} %reshape_squeeze.2.table_ref, bf16[1024,768]{1,0:T(8,128)(2,1)} %refs_0_.5, bf16[1024,768]{1,0:T(8,128)(2,1)} %copy-done.4, bf16[1024,768]{1,0:T(8,128)(2,1)} %copy-done.5, bf16[1024,768]{1,0:T(8,128)(2,1)} %copy-done.9, bf16[512,768]{1,0:T(8,128)(2,1)} %copy-done.12, ...), custom_call_target="tpu_custom_call" | custom-call | flops 1610612736 | bytes 4718592 | tf_op jit(solution)/shard_map/pallas_call | solution.py:131
  142.0 1.2 collective-permute-start.20
  143.2 1.9 %fusion.2 = (f32[1024,128]{1,0:T(8,128)S(1)}, f32[1024,128]{1,0:T(8,128)S(1)}) fusion(f32[128]{0:T(128)S(1)} %get-tuple-element.35, f32[128]{0:T(128)S(1)} %get-tuple-element.36, f32[1024]{0:T(1024)S(1)} %convert_element_type.10, pred[]{:T(512)S(6)} %lt.45), kind=kLoop, calls=%fused_computation.5 | loop fusion | flops 524288 | bytes 1053697 | tf_op jit(solution)/shard_map/jit(_where)/select_n | solution.py:234
  145.2 1.6 copy-done.1
  146.7 5.2 %shard_map.68.total_ref = f32[1024,512]{1,0:T(8,128)S(1)} custom-call(s32[16]{0:T(128)S(1)} %reshape_squeeze.2.table_ref, bf16[1024,768]{1,0:T(8,128)(2,1)} %refs_0_.5, bf16[1024,768]{1,0:T(8,128)(2,1)} %copy-done.4, bf16[1024,768]{1,0:T(8,128)(2,1)} %copy-done.5, bf16[1024,768]{1,0:T(8,128)(2,1)} %copy-done.9, bf16[512,768]{1,0:T(8,128)(2,1)} %copy-done.12, ...), custom_call_target="tpu_custom_call" | custom-call | flops 1610612736 | bytes 4718592 | tf_op jit(solution)/shard_map/pallas_call | solution.py:131
  152.0 2.4 %shard_map.70 = bf16[1024,512]{1,0:T(8,128)(2,1)S(1)} custom-call(f32[1024,512]{1,0:T(8,128)S(1)} %shard_map.68.total_ref, f32[1024,512]{1,0:T(8,128)} %collective-permute-done.20.received_ref, f32[1024,128]{1,0:T(8,128)S(1)} %get-tuple-element.34.cos_ref, f32[1024,128]{1,0:T(8,128)S(1)} %get-tuple-element.33.sin_ref), custom_call_target="tpu_custom_call" | custom-call | flops 2097152 | bytes 6291456 | tf_op jit(solution)/shard_map/pallas_call | solution.py:166
  154.4 18.0 %all_to_all.19 = bf16[16,64,512]{2,1,0:T(8,128)(2,1)S(1)} all-to-all(bf16[16,64,512]{2,1,0:T(8,128)(2,1)S(1)} %bitcast.6), channel_id=1, replica_groups=mesh['xh'=2,'y'=4,'xl'=2,'z'=4,'c'=2] {'xl','z','c'}, dimensions={0} | all-to-all | bytes 2097152 | tf_op jit(solution)/shard_map/all_to_all | solution.py:243
  172.4 0.1 copy.9
  172.5 0.9 slice.20
  173.4 0.7 fusion.7
  (42 shorter events, 0.1 us)
Async XLA Ops:
  0.6 3.1 %copy-start.2 = (bf16[1024,768]{1,0:T(8,128)(2,1)S(1)}, bf16[1024,768]{1,0:T(8,128)(2,1)}, u32[]{:S(2)}) copy-start(bf16[1024,768]{1,0:T(8,128)(2,1)} %refs_0_.5) | copy-start | bytes 4718596
  2.2 5.4 %collective-permute-start.2 = (bf16[768,512]{1,0:T(8,128)(2,1)S(1)}, bf16[768,512]{1,0:T(8,128)(2,1)S(1)}, u32[]{:S(2)}, u32[]{:S(2)}) collective-permute-start(bf16[768,512]{1,0:T(8,128)(2,1)S(1)} %get-tuple-element.30), channel_id=1, source_target_pairs={{0,1},{1,0},{2,3},{3,2},{4,5},{5,4},{6,7},{7,6},{8,9},{9,8},{10,11... | collective-permute-start | bytes 2359304 | tf_op jit(solution)/shard_map/ppermute | solution.py:179
  3.8 37.4 %collective-permute-start = (bf16[1024,768]{1,0:T(8,128)(2,1)S(1)}, bf16[1024,768]{1,0:T(8,128)(2,1)S(1)}, u32[]{:S(2)}, u32[]{:S(2)}) collective-permute-start(bf16[1024,768]{1,0:T(8,128)(2,1)S(1)} %copy-done.2), channel_id=1, source_target_pairs={{0,2},{1,7},{2,4},{3,1},{4,6},{5,3},{6,0},{7,5},{8,10},{9,15},{10,... | collective-permute-start | bytes 4718600 | tf_op jit(solution)/shard_map/ppermute | solution.py:36
  7.6 35.3 %collective-permute-start.1 = (bf16[1024,768]{1,0:T(8,128)(2,1)S(1)}, bf16[1024,768]{1,0:T(8,128)(2,1)S(1)}, u32[]{:S(2)}, u32[]{:S(2)}) collective-permute-start(bf16[1024,768]{1,0:T(8,128)(2,1)S(1)} %copy-done.2), channel_id=1, source_target_pairs={{0,6},{1,3},{2,0},{3,5},{4,2},{5,7},{6,4},{7,1},{8,14},{9,11},{10,... | collective-permute-start | bytes 4718600 | tf_op jit(solution)/shard_map/ppermute | solution.py:36
  7.8 40.7 %copy-start.3 = (bf16[768,1024]{1,0:T(8,128)(2,1)}, bf16[768,1024]{1,0:T(8,128)(2,1)S(1)}, u32[]{:S(2)}) copy-start(bf16[768,1024]{1,0:T(8,128)(2,1)S(1)} %pad_maximum_fusion.refs_10_.refs_12_) | copy-start | bytes 4718596
  7.8 37.1 %collective-permute-start.3 = (bf16[768,1024]{1,0:T(8,128)(2,1)S(1)}, bf16[768,1024]{1,0:T(8,128)(2,1)S(1)}, u32[]{:S(2)}, u32[]{:S(2)}) collective-permute-start(bf16[768,1024]{1,0:T(8,128)(2,1)S(1)} %pad_maximum_fusion.refs_10_.refs_12_), channel_id=1, source_target_pairs={{0,64},{64,0},{1,65},{65,1},{2,66},{66,2},{3,67},{67,3},{4,68},{68... | collective-permute-start | bytes 4718600 | tf_op jit(solution)/shard_map/ppermute | solution.py:179
  10.7 39.2 %collective-permute-start.13 = (bf16[768,1024]{1,0:T(8,128)(2,1)S(1)}, bf16[768,1024]{1,0:T(8,128)(2,1)S(1)}, u32[]{:S(2)}, u32[]{:S(2)}) collective-permute-start(bf16[768,1024]{1,0:T(8,128)(2,1)S(1)} %pad_maximum_fusion.refs_10_.refs_12_), channel_id=1, source_target_pairs={{0,16},{1,49},{16,32},{17,1},{32,48},{33,17},{48,0},{49,33},{2,18}... | collective-permute-start | bytes 4718600 | tf_op jit(solution)/shard_map/ppermute | solution.py:36
  13.4 36.5 %collective-permute-start.14 = (bf16[768,1024]{1,0:T(8,128)(2,1)S(1)}, bf16[768,1024]{1,0:T(8,128)(2,1)S(1)}, u32[]{:S(2)}, u32[]{:S(2)}) collective-permute-start(bf16[768,1024]{1,0:T(8,128)(2,1)S(1)} %pad_maximum_fusion.refs_10_.refs_12_), channel_id=1, source_target_pairs={{0,48},{1,17},{16,0},{17,33},{32,16},{33,49},{48,32},{49,1},{2,50}... | collective-permute-start | bytes 4718600 | tf_op jit(solution)/shard_map/ppermute | solution.py:36
  41.2 7.4 %copy-start.4 = (bf16[1024,768]{1,0:T(8,128)(2,1)}, bf16[1024,768]{1,0:T(8,128)(2,1)S(1)}, u32[]{:S(2)}) copy-start(bf16[1024,768]{1,0:T(8,128)(2,1)S(1)} %collective-permute-done.refs_1_) | copy-start | bytes 4718596
  42.9 51.7 %copy-start.5 = (bf16[1024,768]{1,0:T(8,128)(2,1)}, bf16[1024,768]{1,0:T(8,128)(2,1)S(1)}, u32[]{:S(2)}) copy-start(bf16[1024,768]{1,0:T(8,128)(2,1)S(1)} %collective-permute-done.1.refs_2_) | copy-start | bytes 4718596
  44.9 65.6 %copy-start.6 = (bf16[768,1024]{1,0:T(8,128)(2,1)}, bf16[768,1024]{1,0:T(8,128)(2,1)S(1)}, u32[]{:S(2)}) copy-start(bf16[768,1024]{1,0:T(8,128)(2,1)S(1)} %collective-permute-done.3.refs_14_.refs_16_) | copy-start | bytes 4718596
  44.9 21.7 %collective-permute-start.4 = (bf16[1024,768]{1,0:T(8,128)(2,1)S(1)}, bf16[1024,768]{1,0:T(8,128)(2,1)S(1)}, u32[]{:S(2)}, u32[]{:S(2)}) collective-permute-start(bf16[1024,768]{1,0:T(8,128)(2,1)S(1)} %collective-permute-done.refs_1_), channel_id=1, source_target_pairs={{0,2},{1,7},{2,4},{3,1},{4,6},{5,3},{6,0},{7,5},{8,10},{9,15},{10,... | collective-permute-start | bytes 4718600 | tf_op jit(solution)/shard_map/ppermute | solution.py:36
  48.6 18.1 %collective-permute-start.5 = (bf16[512,768]{1,0:T(8,128)(2,1)S(1)}, bf16[512,768]{1,0:T(8,128)(2,1)S(1)}, u32[]{:S(2)}, u32[]{:S(2)}) collective-permute-start(bf16[512,768]{1,0:T(8,128)(2,1)S(1)} %get-tuple-element.16), channel_id=1, source_target_pairs={{0,8},{8,0},{1,9},{9,1},{2,10},{10,2},{3,11},{11,3},{4,12},{12,4},... | collective-permute-start | bytes 2359304 | tf_op jit(solution)/shard_map/ppermute | solution.py:179
  49.9 60.6 %copy-start.7 = (bf16[768,1024]{1,0:T(8,128)(2,1)}, bf16[768,1024]{1,0:T(8,128)(2,1)S(1)}, u32[]{:S(2)}) copy-start(bf16[768,1024]{1,0:T(8,128)(2,1)S(1)} %collective-permute-done.13.refs_11_.refs_13_) | copy-start | bytes 4718596
  49.9 60.6 %copy-start.8 = (bf16[768,1024]{1,0:T(8,128)(2,1)}, bf16[768,1024]{1,0:T(8,128)(2,1)S(1)}, u32[]{:S(2)}) copy-start(bf16[768,1024]{1,0:T(8,128)(2,1)S(1)} %collective-permute-done.14.refs_12_.refs_14_) | copy-start | bytes 4718596
  49.9 36.2 %collective-permute-start.15 = (bf16[768,1024]{1,0:T(8,128)(2,1)S(1)}, bf16[768,1024]{1,0:T(8,128)(2,1)}, u32[]{:S(2)}, u32[]{:S(2)}) collective-permute-start(bf16[768,1024]{1,0:T(8,128)(2,1)S(1)} %collective-permute-done.3.refs_14_.refs_16_), channel_id=1, source_target_pairs={{0,16},{1,49},{16,32},{17,1},{32,48},{33,17},{48,0},{49,33},{2,18}... | collective-permute-start | bytes 4718600 | tf_op jit(solution)/shard_map/ppermute | solution.py:36
  52.7 34.0 %collective-permute-start.16 = (bf16[768,1024]{1,0:T(8,128)(2,1)S(1)}, bf16[768,1024]{1,0:T(8,128)(2,1)S(1)}, u32[]{:S(2)}, u32[]{:S(2)}) collective-permute-start(bf16[768,1024]{1,0:T(8,128)(2,1)S(1)} %collective-permute-done.3.refs_14_.refs_16_), channel_id=1, source_target_pairs={{0,48},{1,17},{16,0},{17,33},{32,16},{33,49},{48,32},{49,1},{2,50}... | collective-permute-start | bytes 4718600 | tf_op jit(solution)/shard_map/ppermute | solution.py:36
  66.6 43.9 %copy-start.12 = (bf16[512,768]{1,0:T(8,128)(2,1)}, bf16[512,768]{1,0:T(8,128)(2,1)S(1)}, u32[]{:S(2)}) copy-start(bf16[512,768]{1,0:T(8,128)(2,1)S(1)} %collective-permute-done.5.refs_4_) | copy-start | bytes 2359300
  66.6 43.9 %copy-start.9 = (bf16[1024,768]{1,0:T(8,128)(2,1)}, bf16[1024,768]{1,0:T(8,128)(2,1)S(1)}, u32[]{:S(2)}) copy-start(bf16[1024,768]{1,0:T(8,128)(2,1)S(1)} %collective-permute-done.4.refs_3_) | copy-start | bytes 4718596
  66.6 20.0 %collective-permute-start.6 = (bf16[512,768]{1,0:T(8,128)(2,1)S(1)}, bf16[512,768]{1,0:T(8,128)(2,1)S(1)}, u32[]{:S(2)}, u32[]{:S(2)}) collective-permute-start(bf16[512,768]{1,0:T(8,128)(2,1)S(1)} %get-tuple-element.17), channel_id=1, source_target_pairs={{0,8},{8,0},{1,9},{9,1},{2,10},{10,2},{3,11},{11,3},{4,12},{12,4},... | collective-permute-start | bytes 2359304 | tf_op jit(solution)/shard_map/ppermute | solution.py:179
  67.9 18.7 %collective-permute-start.7 = (bf16[512,768]{1,0:T(8,128)(2,1)S(1)}, bf16[512,768]{1,0:T(8,128)(2,1)}, u32[]{:S(2)}, u32[]{:S(2)}) collective-permute-start(bf16[512,768]{1,0:T(8,128)(2,1)S(1)} %collective-permute-done.5.refs_4_), channel_id=1, source_target_pairs={{0,2},{1,7},{2,4},{3,1},{4,6},{5,3},{6,0},{7,5},{8,10},{9,15},{10,... | collective-permute-start | bytes 2359304 | tf_op jit(solution)/shard_map/ppermute | solution.py:36
  70.5 19.9 %collective-permute-start.8 = (bf16[512,768]{1,0:T(8,128)(2,1)S(1)}, bf16[512,768]{1,0:T(8,128)(2,1)}, u32[]{:S(2)}, u32[]{:S(2)}) collective-permute-start(bf16[512,768]{1,0:T(8,128)(2,1)S(1)} %collective-permute-done.5.refs_4_), channel_id=1, source_target_pairs={{0,6},{1,3},{2,0},{3,5},{4,2},{5,7},{6,4},{7,1},{8,14},{9,11},{10,... | collective-permute-start | bytes 2359304 | tf_op jit(solution)/shard_map/ppermute | solution.py:36
  86.7 23.9 %copy-start.10 = (bf16[768,1024]{1,0:T(8,128)(2,1)}, bf16[768,1024]{1,0:T(8,128)(2,1)S(1)}, u32[]{:S(2)}) copy-start(bf16[768,1024]{1,0:T(8,128)(2,1)S(1)} %collective-permute-done.16.refs_16_.refs_18_) | copy-start | bytes 4718596
  86.7 29.2 %copy-start.13 = (bf16[512,768]{1,0:T(8,128)(2,1)}, bf16[512,768]{1,0:T(8,128)(2,1)S(1)}, u32[]{:S(2)}) copy-start(bf16[512,768]{1,0:T(8,128)(2,1)S(1)} %collective-permute-done.6.refs_5_) | copy-start | bytes 2359300
  90.4 20.1 %collective-permute-start.17 = (bf16[768,1024]{1,0:T(8,128)(2,1)S(1)}, bf16[768,1024]{1,0:T(8,128)(2,1)S(1)}, u32[]{:S(2)}, u32[]{:S(2)}) collective-permute-start(bf16[768,1024]{1,0:T(8,128)(2,1)S(1)} %collective-permute-done.13.refs_11_.refs_13_), channel_id=1, source_target_pairs={{0,16},{1,49},{16,32},{17,1},{32,48},{33,17},{48,0},{49,33},{2,18}... | collective-permute-start | bytes 4718600 | tf_op jit(solution)/shard_map/ppermute | solution.py:36
  93.1 22.7 %collective-permute-start.9 = (bf16[512,768]{1,0:T(8,128)(2,1)S(1)}, bf16[512,768]{1,0:T(8,128)(2,1)S(1)}, u32[]{:S(2)}, u32[]{:S(2)}) collective-permute-start(bf16[512,768]{1,0:T(8,128)(2,1)S(1)} %collective-permute-done.6.refs_5_), channel_id=1, source_target_pairs={{0,2},{1,7},{2,4},{3,1},{4,6},{5,3},{6,0},{7,5},{8,10},{9,15},{10,... | collective-permute-start | bytes 2359304 | tf_op jit(solution)/shard_map/ppermute | solution.py:36
  93.1 22.7 %collective-permute-start.10 = (bf16[512,768]{1,0:T(8,128)(2,1)S(1)}, bf16[512,768]{1,0:T(8,128)(2,1)}, u32[]{:S(2)}, u32[]{:S(2)}) collective-permute-start(bf16[512,768]{1,0:T(8,128)(2,1)S(1)} %collective-permute-done.6.refs_5_), channel_id=1, source_target_pairs={{0,6},{1,3},{2,0},{3,5},{4,2},{5,7},{6,4},{7,1},{8,14},{9,11},{10,... | collective-permute-start | bytes 2359304 | tf_op jit(solution)/shard_map/ppermute | solution.py:36
  110.5 1.1 copy-start.11
  111.7 24.9 %collective-permute-start.18 = (bf16[768,1024]{1,0:T(8,128)(2,1)}, bf16[768,1024]{1,0:T(8,128)(2,1)S(1)}, u32[]{:S(2)}, u32[]{:S(2)}) collective-permute-start(bf16[768,1024]{1,0:T(8,128)(2,1)} %collective-permute-done.15.refs_15_.refs_17_), channel_id=1, source_target_pairs={{0,16},{1,49},{16,32},{17,1},{32,48},{33,17},{48,0},{49,33},{2,18}... | collective-permute-start | bytes 4718600 | tf_op jit(solution)/shard_map/ppermute | solution.py:36
  115.9 0.9 copy-start.14
  116.7 15.0 %collective-permute-start.11 = (bf16[512,768]{1,0:T(8,128)(2,1)}, bf16[512,768]{1,0:T(8,128)(2,1)S(1)}, u32[]{:S(2)}, u32[]{:S(2)}) collective-permute-start(bf16[512,768]{1,0:T(8,128)(2,1)} %collective-permute-done.7.refs_6_), channel_id=1, source_target_pairs={{0,2},{1,7},{2,4},{3,1},{4,6},{5,3},{6,0},{7,5},{8,10},{9,15},{10,... | collective-permute-start | bytes 2359304 | tf_op jit(solution)/shard_map/ppermute | solution.py:36
  116.7 19.8 %collective-permute-start.12 = (bf16[512,768]{1,0:T(8,128)(2,1)}, bf16[512,768]{1,0:T(8,128)(2,1)S(1)}, u32[]{:S(2)}, u32[]{:S(2)}) collective-permute-start(bf16[512,768]{1,0:T(8,128)(2,1)} %copy-done.14), channel_id=1, source_target_pairs={{0,2},{1,7},{2,4},{3,1},{4,6},{5,3},{6,0},{7,5},{8,10},{9,15},{10,... | collective-permute-start | bytes 2359304 | tf_op jit(solution)/shard_map/ppermute | solution.py:36
  131.6 10.4 %copy-start = (f32[1024,512]{1,0:T(8,128)}, f32[1024,512]{1,0:T(8,128)S(1)}, u32[]{:S(2)}) copy-start(f32[1024,512]{1,0:T(8,128)S(1)} %get-tuple-element.25.refs_20_) | copy-start | bytes 6291460
  131.6 11.6 %copy-start.15 = (s32[1024]{0:T(1024)S(1)}, s32[1024]{0:T(1024)}, u32[]{:S(2)}) copy-start(s32[1024]{0:T(1024)} %param.6) | copy-start | bytes 12292
  131.6 13.5 %collective-permute-start.19 = (f32[1024,512]{1,0:T(8,128)}, f32[1024,512]{1,0:T(8,128)}, u32[]{:S(2)}, u32[]{:S(2)}) collective-permute-start(f32[1024,512]{1,0:T(8,128)} %get-tuple-element.26), channel_id=1, source_target_pairs={{0,1},{1,0},{2,3},{3,2},{4,5},{5,4},{6,7},{7,6},{8,9},{9,8},{10,11... | collective-permute-start | bytes 6291464 | tf_op jit(solution)/shard_map/ppermute | solution.py:179
  142.0 9.9 %collective-permute-start.20 = (f32[1024,512]{1,0:T(8,128)}, f32[1024,512]{1,0:T(8,128)}, u32[]{:S(2)}, u32[]{:S(2)}) collective-permute-start(f32[1024,512]{1,0:T(8,128)} %shard_map.69), channel_id=1, source_target_pairs={{0,1},{1,0},{2,3},{3,2},{4,5},{5,4},{6,7},{7,6},{8,9},{9,8},{10,11... | collective-permute-start | bytes 6291464 | tf_op jit(solution)/shard_map/ppermute | solution.py:179
  145.2 1.6 copy-start.1

commit v4 on v3

--- a/solution.py
+++ b/solution.py
@@ -147,17 +147,19 @@
     )(*operands, *totals)
 
 
-def turn(total, received, cosine, sine):
-    rows, columns = total.shape
+def turn(totals, cosine, sine):
+    rows, columns = totals[0].shape
     tile = 256
 
-    def kernel(total_ref, received_ref, cos_ref, sin_ref, out_ref):
+    def kernel(*refs):
+        *total_refs, cos_ref, sin_ref, out_ref = refs
+
         @pl.loop(0, rows // tile)
         def _(i):
             span = pl.ds(pl.multiple_of(i * tile, tile), tile)
             for h in range(columns // HEAD_WIDTH):
                 lanes = slice(h * HEAD_WIDTH, (h + 1) * HEAD_WIDTH)
-                head = total_ref[span, lanes] + received_ref[span, lanes]
+                head = sum(ref[span, lanes] for ref in total_refs)
                 swapped = pltpu.roll(head, HEAD_WIDTH // 2, 1)
                 out_ref[span, lanes] = (head * cos_ref[span, :] + swapped * sin_ref[span, :]).astype(
                     jnp.bfloat16
@@ -168,7 +170,7 @@
         out_shape=jax.ShapeDtypeStruct((rows, columns), jnp.bfloat16),
         compiler_params=pltpu.CompilerParams(vmem_limit_bytes=24 * 1024 * 1024),
         cost_estimate=pl.CostEstimate(flops=rows * columns * 4, bytes_accessed=rows * columns * 12, transcendentals=0),
-    )(total, received, cosine, sine)
+    )(*totals, cosine, sine)
 
 
 def after(block, *before):
@@ -182,25 +184,25 @@
 def gathers(a, b):
     part = a.shape[0] // 2
 
-    z_near, z_other = ring_step(a, "z"), ring_step(a, "z", -1)
-    y_near, y_other = ring_step(b, "y"), ring_step(b, "y", -1)
-    r = swap(b, "xh")
-
-    p_0 = swap(after(a[:part], r), "xl")
-    r_in = after(r, y_near, y_other)
-    r_near, r_other = ring_step(r_in, "y"), ring_step(r_in, "y", -1)
-    z_far = ring_step(after(z_near, z_other, r), "z")
-
-    p_0_in = after(p_0, z_far)
-    p_0_near, p_0_other = ring_step(p_0_in, "z"), ring_step(p_0_in, "z", -1)
-    p_1 = swap(after(a[part:], p_0, z_far), "xl")
-
-    y_far = ring_step(after(y_near, r_near, r_other, p_1, p_0_near, p_0_other), "y")
-    p_1_in = after(p_1, p_0_near, p_0_other)
-    p_1_near, p_1_other = ring_step(p_1_in, "z"), ring_step(p_1_in, "z", -1)
-
-    r_far = ring_step(after(r_near, y_far), "y")
-    p_0_far = ring_step(after(p_0_near, p_1_near, p_1_other), "z")
+    z_near = ring_step(a, "z")
+    p_0 = swap(a[:part], "xl")
+    y_near = ring_step(b, "y")
+    z_other = ring_step(a, "z", -1)
+    y_other = ring_step(b, "y", -1)
+
+    r = swap(after(b, p_0), "xh")
+    p_0_near = ring_step(after(p_0, z_near), "z")
+    p_0_other = ring_step(after(p_0, z_other), "z", -1)
+    y_far = ring_step(after(y_near, y_other), "y")
+    z_far = ring_step(after(z_near, p_0_near), "z")
+    p_0_far = ring_step(after(p_0_near, p_0_other), "z")
+
+    p_1 = swap(after(a[part:], r), "xl")
+    r_near = ring_step(after(r, y_other), "y")
+    r_other = ring_step(after(r, y_far), "y", -1)
+    p_1_near = ring_step(after(p_1, z_far, p_0_far), "z")
+    p_1_other = ring_step(after(p_1, z_far, p_0_far), "z", -1)
+    r_far = ring_step(after(r_near, p_1_near), "y")
     p_1_far = ring_step(after(p_1_near, p_1_other), "z")
 
     a_blocks = [
@@ -234,12 +236,13 @@
     cosine, sine = jnp.where(rotated, cosine, 1.0), jnp.where(rotated, sine, 0.0)
 
     early_a, early_b = a_blocks[:7] + [None], b_blocks[:7] + [None]
+    table, cosine, sine = lax.optimization_barrier((table, cosine, sine))
     early, early_sent = product(table, 0, EARLY, early_a, early_b, (0, 1))
     early_received = swap(early_sent, "c")
     (late_sent,) = product(table, EARLY, 8 - EARLY, a_blocks, b_blocks, (1,))
     late_received = swap(late_sent, "c")
-    (total,) = product(table, EARLY, 8 - EARLY, a_blocks, b_blocks, (0,), (early, early_received))
-    turned = turn(total, late_received, cosine, sine)
+    (total,) = product(table, EARLY, 8 - EARLY, a_blocks, b_blocks, (0,), (early,))
+    turned = turn([total, early_received, late_received], cosine, sine)
     received = lax.all_to_all(turned, ("xl", "z", "c"), split_axis=0, concat_axis=1, tiled=True)
     query_columns = QUERY_HEADS * HEAD_WIDTH
     rotated_columns = (QUERY_HEADS + KEY_VALUE_HEADS) * HEAD_WIDTH

time: 175 us -> 162 us (0.926)
  waiting for transfers between devices: 86 us -> 76.2 us
  Pallas kernels: 28 us -> 22.8 us
  starting transfers between devices: 31.3 us -> 36 us
  local copies, waits for them, and re-layouts: 7.83 us -> 5.26 us
    ppermute x15, waiting for transfers between devices: 70 us -> 31.7 us  [ring_step(): return lax.ppermute(block, (axis, 'c'), pairs)]
    ppermute x6, waiting for transfers between devices: 15.9 us -> 44.5 us  [swap(): return lax.ppermute(block, axis, SWAP)]
    pallas_call x3, Pallas kernels: 25.5 us -> 21.8 us  [product(): pl.pallas_call(kernel, out_shape=[jax.ShapeDtypeStruct((rows, width), jnp...]
    ppermute x15, starting transfers between devices: 23.2 us -> 26.1 us  [ring_step(): return lax.ppermute(block, (axis, 'c'), pairs)]
    unnamed x32 -> x26, local copies, waits for them, and re-layouts: 3.62 us -> 0.96 us
  transfers between devices with their start and end apart: 21 -> 21, of which waited for: 9 -> 9; matrix products, arithmetic and copies ran while one was open for 2% -> 2% of each run, Pallas kernels for 15% -> 13%
where the time goes in v4:
time: 162 us
  waiting for transfers between devices  76.2 us (47%)
  starting transfers between devices  36 us (22%)
  Pallas kernels  22.8 us (14%)
  blocking collectives  18.8 us (12%)
  local copies, waits for them, and re-layouts  5.26 us (3%)
  other arithmetic  2.16 us (1%)
    ppermute x6, waiting for transfers between devices, swap(): return lax.ppermute(block, axis, SWAP)  44.5 us
    ppermute x15, waiting for transfers between devices, ring_step(): return lax.ppermute(block, (axis, 'c'), pairs)  31.7 us
    ppermute x15, starting transfers between devices, ring_step(): return lax.ppermute(block, (axis, 'c'), pairs)  26.1 us
    pallas_call x3, Pallas kernels, product(): pl.pallas_call(kernel, out_shape=[jax.ShapeDtypeStruct((rows, width), jnp...  21.8 us
    all_to_all x1, blocking collectives, shards(): lax.all_to_all(turned, ('xl', 'z', 'c'), split_axis=0, concat_axis=1, til...  18.8 us
    ppermute x6, starting transfers between devices, swap(): return lax.ppermute(block, axis, SWAP)  9.87 us
  transfers between devices with their start and end apart: 21, of which 9 were waited for; matrix products, arithmetic and copies ran while one was open for 2% of the time, Pallas kernels for 13%

profile of v4, /device:TPU:1, one launch (start us, length us, event | category | flops | bytes accessed | tf_op | source)
XLA Modules:
  0.0 162.1 jit_solution(4878690880819235819)
XLA Ops:
  0.6 0.0 copy-start
  0.6 1.6 constant_dynamic-slice_fusion.1
  2.2 1.5 collective-permute-start.5
  3.8 3.8 %collective-permute-start = (bf16[1024,768]{1,0:T(8,128)(2,1)S(1)}, bf16[1024,768]{1,0:T(8,128)(2,1)S(1)}, u32[]{:S(2)}, u32[]{:S(2)}) collective-permute-start(bf16[1024,768]{1,0:T(8,128)(2,1)S(1)} %copy-done), channel_id=1, source_target_pairs={{0,2},{1,7},{2,4},{3,1},{4,6},{5,3},{6,0},{7,5},{8,10},{9,15},{10,... | collective-permute-start | bytes 4718600 | tf_op jit(solution)/shard_map/ppermute | solution.py:36
  7.6 0.2 pad_maximum_fusion.refs_10_.refs_12_
  7.8 0.0 copy-start.12
  7.8 2.8 %collective-permute-start.13 = (bf16[768,1024]{1,0:T(8,128)(2,1)S(1)}, bf16[768,1024]{1,0:T(8,128)(2,1)S(1)}, u32[]{:S(2)}, u32[]{:S(2)}) collective-permute-start(bf16[768,1024]{1,0:T(8,128)(2,1)S(1)} %pad_maximum_fusion.refs_10_.refs_12_), channel_id=1, source_target_pairs={{0,16},{1,49},{16,32},{17,1},{32,48},{33,17},{48,0},{49,33},{2,18}... | collective-permute-start | bytes 4718600 | tf_op jit(solution)/shard_map/ppermute | solution.py:36
  10.7 0.0 collective-permute-start.14
  10.7 0.1 fusion.6
  10.8 1.3 collective-permute-start.2
  12.1 0.0 collective-permute-start.1
  12.1 17.7 %collective-permute-done.2.refs_4_ = bf16[512,768]{1,0:T(8,128)(2,1)S(1)} collective-permute-done((bf16[512,768]{1,0:T(8,128)(2,1)S(1)}, bf16[512,768]{1,0:T(8,128)(2,1)S(1)}, u32[]{:S(2)}, u32[]{:S(2)}) %collective-permute-start.2) | collective-permute-done | bytes 786464 | tf_op jit(solution)/shard_map/ppermute | solution.py:181
  29.8 2.8 %collective-permute-start.6 = (bf16[768,1024]{1,0:T(8,128)(2,1)S(1)}, bf16[768,1024]{1,0:T(8,128)(2,1)}, u32[]{:S(2)}, u32[]{:S(2)}) collective-permute-start(bf16[768,1024]{1,0:T(8,128)(2,1)S(1)} %pad_maximum_fusion.refs_10_.refs_12_), channel_id=1, source_target_pairs={{0,64},{64,0},{1,65},{65,1},{2,66},{66,2},{3,67},{67,3},{4,68},{68... | collective-permute-start | bytes 4718600 | tf_op jit(solution)/shard_map/ppermute | solution.py:181
  32.6 1.1 collective-permute-done.refs_1_
  33.8 3.4 %collective-permute-start.3 = (bf16[512,768]{1,0:T(8,128)(2,1)S(1)}, bf16[512,768]{1,0:T(8,128)(2,1)S(1)}, u32[]{:S(2)}, u32[]{:S(2)}) collective-permute-start(bf16[512,768]{1,0:T(8,128)(2,1)S(1)} %collective-permute-done.2.refs_4_), channel_id=1, source_target_pairs={{0,2},{1,7},{2,4},{3,1},{4,6},{5,3},{6,0},{7,5},{8,10},{9,15},{10,... | collective-permute-start | bytes 2359304 | tf_op jit(solution)/shard_map/ppermute | solution.py:36
  37.2 6.8 %collective-permute-done.13.refs_11_.refs_13_ = bf16[768,1024]{1,0:T(8,128)(2,1)S(1)} collective-permute-done((bf16[768,1024]{1,0:T(8,128)(2,1)S(1)}, bf16[768,1024]{1,0:T(8,128)(2,1)S(1)}, u32[]{:S(2)}, u32[]{:S(2)}) %collective-permute-start.13) | collective-permute-done | bytes 1572896 | tf_op jit(solution)/shard_map/ppermute | solution.py:36
  44.0 0.6 collective-permute-done.14.refs_12_.refs_14_
  44.5 3.0 %collective-permute-start.15 = (bf16[768,1024]{1,0:T(8,128)(2,1)S(1)}, bf16[768,1024]{1,0:T(8,128)(2,1)S(1)}, u32[]{:S(2)}, u32[]{:S(2)}) collective-permute-start(bf16[768,1024]{1,0:T(8,128)(2,1)S(1)} %collective-permute-done.13.refs_11_.refs_13_), channel_id=1, source_target_pairs={{0,16},{1,49},{16,32},{17,1},{32,48},{33,17},{48,0},{49,33},{2,18}... | collective-permute-start | bytes 4718600 | tf_op jit(solution)/shard_map/ppermute | solution.py:36
  47.6 0.0 collective-permute-done.1.refs_2_
  47.6 2.6 %collective-permute-done.3.refs_6_ = bf16[512,768]{1,0:T(8,128)(2,1)S(1)} collective-permute-done((bf16[512,768]{1,0:T(8,128)(2,1)S(1)}, bf16[512,768]{1,0:T(8,128)(2,1)S(1)}, u32[]{:S(2)}, u32[]{:S(2)}) %collective-permute-start.3) | collective-permute-done | bytes 786464 | tf_op jit(solution)/shard_map/ppermute | solution.py:36
  50.2 3.5 %collective-permute-start.4 = (bf16[1024,768]{1,0:T(8,128)(2,1)S(1)}, bf16[1024,768]{1,0:T(8,128)(2,1)S(1)}, u32[]{:S(2)}, u32[]{:S(2)}) collective-permute-start(bf16[1024,768]{1,0:T(8,128)(2,1)S(1)} %collective-permute-done.refs_1_), channel_id=1, source_target_pairs={{0,2},{1,7},{2,4},{3,1},{4,6},{5,3},{6,0},{7,5},{8,10},{9,15},{10,... | collective-permute-start | bytes 4718600 | tf_op jit(solution)/shard_map/ppermute | solution.py:36
  53.8 13.8 %collective-permute-done.6.refs_14_.refs_16_ = bf16[768,1024]{1,0:T(8,128)(2,1)} collective-permute-done((bf16[768,1024]{1,0:T(8,128)(2,1)S(1)}, bf16[768,1024]{1,0:T(8,128)(2,1)}, u32[]{:S(2)}, u32[]{:S(2)}) %collective-permute-start.6) | collective-permute-done | bytes 1572896 | tf_op jit(solution)/shard_map/ppermute | solution.py:181
  67.5 1.3 collective-permute-start.7
  68.8 0.0 collective-permute-done.8.refs_8_
  68.8 0.0 collective-permute-start.9
  68.8 4.2 %collective-permute-start.16 = (bf16[768,1024]{1,0:T(8,128)(2,1)}, bf16[768,1024]{1,0:T(8,128)(2,1)}, u32[]{:S(2)}, u32[]{:S(2)}) collective-permute-start(bf16[768,1024]{1,0:T(8,128)(2,1)} %collective-permute-done.6.refs_14_.refs_16_), channel_id=1, source_target_pairs={{0,16},{1,49},{16,32},{17,1},{32,48},{33,17},{48,0},{49,33},{2,18}... | collective-permute-start | bytes 4718600 | tf_op jit(solution)/shard_map/ppermute | solution.py:36
  73.0 13.0 %collective-permute-done.7.refs_5_ = bf16[512,768]{1,0:T(8,128)(2,1)} collective-permute-done((bf16[512,768]{1,0:T(8,128)(2,1)S(1)}, bf16[512,768]{1,0:T(8,128)(2,1)}, u32[]{:S(2)}, u32[]{:S(2)}) %collective-permute-start.7) | collective-permute-done | bytes 786464 | tf_op jit(solution)/shard_map/ppermute | solution.py:181
  86.0 0.0 collective-permute-done.9.refs_10_
  86.0 1.9 %collective-permute-start.10 = (bf16[512,768]{1,0:T(8,128)(2,1)}, bf16[512,768]{1,0:T(8,128)(2,1)S(1)}, u32[]{:S(2)}, u32[]{:S(2)}) collective-permute-start(bf16[512,768]{1,0:T(8,128)(2,1)} %collective-permute-done.7.refs_5_), channel_id=1, source_target_pairs={{0,2},{1,7},{2,4},{3,1},{4,6},{5,3},{6,0},{7,5},{8,10},{9,15},{10,... | collective-permute-start | bytes 2359304 | tf_op jit(solution)/shard_map/ppermute | solution.py:36
  87.9 19.3 %collective-permute-done.16.refs_15_.refs_17_ = bf16[768,1024]{1,0:T(8,128)(2,1)} collective-permute-done((bf16[768,1024]{1,0:T(8,128)(2,1)}, bf16[768,1024]{1,0:T(8,128)(2,1)}, u32[]{:S(2)}, u32[]{:S(2)}) %collective-permute-start.16) | collective-permute-done | bytes 1572896 | tf_op jit(solution)/shard_map/ppermute | solution.py:36
  107.3 0.9 copy-done.11
  108.2 3.4 %collective-permute-start.18 = (bf16[768,1024]{1,0:T(8,128)(2,1)}, bf16[768,1024]{1,0:T(8,128)(2,1)S(1)}, u32[]{:S(2)}, u32[]{:S(2)}) collective-permute-start(bf16[768,1024]{1,0:T(8,128)(2,1)} %collective-permute-done.16.refs_15_.refs_17_), channel_id=1, source_target_pairs={{0,16},{1,49},{16,32},{17,1},{32,48},{33,17},{48,0},{49,33},{2,18}... | collective-permute-start | bytes 4718600 | tf_op jit(solution)/shard_map/ppermute | solution.py:36
  111.6 0.7 dynamic-slice_bitcast_fusion
  112.3 1.9 %fusion.2 = (f32[1024,128]{1,0:T(8,128)S(1)}, f32[1024,128]{1,0:T(8,128)S(1)}) fusion(f32[128]{0:T(128)S(1)} %get-tuple-element.45, f32[128]{0:T(128)S(1)} %get-tuple-element.46, f32[1024]{0:T(1024)S(1)} %convert_element_type.10, pred[]{:T(512)S(6)} %lt.43), kind=kLoop, calls=%fused_computation.5 | loop fusion | flops 524288 | bytes 1053697 | tf_op jit(solution)/shard_map/jit(_where)/select_n | solution.py:236
  114.2 0.1 copy.9
  114.3 0.1 reshape.32.table_ref
  114.4 0.1 collective-permute-start.12
  114.5 13.5 %shard_map.67 = (f32[1024,512]{1,0:T(8,128)S(1)}, f32[1024,512]{1,0:T(8,128)S(1)}) custom-call(s32[16]{0:T(128)S(1)} %reshape.32.table_ref, bf16[1024,768]{1,0:T(8,128)(2,1)} %refs_0_.5, bf16[1024,768]{1,0:T(8,128)(2,1)} %copy-done.2, bf16[1024,768]{1,0:T(8,128)(2,1)} %copy-done.5, bf16[1024,768]{1,0:T(8,128)(2,1)} %copy-done.7, bf16[512,768]{1,0:T(8,128)(2,1)} %copy-done.8, ...), custom_call_target="tpu_custom_call" | custom-call | flops 9663676416 | bytes 18874368 | tf_op jit(solution)/shard_map/pallas_call | solution.py:131
  128.0 0.1 collective-permute-start.19
  128.1 1.2 collective-permute-done.18.refs_19_
  129.3 4.1 %shard_map.69 = f32[1024,512]{1,0:T(8,128)S(1)} custom-call(s32[16]{0:T(128)S(1)} %reshape.32.table_ref, bf16[1024,768]{1,0:T(8,128)(2,1)} %refs_0_.5, bf16[1024,768]{1,0:T(8,128)(2,1)} %copy-done.2, bf16[1024,768]{1,0:T(8,128)(2,1)} %copy-done.5, bf16[1024,768]{1,0:T(8,128)(2,1)} %copy-done.7, bf16[512,768]{1,0:T(8,128)(2,1)} %copy-done.8, ...), custom_call_target="tpu_custom_call" | custom-call | flops 1610612736 | bytes 4718592 | tf_op jit(solution)/shard_map/pallas_call | solution.py:131
  133.4 2.9 %collective-permute-start.20 = (f32[1024,512]{1,0:T(8,128)S(1)}, f32[1024,512]{1,0:T(8,128)S(1)}, u32[]{:S(2)}, u32[]{:S(2)}) collective-permute-start(f32[1024,512]{1,0:T(8,128)S(1)} %shard_map.69), channel_id=1, source_target_pairs={{0,1},{1,0},{2,3},{3,2},{4,5},{5,4},{6,7},{7,6},{8,9},{9,8},{10,11... | collective-permute-start | bytes 6291464 | tf_op jit(solution)/shard_map/ppermute | solution.py:181
  136.3 4.1 %shard_map.68.refs_0_ = f32[1024,512]{1,0:T(8,128)S(1)} custom-call(s32[16]{0:T(128)S(1)} %reshape.32.table_ref, bf16[1024,768]{1,0:T(8,128)(2,1)} %refs_0_.5, bf16[1024,768]{1,0:T(8,128)(2,1)} %copy-done.2, bf16[1024,768]{1,0:T(8,128)(2,1)} %copy-done.5, bf16[1024,768]{1,0:T(8,128)(2,1)} %copy-done.7, bf16[512,768]{1,0:T(8,128)(2,1)} %copy-done.8, ...), custom_call_target="tpu_custom_call" | custom-call | flops 1610612736 | bytes 4718592 | tf_op jit(solution)/shard_map/pallas_call | solution.py:131
  140.5 1.1 shard_map.70
  141.5 18.8 %all_to_all.19 = bf16[16,64,512]{2,1,0:T(8,128)(2,1)S(1)} all-to-all(bf16[16,64,512]{2,1,0:T(8,128)(2,1)S(1)} %bitcast.6), channel_id=1, replica_groups=mesh['xh'=2,'y'=4,'xl'=2,'z'=4,'c'=2] {'xl','z','c'}, dimensions={0} | all-to-all | bytes 2097152 | tf_op jit(solution)/shard_map/all_to_all | solution.py:246
  160.3 0.1 copy.11
  160.4 0.9 slice.20
  161.3 0.7 fusion.7
  (37 shorter events, 0.1 us)
Async XLA Ops:
  0.6 3.1 %copy-start = (bf16[1024,768]{1,0:T(8,128)(2,1)S(1)}, bf16[1024,768]{1,0:T(8,128)(2,1)}, u32[]{:S(2)}) copy-start(bf16[1024,768]{1,0:T(8,128)(2,1)} %refs_0_.5) | copy-start | bytes 4718596
  2.2 5.3 %collective-permute-start.5 = (bf16[768,512]{1,0:T(8,128)(2,1)S(1)}, bf16[768,512]{1,0:T(8,128)(2,1)S(1)}, u32[]{:S(2)}, u32[]{:S(2)}) collective-permute-start(bf16[768,512]{1,0:T(8,128)(2,1)S(1)} %get-tuple-element.38), channel_id=1, source_target_pairs={{0,1},{1,0},{2,3},{3,2},{4,5},{5,4},{6,7},{7,6},{8,9},{9,8},{10,11... | collective-permute-start | bytes 2359304 | tf_op jit(solution)/shard_map/ppermute | solution.py:181
  3.8 30.0 %collective-permute-start = (bf16[1024,768]{1,0:T(8,128)(2,1)S(1)}, bf16[1024,768]{1,0:T(8,128)(2,1)S(1)}, u32[]{:S(2)}, u32[]{:S(2)}) collective-permute-start(bf16[1024,768]{1,0:T(8,128)(2,1)S(1)} %copy-done), channel_id=1, source_target_pairs={{0,2},{1,7},{2,4},{3,1},{4,6},{5,3},{6,0},{7,5},{8,10},{9,15},{10,... | collective-permute-start | bytes 4718600 | tf_op jit(solution)/shard_map/ppermute | solution.py:36
  7.8 22.0 %copy-start.1 = (bf16[768,1024]{1,0:T(8,128)(2,1)}, bf16[768,1024]{1,0:T(8,128)(2,1)S(1)}, u32[]{:S(2)}) copy-start(bf16[768,1024]{1,0:T(8,128)(2,1)S(1)} %pad_maximum_fusion.refs_10_.refs_12_) | copy-start | bytes 4718596
  7.8 103.8 %copy-start.12 = (s32[1024]{0:T(1024)S(1)}, s32[1024]{0:T(1024)}, u32[]{:S(2)}) copy-start(s32[1024]{0:T(1024)} %param.6) | copy-start | bytes 12292
  7.8 36.1 %collective-permute-start.13 = (bf16[768,1024]{1,0:T(8,128)(2,1)S(1)}, bf16[768,1024]{1,0:T(8,128)(2,1)S(1)}, u32[]{:S(2)}, u32[]{:S(2)}) collective-permute-start(bf16[768,1024]{1,0:T(8,128)(2,1)S(1)} %pad_maximum_fusion.refs_10_.refs_12_), channel_id=1, source_target_pairs={{0,16},{1,49},{16,32},{17,1},{32,48},{33,17},{48,0},{49,33},{2,18}... | collective-permute-start | bytes 4718600 | tf_op jit(solution)/shard_map/ppermute | solution.py:36
  10.7 33.9 %collective-permute-start.14 = (bf16[768,1024]{1,0:T(8,128)(2,1)S(1)}, bf16[768,1024]{1,0:T(8,128)(2,1)S(1)}, u32[]{:S(2)}, u32[]{:S(2)}) collective-permute-start(bf16[768,1024]{1,0:T(8,128)(2,1)S(1)} %pad_maximum_fusion.refs_10_.refs_12_), channel_id=1, source_target_pairs={{0,48},{1,17},{16,0},{17,33},{32,16},{33,49},{48,32},{49,1},{2,50}... | collective-permute-start | bytes 4718600 | tf_op jit(solution)/shard_map/ppermute | solution.py:36
  10.8 19.0 %collective-permute-start.2 = (bf16[512,768]{1,0:T(8,128)(2,1)S(1)}, bf16[512,768]{1,0:T(8,128)(2,1)S(1)}, u32[]{:S(2)}, u32[]{:S(2)}) collective-permute-start(bf16[512,768]{1,0:T(8,128)(2,1)S(1)} %get-tuple-element.40), channel_id=1, source_target_pairs={{0,8},{8,0},{1,9},{9,1},{2,10},{10,2},{3,11},{11,3},{4,12},{12,4},... | collective-permute-start | bytes 2359304 | tf_op jit(solution)/shard_map/ppermute | solution.py:181
  12.1 35.5 %collective-permute-start.1 = (bf16[1024,768]{1,0:T(8,128)(2,1)S(1)}, bf16[1024,768]{1,0:T(8,128)(2,1)S(1)}, u32[]{:S(2)}, u32[]{:S(2)}) collective-permute-start(bf16[1024,768]{1,0:T(8,128)(2,1)S(1)} %copy-done), channel_id=1, source_target_pairs={{0,6},{1,3},{2,0},{3,5},{4,2},{5,7},{6,4},{7,1},{8,14},{9,11},{10,... | collective-permute-start | bytes 4718600 | tf_op jit(solution)/shard_map/ppermute | solution.py:36
  29.8 77.4 %copy-start.8 = (bf16[512,768]{1,0:T(8,128)(2,1)}, bf16[512,768]{1,0:T(8,128)(2,1)S(1)}, u32[]{:S(2)}) copy-start(bf16[512,768]{1,0:T(8,128)(2,1)S(1)} %collective-permute-done.2.refs_4_) | copy-start | bytes 2359300
  29.8 37.7 %collective-permute-start.6 = (bf16[768,1024]{1,0:T(8,128)(2,1)S(1)}, bf16[768,1024]{1,0:T(8,128)(2,1)}, u32[]{:S(2)}, u32[]{:S(2)}) collective-permute-start(bf16[768,1024]{1,0:T(8,128)(2,1)S(1)} %pad_maximum_fusion.refs_10_.refs_12_), channel_id=1, source_target_pairs={{0,64},{64,0},{1,65},{65,1},{2,66},{66,2},{3,67},{67,3},{4,68},{68... | collective-permute-start | bytes 4718600 | tf_op jit(solution)/shard_map/ppermute | solution.py:181
  33.8 73.4 %copy-start.2 = (bf16[1024,768]{1,0:T(8,128)(2,1)}, bf16[1024,768]{1,0:T(8,128)(2,1)S(1)}, u32[]{:S(2)}) copy-start(bf16[1024,768]{1,0:T(8,128)(2,1)S(1)} %collective-permute-done.refs_1_) | copy-start | bytes 4718596
  33.8 16.5 %collective-permute-start.3 = (bf16[512,768]{1,0:T(8,128)(2,1)S(1)}, bf16[512,768]{1,0:T(8,128)(2,1)S(1)}, u32[]{:S(2)}, u32[]{:S(2)}) collective-permute-start(bf16[512,768]{1,0:T(8,128)(2,1)S(1)} %collective-permute-done.2.refs_4_), channel_id=1, source_target_pairs={{0,2},{1,7},{2,4},{3,1},{4,6},{5,3},{6,0},{7,5},{8,10},{9,15},{10,... | collective-permute-start | bytes 2359304 | tf_op jit(solution)/shard_map/ppermute | solution.py:36
  44.0 63.2 %copy-start.3 = (bf16[768,1024]{1,0:T(8,128)(2,1)}, bf16[768,1024]{1,0:T(8,128)(2,1)S(1)}, u32[]{:S(2)}) copy-start(bf16[768,1024]{1,0:T(8,128)(2,1)S(1)} %collective-permute-done.13.refs_11_.refs_13_) | copy-start | bytes 4718596
  44.5 62.6 %copy-start.4 = (bf16[768,1024]{1,0:T(8,128)(2,1)}, bf16[768,1024]{1,0:T(8,128)(2,1)S(1)}, u32[]{:S(2)}) copy-start(bf16[768,1024]{1,0:T(8,128)(2,1)S(1)} %collective-permute-done.14.refs_12_.refs_14_) | copy-start | bytes 4718596
  44.5 28.4 %collective-permute-start.15 = (bf16[768,1024]{1,0:T(8,128)(2,1)S(1)}, bf16[768,1024]{1,0:T(8,128)(2,1)S(1)}, u32[]{:S(2)}, u32[]{:S(2)}) collective-permute-start(bf16[768,1024]{1,0:T(8,128)(2,1)S(1)} %collective-permute-done.13.refs_11_.refs_13_), channel_id=1, source_target_pairs={{0,16},{1,49},{16,32},{17,1},{32,48},{33,17},{48,0},{49,33},{2,18}... | collective-permute-start | bytes 4718600 | tf_op jit(solution)/shard_map/ppermute | solution.py:36
  47.6 59.6 %copy-start.5 = (bf16[1024,768]{1,0:T(8,128)(2,1)}, bf16[1024,768]{1,0:T(8,128)(2,1)S(1)}, u32[]{:S(2)}) copy-start(bf16[1024,768]{1,0:T(8,128)(2,1)S(1)} %collective-permute-done.1.refs_2_) | copy-start | bytes 4718596
  47.6 21.2 %collective-permute-start.8 = (bf16[512,768]{1,0:T(8,128)(2,1)S(1)}, bf16[512,768]{1,0:T(8,128)(2,1)S(1)}, u32[]{:S(2)}, u32[]{:S(2)}) collective-permute-start(bf16[512,768]{1,0:T(8,128)(2,1)S(1)} %collective-permute-done.2.refs_4_), channel_id=1, source_target_pairs={{0,6},{1,3},{2,0},{3,5},{4,2},{5,7},{6,4},{7,1},{8,14},{9,11},{10,... | collective-permute-start | bytes 2359304 | tf_op jit(solution)/shard_map/ppermute | solution.py:36
  50.2 57.0 %copy-start.9 = (bf16[512,768]{1,0:T(8,128)(2,1)}, bf16[512,768]{1,0:T(8,128)(2,1)S(1)}, u32[]{:S(2)}) copy-start(bf16[512,768]{1,0:T(8,128)(2,1)S(1)} %collective-permute-done.3.refs_6_) | copy-start | bytes 2359300
  50.2 35.8 %collective-permute-start.4 = (bf16[1024,768]{1,0:T(8,128)(2,1)S(1)}, bf16[1024,768]{1,0:T(8,128)(2,1)S(1)}, u32[]{:S(2)}, u32[]{:S(2)}) collective-permute-start(bf16[1024,768]{1,0:T(8,128)(2,1)S(1)} %collective-permute-done.refs_1_), channel_id=1, source_target_pairs={{0,2},{1,7},{2,4},{3,1},{4,6},{5,3},{6,0},{7,5},{8,10},{9,15},{10,... | collective-permute-start | bytes 4718600 | tf_op jit(solution)/shard_map/ppermute | solution.py:36
  67.5 18.5 %collective-permute-start.7 = (bf16[512,768]{1,0:T(8,128)(2,1)S(1)}, bf16[512,768]{1,0:T(8,128)(2,1)}, u32[]{:S(2)}, u32[]{:S(2)}) collective-permute-start(bf16[512,768]{1,0:T(8,128)(2,1)S(1)} %get-tuple-element.24), channel_id=1, source_target_pairs={{0,8},{8,0},{1,9},{9,1},{2,10},{10,2},{3,11},{11,3},{4,12},{12,4},... | collective-permute-start | bytes 2359304 | tf_op jit(solution)/shard_map/ppermute | solution.py:181
  68.8 38.4 %copy-start.10 = (bf16[512,768]{1,0:T(8,128)(2,1)}, bf16[512,768]{1,0:T(8,128)(2,1)S(1)}, u32[]{:S(2)}) copy-start(bf16[512,768]{1,0:T(8,128)(2,1)S(1)} %collective-permute-done.8.refs_8_) | copy-start | bytes 2359300
  68.8 17.2 %collective-permute-start.9 = (bf16[512,768]{1,0:T(8,128)(2,1)S(1)}, bf16[512,768]{1,0:T(8,128)(2,1)S(1)}, u32[]{:S(2)}, u32[]{:S(2)}) collective-permute-start(bf16[512,768]{1,0:T(8,128)(2,1)S(1)} %collective-permute-done.3.refs_6_), channel_id=1, source_target_pairs={{0,2},{1,7},{2,4},{3,1},{4,6},{5,3},{6,0},{7,5},{8,10},{9,15},{10,... | collective-permute-start | bytes 2359304 | tf_op jit(solution)/shard_map/ppermute | solution.py:36
  68.8 38.4 %collective-permute-start.16 = (bf16[768,1024]{1,0:T(8,128)(2,1)}, bf16[768,1024]{1,0:T(8,128)(2,1)}, u32[]{:S(2)}, u32[]{:S(2)}) collective-permute-start(bf16[768,1024]{1,0:T(8,128)(2,1)} %collective-permute-done.6.refs_14_.refs_16_), channel_id=1, source_target_pairs={{0,16},{1,49},{16,32},{17,1},{32,48},{33,17},{48,0},{49,33},{2,18}... | collective-permute-start | bytes 4718600 | tf_op jit(solution)/shard_map/ppermute | solution.py:36
  73.0 34.2 %copy-start.6 = (bf16[768,1024]{1,0:T(8,128)(2,1)}, bf16[768,1024]{1,0:T(8,128)(2,1)S(1)}, u32[]{:S(2)}) copy-start(bf16[768,1024]{1,0:T(8,128)(2,1)S(1)} %collective-permute-done.15.refs_13_.refs_15_) | copy-start | bytes 4718596
  73.0 41.5 %collective-permute-start.17 = (bf16[768,1024]{1,0:T(8,128)(2,1)}, bf16[768,1024]{1,0:T(8,128)(2,1)}, u32[]{:S(2)}, u32[]{:S(2)}) collective-permute-start(bf16[768,1024]{1,0:T(8,128)(2,1)} %collective-permute-done.6.refs_14_.refs_16_), channel_id=1, source_target_pairs={{0,48},{1,17},{16,0},{17,33},{32,16},{33,49},{48,32},{49,1},{2,50}... | collective-permute-start | bytes 4718600 | tf_op jit(solution)/shard_map/ppermute | solution.py:36
  86.0 21.2 %copy-start.7 = (bf16[1024,768]{1,0:T(8,128)(2,1)}, bf16[1024,768]{1,0:T(8,128)(2,1)S(1)}, u32[]{:S(2)}) copy-start(bf16[1024,768]{1,0:T(8,128)(2,1)S(1)} %collective-permute-done.4.refs_3_) | copy-start | bytes 4718596
  86.0 21.2 %collective-permute-start.10 = (bf16[512,768]{1,0:T(8,128)(2,1)}, bf16[512,768]{1,0:T(8,128)(2,1)S(1)}, u32[]{:S(2)}, u32[]{:S(2)}) collective-permute-start(bf16[512,768]{1,0:T(8,128)(2,1)} %collective-permute-done.7.refs_5_), channel_id=1, source_target_pairs={{0,2},{1,7},{2,4},{3,1},{4,6},{5,3},{6,0},{7,5},{8,10},{9,15},{10,... | collective-permute-start | bytes 2359304 | tf_op jit(solution)/shard_map/ppermute | solution.py:36
  87.9 26.5 %collective-permute-start.11 = (bf16[512,768]{1,0:T(8,128)(2,1)}, bf16[512,768]{1,0:T(8,128)(2,1)}, u32[]{:S(2)}, u32[]{:S(2)}) collective-permute-start(bf16[512,768]{1,0:T(8,128)(2,1)} %collective-permute-done.7.refs_5_), channel_id=1, source_target_pairs={{0,6},{1,3},{2,0},{3,5},{4,2},{5,7},{6,4},{7,1},{8,14},{9,11},{10,... | collective-permute-start | bytes 2359304 | tf_op jit(solution)/shard_map/ppermute | solution.py:36
  107.3 0.9 copy-start.11
  108.2 21.1 %collective-permute-start.18 = (bf16[768,1024]{1,0:T(8,128)(2,1)}, bf16[768,1024]{1,0:T(8,128)(2,1)S(1)}, u32[]{:S(2)}, u32[]{:S(2)}) collective-permute-start(bf16[768,1024]{1,0:T(8,128)(2,1)} %collective-permute-done.16.refs_15_.refs_17_), channel_id=1, source_target_pairs={{0,16},{1,49},{16,32},{17,1},{32,48},{33,17},{48,0},{49,33},{2,18}... | collective-permute-start | bytes 4718600 | tf_op jit(solution)/shard_map/ppermute | solution.py:36
  114.4 13.7 %collective-permute-start.12 = (bf16[512,768]{1,0:T(8,128)(2,1)}, bf16[512,768]{1,0:T(8,128)(2,1)S(1)}, u32[]{:S(2)}, u32[]{:S(2)}) collective-permute-start(bf16[512,768]{1,0:T(8,128)(2,1)} %copy-done.11), channel_id=1, source_target_pairs={{0,2},{1,7},{2,4},{3,1},{4,6},{5,3},{6,0},{7,5},{8,10},{9,15},{10,... | collective-permute-start | bytes 2359304 | tf_op jit(solution)/shard_map/ppermute | solution.py:36
  128.0 12.5 %collective-permute-start.19 = (f32[1024,512]{1,0:T(8,128)S(1)}, f32[1024,512]{1,0:T(8,128)S(1)}, u32[]{:S(2)}, u32[]{:S(2)}) collective-permute-start(f32[1024,512]{1,0:T(8,128)S(1)} %get-tuple-element.34), channel_id=1, source_target_pairs={{0,1},{1,0},{2,3},{3,2},{4,5},{5,4},{6,7},{7,6},{8,9},{9,8},{10,11... | collective-permute-start | bytes 6291464 | tf_op jit(solution)/shard_map/ppermute | solution.py:181
  133.4 7.0 %collective-permute-start.20 = (f32[1024,512]{1,0:T(8,128)S(1)}, f32[1024,512]{1,0:T(8,128)S(1)}, u32[]{:S(2)}, u32[]{:S(2)}) collective-permute-start(f32[1024,512]{1,0:T(8,128)S(1)} %shard_map.69), channel_id=1, source_target_pairs={{0,1},{1,0},{2,3},{3,2},{4,5},{5,4},{6,7},{7,6},{8,9},{9,8},{10,11... | collective-permute-start | bytes 6291464 | tf_op jit(solution)/shard_map/ppermute | solution.py:181

commit v5 on v4

--- a/solution.py
+++ b/solution.py
@@ -44,18 +44,18 @@
         a_blocks = {(xl ^ p, (z + d) % 4): p * 4 + i for p in range(2) for i, d in enumerate(places)}
         b_blocks = {(xh ^ p, (y + d) % 4): p * 4 + i for p in range(2) for i, d in enumerate(places)}
         pairs = [(a_blocks[f], b_blocks[f]) for f in np.ndindex(2, 4)]
-        table[xh, y, xl, z, c] = sorted(pairs, key=lambda p: (7 in p, max(p), p))
+        table[xh, y, xl, z, c] = sorted(pairs, key=lambda p: (7 in p, max(p[0] > 4, p[1] > 4), max(p), p))
     return table
 
 
 TABLE = piece_table()
-EARLY = 6
+FIRST, EARLY = 2, 6
 
 
 def product(table, first, count, a_blocks, b_blocks, parts, totals=()):
     depth = a_blocks[0][0].shape[1]
     rows = sum(v.shape[0] for v in a_blocks[0])
-    width = b_blocks[0].shape[1] // 2
+    width = b_blocks[0][0].shape[1] // 2
     slots = 2
     used_a = [p for p in range(len(a_blocks)) if a_blocks[p] is not None]
     used_b = [q for q in range(len(b_blocks)) if b_blocks[q] is not None]
@@ -64,7 +64,7 @@
     def kernel(table_ref, *refs):
         refs = list(refs)
         a_refs = {p: [refs.pop(0) for _ in a_blocks[p]] for p in used_a}
-        b_refs = {q: refs.pop(0) for q in used_b}
+        b_refs = {q: [refs.pop(0) for _ in b_blocks[q]] for q in used_b}
         total_refs = [refs.pop(0) for _ in totals]
         out_refs = [refs.pop(0) for _ in parts]
         a_buf, b_buf, sems = refs
@@ -88,9 +88,14 @@
 
                 @pl.when(b_id == q)
                 def _():
-                    pltpu.make_async_copy(
-                        b_refs[q].at[:, pl.ds(low, high - low)], b_buf.at[slot], sems.at[slot]
-                    ).start()
+                    row = 0
+                    for ref in b_refs[q]:
+                        pltpu.make_async_copy(
+                            ref.at[:, pl.ds(low, high - low)],
+                            b_buf.at[slot, pl.ds(row, ref.shape[0]), :],
+                            sems.at[slot],
+                        ).start()
+                        row += ref.shape[0]
 
         def wait(k):
             slot = lax.rem(k, slots)
@@ -98,11 +103,8 @@
             pltpu.make_async_copy(b_buf.at[slot], b_buf.at[slot], sems.at[slot]).wait()
 
         start(0)
-        if totals:
-            out_refs[0][...] = sum(ref[...] for ref in total_refs)
-        else:
-            for ref in out_refs:
-                ref[...] = jnp.zeros(ref.shape, jnp.float32)
+        for i, ref in enumerate(out_refs):
+            ref[...] = total_refs[i][...] if totals else jnp.zeros(ref.shape, jnp.float32)
 
         @pl.loop(0, count)
         def _(k):
@@ -121,8 +123,8 @@
 
     anywhere = pl.BlockSpec(memory_space=pl.ANY)
     vmem = pl.BlockSpec(memory_space=pltpu.VMEM)
-    pieces = [v for p in used_a for v in a_blocks[p]] + [b_blocks[q] for q in used_b]
-    late = [7 in used_a and p == 7 for p in used_a for _ in a_blocks[p]] + [q == 7 for q in used_b]
+    pieces = [v for p in used_a for v in a_blocks[p]] + [v for q in used_b for v in b_blocks[q]]
+    late = [p == 7 for p in used_a for _ in a_blocks[p]] + [q == 7 for q in used_b for _ in b_blocks[q]]
     operands = [table.reshape(-1)]
     operands += [
         pltpu.with_memory_space_constraint(v, pltpu.VMEM if near else pltpu.HBM)
@@ -181,8 +183,8 @@
     return lax.ppermute(block, axis, SWAP)
 
 
-def gathers(a, b):
-    part = a.shape[0] // 2
+def gathers(a, b, first_product, *early):
+    part = a.shape[0] // 8 * 6
 
     z_near = ring_step(a, "z")
     p_0 = swap(a[:part], "xl")
@@ -194,16 +196,20 @@
     p_0_near = ring_step(after(p_0, z_near), "z")
     p_0_other = ring_step(after(p_0, z_other), "z", -1)
     y_far = ring_step(after(y_near, y_other), "y")
-    z_far = ring_step(after(z_near, p_0_near), "z")
+    z_far = ring_step(after(z_near, p_0_near, *early), "z")
     p_0_far = ring_step(after(p_0_near, p_0_other), "z")
 
     p_1 = swap(after(a[part:], r), "xl")
     r_near = ring_step(after(r, y_other), "y")
-    r_other = ring_step(after(r, y_far), "y", -1)
+    r_other = ring_step(after(r, y_far, p_1), "y", -1)
+    split = b.shape[0] // 2
+    r_far_1 = swap(after(y_far[split:], p_1), "xh")
     p_1_near = ring_step(after(p_1, z_far, p_0_far), "z")
-    p_1_other = ring_step(after(p_1, z_far, p_0_far), "z", -1)
-    r_far = ring_step(after(r_near, p_1_near), "y")
-    p_1_far = ring_step(after(p_1_near, p_1_other), "z")
+    first = first_product([[a], [z_near], [z_other], [z_far], [p_0, p_1]], [[b], [y_near], [y_other], [y_far], [r]])
+    p_1_other = ring_step(after(p_1, z_far, p_0_far, *first), "z", -1)
+    p_1_far = ring_step(p_1_near, "z")
+    r_far_0 = ring_step(after(r_near[:split], r_far_1), "y")
+    r_far = [r_far_0, r_far_1]
 
     a_blocks = [
         [a],
@@ -215,7 +221,7 @@
         [p_0_other, p_1_other],
         [p_0_far, p_1_far],
     ]
-    return a_blocks, [b, y_near, y_other, y_far, r, r_near, r_other, r_far]
+    return a_blocks, [[b], [y_near], [y_other], [y_far], [r], [r_near], [r_other], r_far], first
 
 
 def shards(tokens, joined_weight, positions):
@@ -228,21 +234,23 @@
     mine = lax.dynamic_slice_in_dim(joined_weight, core * depth, depth, 0)
     sent = lax.dynamic_slice_in_dim(joined_weight, (1 - core) * depth, depth, 0)
     weight = jnp.concatenate([mine, swap(sent, "c")], axis=1)
-    a_blocks, b_blocks = gathers(tokens, weight)
-
     column_block = (place[2] * 4 + place[3]) * 2 + place[4]
     rotated = column_block * columns < (QUERY_HEADS + KEY_VALUE_HEADS) * HEAD_WIDTH
     cosine, sine = rotary_tables(positions, HEAD_WIDTH)
     cosine, sine = jnp.where(rotated, cosine, 1.0), jnp.where(rotated, sine, 0.0)
+    table, cosine, sine = lax.optimization_barrier((table, cosine, sine))
+
+    def first_product(first_a, first_b):
+        return product(table, 0, FIRST, first_a, first_b, (0, 1))
+
+    a_blocks, b_blocks, first = gathers(tokens, weight, first_product, table, cosine, sine)
 
     early_a, early_b = a_blocks[:7] + [None], b_blocks[:7] + [None]
-    table, cosine, sine = lax.optimization_barrier((table, cosine, sine))
-    early, early_sent = product(table, 0, EARLY, early_a, early_b, (0, 1))
-    early_received = swap(early_sent, "c")
-    (late_sent,) = product(table, EARLY, 8 - EARLY, a_blocks, b_blocks, (1,))
-    late_received = swap(late_sent, "c")
+    early, early_sent = product(table, FIRST, EARLY - FIRST, early_a, early_b, (0, 1), first)
+    (sent,) = product(table, EARLY, 8 - EARLY, a_blocks, b_blocks, (1,), (early_sent,))
+    from_sibling = swap(sent, "c")
     (total,) = product(table, EARLY, 8 - EARLY, a_blocks, b_blocks, (0,), (early,))
-    turned = turn([total, early_received, late_received], cosine, sine)
+    turned = turn([total, from_sibling], cosine, sine)
     received = lax.all_to_all(turned, ("xl", "z", "c"), split_axis=0, concat_axis=1, tiled=True)
     query_columns = QUERY_HEADS * HEAD_WIDTH
     rotated_columns = (QUERY_HEADS + KEY_VALUE_HEADS) * HEAD_WIDTH

time: 162 us -> 154 us (0.951)
  waiting for transfers between devices: 76.2 us -> 57.2 us
  starting transfers between devices: 36 us -> 40.2 us
  local copies, waits for them, and re-layouts: 5.26 us -> 8.71 us
  Pallas kernels: 22.8 us -> 25 us
    ppermute x15, waiting for transfers between devices: 31.7 us -> 14.3 us  [ring_step(): return lax.ppermute(block, (axis, 'c'), pairs)]
    slice x0 -> x3, local copies, waits for them, and re-layouts: none -> 3.32 us  [the longest x1 2.06 us: gathers(): r_far_1 = swap(after(y_far[split:], p_1), 'xh')]
    ppermute x6, starting transfers between devices: 9.87 us -> 12.5 us  [swap(): return lax.ppermute(block, axis, SWAP)]
    pallas_call x3 -> x4, Pallas kernels: 21.8 us -> 24.1 us  [product(): pl.pallas_call(kernel, out_shape=[jax.ShapeDtypeStruct((rows, width), jnp...]
  transfers between devices with their start and end apart: 21 -> 21, of which waited for: 9 -> 11; matrix products, arithmetic and copies ran while one was open for 2% -> 5% of each run, Pallas kernels for 13% -> 13%
where the time goes in v5:
time: 154 us; the launch traced here: 153 us
  waiting for transfers between devices  57.2 us (37%)
  starting transfers between devices  40.2 us (26%)
  Pallas kernels  25 us (16%)
  blocking collectives  18 us (12%)
  local copies, waits for them, and re-layouts  8.71 us (6%)
  other arithmetic  3.38 us (2%)
    ppermute x6, waiting for transfers between devices, swap(): return lax.ppermute(block, axis, SWAP)  42.9 us
    ppermute x15, starting transfers between devices, ring_step(): return lax.ppermute(block, (axis, 'c'), pairs)  27.7 us
    pallas_call x4, Pallas kernels, product(): pl.pallas_call(kernel, out_shape=[jax.ShapeDtypeStruct((rows, width), jnp...  24.1 us
    all_to_all x1, blocking collectives, shards(): lax.all_to_all(turned, ('xl', 'z', 'c'), split_axis=0, concat_axis=1, til...  18 us
    ppermute x15, waiting for transfers between devices, ring_step(): return lax.ppermute(block, (axis, 'c'), pairs)  14.3 us
    ppermute x6, starting transfers between devices, swap(): return lax.ppermute(block, axis, SWAP)  12.5 us
  transfers between devices with their start and end apart: 21, of which 11 were waited for; matrix products, arithmetic and copies ran while one was open for 5% of the time, Pallas kernels for 13%

profile of v5, /device:TPU:1, one launch (start us, length us, event | category | flops | bytes accessed | tf_op | source)
XLA Modules:
  0.0 153.2 jit_solution(14908305605116431227)
XLA Ops:
  0.6 0.0 copy-start
  0.6 1.6 %constant_dynamic-slice_fusion.1 = (bf16[768,512]{1,0:T(8,128)(2,1)S(1)}, bf16[768,512]{1,0:T(8,128)(2,1)S(1)}) fusion(bf16[1536,512]{1,0:T(8,128)(2,1)} %param.5, s32[]{:T(128)S(6)} %select_n.62, s32[]{:T(128)S(6)} %select_n.63), kind=kLoop, calls=%fused_computation.10 | loop fusion | bytes 3145736 | tf_op jit(solution)/shard_map/dynamic_slice | solution.py:234
  2.2 1.5 collective-permute-start.5
  3.8 3.8 %collective-permute-start = (bf16[1024,768]{1,0:T(8,128)(2,1)S(1)}, bf16[1024,768]{1,0:T(8,128)(2,1)S(1)}, u32[]{:S(2)}, u32[]{:S(2)}) collective-permute-start(bf16[1024,768]{1,0:T(8,128)(2,1)S(1)} %copy-done), channel_id=1, source_target_pairs={{0,2},{1,7},{2,4},{3,1},{4,6},{5,3},{6,0},{7,5},{8,10},{9,15},{10,... | collective-permute-start | bytes 4718600 | tf_op jit(solution)/shard_map/ppermute | solution.py:36
  7.6 0.1 slice.21
  7.7 1.3 collective-permute-start.2
  9.0 1.4 pad_maximum_fusion.refs_6_.refs_10_.refs_12_
  10.4 1.3 collective-permute-start.12
  11.7 1.4 collective-permute-start.11
  13.1 21.5 %collective-permute-done.2.refs_4_ = bf16[768,768]{1,0:T(8,128)(2,1)} collective-permute-done((bf16[768,768]{1,0:T(8,128)(2,1)S(1)}, bf16[768,768]{1,0:T(8,128)(2,1)}, u32[]{:S(2)}, u32[]{:S(2)}) %collective-permute-start.2) | collective-permute-done | bytes 1179680 | tf_op jit(solution)/shard_map/ppermute | solution.py:183
  34.7 2.7 %collective-permute-start.6 = (bf16[768,1024]{1,0:T(8,128)(2,1)}, bf16[768,1024]{1,0:T(8,128)(2,1)}, u32[]{:S(2)}, u32[]{:S(2)}) collective-permute-start(bf16[768,1024]{1,0:T(8,128)(2,1)} %pad_maximum_fusion.refs_6_.refs_10_.refs_12_), channel_id=1, source_target_pairs={{0,64},{64,0},{1,65},{65,1},{2,66},{66,2},{3,67},{67,3},{4,68},{68... | collective-permute-start | bytes 4718600 | tf_op jit(solution)/shard_map/ppermute | solution.py:183
  37.4 0.8 collective-permute-start.3
  38.3 8.0 %collective-permute-done.12.refs_8_.refs_12_.refs_14_ = bf16[768,1024]{1,0:T(8,128)(2,1)S(1)} collective-permute-done((bf16[768,1024]{1,0:T(8,128)(2,1)}, bf16[768,1024]{1,0:T(8,128)(2,1)S(1)}, u32[]{:S(2)}, u32[]{:S(2)}) %collective-permute-start.12) | collective-permute-done | bytes 1572896 | tf_op jit(solution)/shard_map/ppermute | solution.py:36
  46.3 0.5 collective-permute-done.11.refs_7_.refs_11_.refs_13_
  46.8 3.4 %collective-permute-start.13 = (bf16[768,1024]{1,0:T(8,128)(2,1)}, bf16[768,1024]{1,0:T(8,128)(2,1)}, u32[]{:S(2)}, u32[]{:S(2)}) collective-permute-start(bf16[768,1024]{1,0:T(8,128)(2,1)} %collective-permute-done.11.refs_7_.refs_11_.refs_13_), channel_id=1, source_target_pairs={{0,16},{1,49},{16,32},{17,1},{32,48},{33,17},{48,0},{49,33},{2,18}... | collective-permute-start | bytes 4718600 | tf_op jit(solution)/shard_map/ppermute | solution.py:36
  50.2 1.1 copy-done.3
  51.4 0.7 dynamic-slice_bitcast_fusion
  52.1 1.9 %fusion.2 = (f32[1024,128]{1,0:T(8,128)S(1)}, f32[1024,128]{1,0:T(8,128)S(1)}) fusion(f32[128]{0:T(128)S(1)} %get-tuple-element.49, f32[128]{0:T(128)S(1)} %get-tuple-element.50, f32[1024]{0:T(1024)S(1)} %convert_element_type.10, pred[]{:T(512)S(6)} %lt.43), kind=kLoop, calls=%fused_computation.5 | loop fusion | flops 524288 | bytes 1053697 | tf_op jit(solution)/shard_map/jit(_where)/select_n | solution.py:240
  54.0 2.6 %collective-permute-done.3.refs_6_ = bf16[768,768]{1,0:T(8,128)(2,1)} collective-permute-done((bf16[768,768]{1,0:T(8,128)(2,1)}, bf16[768,768]{1,0:T(8,128)(2,1)}, u32[]{:S(2)}, u32[]{:S(2)}) %collective-permute-start.3) | collective-permute-done | bytes 1179680 | tf_op jit(solution)/shard_map/ppermute | solution.py:36
  56.6 3.4 %collective-permute-start.4 = (bf16[1024,768]{1,0:T(8,128)(2,1)}, bf16[1024,768]{1,0:T(8,128)(2,1)}, u32[]{:S(2)}, u32[]{:S(2)}) collective-permute-start(bf16[1024,768]{1,0:T(8,128)(2,1)} %copy-done.1), channel_id=1, source_target_pairs={{0,2},{1,7},{2,4},{3,1},{4,6},{5,3},{6,0},{7,5},{8,10},{9,15},{10,... | collective-permute-start | bytes 4718600 | tf_op jit(solution)/shard_map/ppermute | solution.py:36
  60.0 12.2 %collective-permute-done.6.refs_10_.refs_14_.refs_16_ = bf16[768,1024]{1,0:T(8,128)(2,1)} collective-permute-done((bf16[768,1024]{1,0:T(8,128)(2,1)}, bf16[768,1024]{1,0:T(8,128)(2,1)}, u32[]{:S(2)}, u32[]{:S(2)}) %collective-permute-start.6) | collective-permute-done | bytes 1572896 | tf_op jit(solution)/shard_map/ppermute | solution.py:183
  72.3 1.5 collective-permute-start.7
  73.7 2.7 %collective-permute-start.16 = (bf16[768,1024]{1,0:T(8,128)(2,1)}, bf16[768,1024]{1,0:T(8,128)(2,1)}, u32[]{:S(2)}, u32[]{:S(2)}) collective-permute-start(bf16[768,1024]{1,0:T(8,128)(2,1)} %collective-permute-done.6.refs_10_.refs_14_.refs_16_), channel_id=1, source_target_pairs={{0,16},{1,49},{16,32},{17,1},{32,48},{33,17},{48,0},{49,33},{2,18}... | collective-permute-start | bytes 4718600 | tf_op jit(solution)/shard_map/ppermute | solution.py:36
  76.5 6.2 %collective-permute-done.7.refs_5_ = bf16[256,768]{1,0:T(8,128)(2,1)S(1)} collective-permute-done((bf16[256,768]{1,0:T(8,128)(2,1)S(1)}, bf16[256,768]{1,0:T(8,128)(2,1)S(1)}, u32[]{:S(2)}, u32[]{:S(2)}) %collective-permute-start.7) | collective-permute-done | bytes 393248 | tf_op jit(solution)/shard_map/ppermute | solution.py:183
  82.7 1.3 collective-permute-start.17
  84.0 2.1 %slice.29 = bf16[384,1024]{1,0:T(8,128)(2,1)} slice(bf16[768,1024]{1,0:T(8,128)(2,1)} %collective-permute-done.13.refs_9_.refs_13_.refs_15_), slice={[384:768], [0:1024]} | slice | bytes 1572864 | tf_op jit(solution)/shard_map/slice | solution.py:206
  86.1 3.3 %collective-permute-start.18 = (bf16[384,1024]{1,0:T(8,128)(2,1)}, bf16[384,1024]{1,0:T(8,128)(2,1)S(1)}, u32[]{:S(2)}, u32[]{:S(2)}) collective-permute-start(bf16[384,1024]{1,0:T(8,128)(2,1)} %slice.29), channel_id=1, source_target_pairs={{0,64},{64,0},{1,65},{65,1},{2,66},{66,2},{3,67},{67,3},{4,68},{68... | collective-permute-start | bytes 2359304 | tf_op jit(solution)/shard_map/ppermute | solution.py:183
  89.3 0.1 copy.9
  89.4 0.1 reshape.33.table_ref
  89.5 6.1 %shard_map.67 = (f32[1024,512]{1,0:T(8,128)S(1)}, f32[1024,512]{1,0:T(8,128)S(1)}) custom-call(s32[16]{0:T(128)S(1)} %reshape.33.table_ref, bf16[1024,768]{1,0:T(8,128)(2,1)} %refs_0_.7, bf16[1024,768]{1,0:T(8,128)(2,1)} %copy-done.1, bf16[1024,768]{1,0:T(8,128)(2,1)} %copy-done.3, bf16[1024,768]{1,0:T(8,128)(2,1)} %collective-permute-done.4.refs_3_, ...), custom_call_target="tpu_custom_call" | custom-call | flops 3221225472 | bytes 6291456 | tf_op jit(solution)/shard_map/pallas_call | solution.py:133
  95.6 1.1 collective-permute-done.9.refs_10_
  96.7 3.4 %collective-permute-start.10 = (bf16[256,768]{1,0:T(8,128)(2,1)S(1)}, bf16[256,768]{1,0:T(8,128)(2,1)S(1)}, u32[]{:S(2)}, u32[]{:S(2)}) collective-permute-start(bf16[256,768]{1,0:T(8,128)(2,1)S(1)} %copy-done.5), channel_id=1, source_target_pairs={{0,2},{1,7},{2,4},{3,1},{4,6},{5,3},{6,0},{7,5},{8,10},{9,15},{10,... | collective-permute-start | bytes 1179656 | tf_op jit(solution)/shard_map/ppermute | solution.py:36
  100.1 0.3 collective-permute-done.16.refs_15_.refs_17_
  100.4 1.2 slice.28
  101.6 3.0 %collective-permute-done.18.refs_20_ = bf16[384,1024]{1,0:T(8,128)(2,1)S(1)} collective-permute-done((bf16[384,1024]{1,0:T(8,128)(2,1)}, bf16[384,1024]{1,0:T(8,128)(2,1)S(1)}, u32[]{:S(2)}, u32[]{:S(2)}) %collective-permute-start.18) | collective-permute-done | bytes 786464 | tf_op jit(solution)/shard_map/ppermute | solution.py:183
  104.6 2.7 %collective-permute-start.19 = (bf16[384,1024]{1,0:T(8,128)(2,1)S(1)}, bf16[384,1024]{1,0:T(8,128)(2,1)S(1)}, u32[]{:S(2)}, u32[]{:S(2)}) collective-permute-start(bf16[384,1024]{1,0:T(8,128)(2,1)S(1)} %slice.28), channel_id=1, source_target_pairs={{0,16},{1,49},{16,32},{17,1},{32,48},{33,17},{48,0},{49,33},{2,18}... | collective-permute-start | bytes 2359304 | tf_op jit(solution)/shard_map/ppermute | solution.py:36
  107.3 3.3 %collective-permute-start.15 = (bf16[256,768]{1,0:T(8,128)(2,1)S(1)}, bf16[256,768]{1,0:T(8,128)(2,1)S(1)}, u32[]{:S(2)}, u32[]{:S(2)}) collective-permute-start(bf16[256,768]{1,0:T(8,128)(2,1)S(1)} %collective-permute-done.10.refs_7_), channel_id=1, source_target_pairs={{0,2},{1,7},{2,4},{3,1},{4,6},{5,3},{6,0},{7,5},{8,10},{9,15},{10,... | collective-permute-start | bytes 1179656 | tf_op jit(solution)/shard_map/ppermute | solution.py:36
  110.6 0.4 collective-permute-done.14.refs_9_
  111.0 1.3 collective-permute-done.17.refs_16_.refs_18_
  112.3 9.8 %shard_map.68 = (f32[1024,512]{1,0:T(8,128)S(1)}, f32[1024,512]{1,0:T(8,128)S(1)}) custom-call(s32[16]{0:T(128)S(1)} %reshape.33.table_ref, bf16[1024,768]{1,0:T(8,128)(2,1)} %refs_0_.7, bf16[1024,768]{1,0:T(8,128)(2,1)} %copy-done.1, bf16[1024,768]{1,0:T(8,128)(2,1)} %copy-done.3, bf16[1024,768]{1,0:T(8,128)(2,1)} %collective-permute-done.4.refs_3_, ...), custom_call_target="tpu_custom_call" | custom-call | flops 6442450944 | bytes 12582912 | tf_op jit(solution)/shard_map/pallas_call | solution.py:133
  122.1 4.2 %shard_map.70 = f32[1024,512]{1,0:T(8,128)S(1)} custom-call(s32[16]{0:T(128)S(1)} %reshape.33.table_ref, bf16[1024,768]{1,0:T(8,128)(2,1)} %refs_0_.7, bf16[1024,768]{1,0:T(8,128)(2,1)} %copy-done.1, bf16[1024,768]{1,0:T(8,128)(2,1)} %copy-done.3, bf16[1024,768]{1,0:T(8,128)(2,1)} %collective-permute-done.4.refs_3_, ...), custom_call_target="tpu_custom_call" | custom-call | flops 1610612736 | bytes 4718592 | tf_op jit(solution)/shard_map/pallas_call | solution.py:133
  126.2 2.3 %collective-permute-start.20 = (f32[1024,512]{1,0:T(8,128)S(1)}, f32[1024,512]{1,0:T(8,128)S(1)}, u32[]{:S(2)}, u32[]{:S(2)}) collective-permute-start(f32[1024,512]{1,0:T(8,128)S(1)} %shard_map.70), channel_id=1, source_target_pairs={{0,1},{1,0},{2,3},{3,2},{4,5},{5,4},{6,7},{7,6},{8,9},{9,8},{10,11... | collective-permute-start | bytes 6291464 | tf_op jit(solution)/shard_map/ppermute | solution.py:183
  128.5 4.1 %shard_map.69.refs_0_ = f32[1024,512]{1,0:T(8,128)S(1)} custom-call(s32[16]{0:T(128)S(1)} %reshape.33.table_ref, bf16[1024,768]{1,0:T(8,128)(2,1)} %refs_0_.7, bf16[1024,768]{1,0:T(8,128)(2,1)} %copy-done.1, bf16[1024,768]{1,0:T(8,128)(2,1)} %copy-done.3, bf16[1024,768]{1,0:T(8,128)(2,1)} %collective-permute-done.4.refs_3_, ...), custom_call_target="tpu_custom_call" | custom-call | flops 1610612736 | bytes 4718592 | tf_op jit(solution)/shard_map/pallas_call | solution.py:133
  132.6 0.9 shard_map.71
  133.5 18.0 %all_to_all.19 = bf16[16,64,512]{2,1,0:T(8,128)(2,1)S(1)} all-to-all(bf16[16,64,512]{2,1,0:T(8,128)(2,1)S(1)} %bitcast.6), channel_id=1, replica_groups=mesh['xh'=2,'y'=4,'xl'=2,'z'=4,'c'=2] {'xl','z','c'}, dimensions={0} | all-to-all | bytes 2097152 | tf_op jit(solution)/shard_map/all_to_all | solution.py:254
  151.5 0.1 copy.11
  151.6 0.9 slice.30
  152.5 0.7 fusion.6
  (33 shorter events, 0.1 us)
Async XLA Ops:
  0.6 3.1 %copy-start = (bf16[1024,768]{1,0:T(8,128)(2,1)S(1)}, bf16[1024,768]{1,0:T(8,128)(2,1)}, u32[]{:S(2)}) copy-start(bf16[1024,768]{1,0:T(8,128)(2,1)} %refs_0_.7) | copy-start | bytes 4718596
  2.2 6.7 %collective-permute-start.5 = (bf16[768,512]{1,0:T(8,128)(2,1)S(1)}, bf16[768,512]{1,0:T(8,128)(2,1)S(1)}, u32[]{:S(2)}, u32[]{:S(2)}) collective-permute-start(bf16[768,512]{1,0:T(8,128)(2,1)S(1)} %get-tuple-element.44), channel_id=1, source_target_pairs={{0,1},{1,0},{2,3},{3,2},{4,5},{5,4},{6,7},{7,6},{8,9},{9,8},{10,11... | collective-permute-start | bytes 2359304 | tf_op jit(solution)/shard_map/ppermute | solution.py:183
  3.8 33.7 %collective-permute-start = (bf16[1024,768]{1,0:T(8,128)(2,1)S(1)}, bf16[1024,768]{1,0:T(8,128)(2,1)S(1)}, u32[]{:S(2)}, u32[]{:S(2)}) collective-permute-start(bf16[1024,768]{1,0:T(8,128)(2,1)S(1)} %copy-done), channel_id=1, source_target_pairs={{0,2},{1,7},{2,4},{3,1},{4,6},{5,3},{6,0},{7,5},{8,10},{9,15},{10,... | collective-permute-start | bytes 4718600 | tf_op jit(solution)/shard_map/ppermute | solution.py:36
  7.7 27.0 %collective-permute-start.2 = (bf16[768,768]{1,0:T(8,128)(2,1)S(1)}, bf16[768,768]{1,0:T(8,128)(2,1)}, u32[]{:S(2)}, u32[]{:S(2)}) collective-permute-start(bf16[768,768]{1,0:T(8,128)(2,1)S(1)} %slice.21), channel_id=1, source_target_pairs={{0,8},{8,0},{1,9},{9,1},{2,10},{10,2},{3,11},{11,3},{4,12},{12,4},... | collective-permute-start | bytes 3538952 | tf_op jit(solution)/shard_map/ppermute | solution.py:183
  9.0 42.4 %copy-start.8 = (s32[1024]{0:T(1024)S(1)}, s32[1024]{0:T(1024)}, u32[]{:S(2)}) copy-start(s32[1024]{0:T(1024)} %param.6) | copy-start | bytes 12292
  10.4 35.9 %collective-permute-start.12 = (bf16[768,1024]{1,0:T(8,128)(2,1)}, bf16[768,1024]{1,0:T(8,128)(2,1)S(1)}, u32[]{:S(2)}, u32[]{:S(2)}) collective-permute-start(bf16[768,1024]{1,0:T(8,128)(2,1)} %pad_maximum_fusion.refs_6_.refs_10_.refs_12_), channel_id=1, source_target_pairs={{0,48},{1,17},{16,0},{17,33},{32,16},{33,49},{48,32},{49,1},{2,50}... | collective-permute-start | bytes 4718600 | tf_op jit(solution)/shard_map/ppermute | solution.py:36
  11.7 35.1 %collective-permute-start.11 = (bf16[768,1024]{1,0:T(8,128)(2,1)}, bf16[768,1024]{1,0:T(8,128)(2,1)}, u32[]{:S(2)}, u32[]{:S(2)}) collective-permute-start(bf16[768,1024]{1,0:T(8,128)(2,1)} %pad_maximum_fusion.refs_6_.refs_10_.refs_12_), channel_id=1, source_target_pairs={{0,16},{1,49},{16,32},{17,1},{32,48},{33,17},{48,0},{49,33},{2,18}... | collective-permute-start | bytes 4718600 | tf_op jit(solution)/shard_map/ppermute | solution.py:36
  13.1 37.0 %collective-permute-start.1 = (bf16[1024,768]{1,0:T(8,128)(2,1)S(1)}, bf16[1024,768]{1,0:T(8,128)(2,1)S(1)}, u32[]{:S(2)}, u32[]{:S(2)}) collective-permute-start(bf16[1024,768]{1,0:T(8,128)(2,1)S(1)} %copy-done), channel_id=1, source_target_pairs={{0,6},{1,3},{2,0},{3,5},{4,2},{5,7},{6,4},{7,1},{8,14},{9,11},{10,... | collective-permute-start | bytes 4718600 | tf_op jit(solution)/shard_map/ppermute | solution.py:36
  34.7 37.6 %collective-permute-start.6 = (bf16[768,1024]{1,0:T(8,128)(2,1)}, bf16[768,1024]{1,0:T(8,128)(2,1)}, u32[]{:S(2)}, u32[]{:S(2)}) collective-permute-start(bf16[768,1024]{1,0:T(8,128)(2,1)} %pad_maximum_fusion.refs_6_.refs_10_.refs_12_), channel_id=1, source_target_pairs={{0,64},{64,0},{1,65},{65,1},{2,66},{66,2},{3,67},{67,3},{4,68},{68... | collective-permute-start | bytes 4718600 | tf_op jit(solution)/shard_map/ppermute | solution.py:183
  37.4 12.8 %copy-start.1 = (bf16[1024,768]{1,0:T(8,128)(2,1)}, bf16[1024,768]{1,0:T(8,128)(2,1)S(1)}, u32[]{:S(2)}) copy-start(bf16[1024,768]{1,0:T(8,128)(2,1)S(1)} %collective-permute-done.refs_1_) | copy-start | bytes 4718596
  37.4 19.2 %collective-permute-start.3 = (bf16[768,768]{1,0:T(8,128)(2,1)}, bf16[768,768]{1,0:T(8,128)(2,1)}, u32[]{:S(2)}, u32[]{:S(2)}) collective-permute-start(bf16[768,768]{1,0:T(8,128)(2,1)} %collective-permute-done.2.refs_4_), channel_id=1, source_target_pairs={{0,2},{1,7},{2,4},{3,1},{4,6},{5,3},{6,0},{7,5},{8,10},{9,15},{10,... | collective-permute-start | bytes 3538952 | tf_op jit(solution)/shard_map/ppermute | solution.py:36
  46.3 3.9 %copy-start.2 = (bf16[768,1024]{1,0:T(8,128)(2,1)}, bf16[768,1024]{1,0:T(8,128)(2,1)S(1)}, u32[]{:S(2)}) copy-start(bf16[768,1024]{1,0:T(8,128)(2,1)S(1)} %collective-permute-done.12.refs_8_.refs_12_.refs_14_) | copy-start | bytes 4718596
  46.8 36.0 %collective-permute-start.13 = (bf16[768,1024]{1,0:T(8,128)(2,1)}, bf16[768,1024]{1,0:T(8,128)(2,1)}, u32[]{:S(2)}, u32[]{:S(2)}) collective-permute-start(bf16[768,1024]{1,0:T(8,128)(2,1)} %collective-permute-done.11.refs_7_.refs_11_.refs_13_), channel_id=1, source_target_pairs={{0,16},{1,49},{16,32},{17,1},{32,48},{33,17},{48,0},{49,33},{2,18}... | collective-permute-start | bytes 4718600 | tf_op jit(solution)/shard_map/ppermute | solution.py:36
  50.2 1.1 copy-start.3
  51.3 25.1 %collective-permute-start.8 = (bf16[768,768]{1,0:T(8,128)(2,1)}, bf16[768,768]{1,0:T(8,128)(2,1)}, u32[]{:S(2)}, u32[]{:S(2)}) collective-permute-start(bf16[768,768]{1,0:T(8,128)(2,1)} %collective-permute-done.2.refs_4_), channel_id=1, source_target_pairs={{0,6},{1,3},{2,0},{3,5},{4,2},{5,7},{6,4},{7,1},{8,14},{9,11},{10,... | collective-permute-start | bytes 3538952 | tf_op jit(solution)/shard_map/ppermute | solution.py:36
  56.6 32.9 %collective-permute-start.4 = (bf16[1024,768]{1,0:T(8,128)(2,1)}, bf16[1024,768]{1,0:T(8,128)(2,1)}, u32[]{:S(2)}, u32[]{:S(2)}) collective-permute-start(bf16[1024,768]{1,0:T(8,128)(2,1)} %copy-done.1), channel_id=1, source_target_pairs={{0,2},{1,7},{2,4},{3,1},{4,6},{5,3},{6,0},{7,5},{8,10},{9,15},{10,... | collective-permute-start | bytes 4718600 | tf_op jit(solution)/shard_map/ppermute | solution.py:36
  72.3 10.4 %collective-permute-start.7 = (bf16[256,768]{1,0:T(8,128)(2,1)S(1)}, bf16[256,768]{1,0:T(8,128)(2,1)S(1)}, u32[]{:S(2)}, u32[]{:S(2)}) collective-permute-start(bf16[256,768]{1,0:T(8,128)(2,1)S(1)} %slice.22), channel_id=1, source_target_pairs={{0,8},{8,0},{1,9},{9,1},{2,10},{10,2},{3,11},{11,3},{4,12},{12,4},... | collective-permute-start | bytes 1179656 | tf_op jit(solution)/shard_map/ppermute | solution.py:183
  73.7 26.7 %collective-permute-start.16 = (bf16[768,1024]{1,0:T(8,128)(2,1)}, bf16[768,1024]{1,0:T(8,128)(2,1)}, u32[]{:S(2)}, u32[]{:S(2)}) collective-permute-start(bf16[768,1024]{1,0:T(8,128)(2,1)} %collective-permute-done.6.refs_10_.refs_14_.refs_16_), channel_id=1, source_target_pairs={{0,16},{1,49},{16,32},{17,1},{32,48},{33,17},{48,0},{49,33},{2,18}... | collective-permute-start | bytes 4718600 | tf_op jit(solution)/shard_map/ppermute | solution.py:36
  76.5 20.2 %collective-permute-start.9 = (bf16[768,768]{1,0:T(8,128)(2,1)}, bf16[768,768]{1,0:T(8,128)(2,1)S(1)}, u32[]{:S(2)}, u32[]{:S(2)}) collective-permute-start(bf16[768,768]{1,0:T(8,128)(2,1)} %collective-permute-done.3.refs_6_), channel_id=1, source_target_pairs={{0,2},{1,7},{2,4},{3,1},{4,6},{5,3},{6,0},{7,5},{8,10},{9,15},{10,... | collective-permute-start | bytes 3538952 | tf_op jit(solution)/shard_map/ppermute | solution.py:36
  82.7 6.6 %copy-start.4 = (bf16[256,768]{1,0:T(8,128)(2,1)}, bf16[256,768]{1,0:T(8,128)(2,1)S(1)}, u32[]{:S(2)}) copy-start(bf16[256,768]{1,0:T(8,128)(2,1)S(1)} %collective-permute-done.7.refs_5_) | copy-start | bytes 1179652
  82.7 29.6 %collective-permute-start.17 = (bf16[768,1024]{1,0:T(8,128)(2,1)}, bf16[768,1024]{1,0:T(8,128)(2,1)}, u32[]{:S(2)}, u32[]{:S(2)}) collective-permute-start(bf16[768,1024]{1,0:T(8,128)(2,1)} %collective-permute-done.6.refs_10_.refs_14_.refs_16_), channel_id=1, source_target_pairs={{0,48},{1,17},{16,0},{17,33},{32,16},{33,49},{48,32},{49,1},{2,50}... | collective-permute-start | bytes 4718600 | tf_op jit(solution)/shard_map/ppermute | solution.py:36
  86.1 18.5 %collective-permute-start.18 = (bf16[384,1024]{1,0:T(8,128)(2,1)}, bf16[384,1024]{1,0:T(8,128)(2,1)S(1)}, u32[]{:S(2)}, u32[]{:S(2)}) collective-permute-start(bf16[384,1024]{1,0:T(8,128)(2,1)} %slice.29), channel_id=1, source_target_pairs={{0,64},{64,0},{1,65},{65,1},{2,66},{66,2},{3,67},{67,3},{4,68},{68... | collective-permute-start | bytes 2359304 | tf_op jit(solution)/shard_map/ppermute | solution.py:183
  89.5 7.2 %copy-start.5 = (bf16[256,768]{1,0:T(8,128)(2,1)S(1)}, bf16[256,768]{1,0:T(8,128)(2,1)}, u32[]{:S(2)}) copy-start(bf16[256,768]{1,0:T(8,128)(2,1)} %copy-done.4) | copy-start | bytes 1179652
  96.7 10.6 %collective-permute-start.10 = (bf16[256,768]{1,0:T(8,128)(2,1)S(1)}, bf16[256,768]{1,0:T(8,128)(2,1)S(1)}, u32[]{:S(2)}, u32[]{:S(2)}) collective-permute-start(bf16[256,768]{1,0:T(8,128)(2,1)S(1)} %copy-done.5), channel_id=1, source_target_pairs={{0,2},{1,7},{2,4},{3,1},{4,6},{5,3},{6,0},{7,5},{8,10},{9,15},{10,... | collective-permute-start | bytes 1179656 | tf_op jit(solution)/shard_map/ppermute | solution.py:36
  100.1 10.9 %collective-permute-start.14 = (bf16[256,768]{1,0:T(8,128)(2,1)S(1)}, bf16[256,768]{1,0:T(8,128)(2,1)S(1)}, u32[]{:S(2)}, u32[]{:S(2)}) collective-permute-start(bf16[256,768]{1,0:T(8,128)(2,1)S(1)} %copy-done.5), channel_id=1, source_target_pairs={{0,6},{1,3},{2,0},{3,5},{4,2},{5,7},{6,4},{7,1},{8,14},{9,11},{10,... | collective-permute-start | bytes 1179656 | tf_op jit(solution)/shard_map/ppermute | solution.py:36
  104.6 17.5 %collective-permute-start.19 = (bf16[384,1024]{1,0:T(8,128)(2,1)S(1)}, bf16[384,1024]{1,0:T(8,128)(2,1)S(1)}, u32[]{:S(2)}, u32[]{:S(2)}) collective-permute-start(bf16[384,1024]{1,0:T(8,128)(2,1)S(1)} %slice.28), channel_id=1, source_target_pairs={{0,16},{1,49},{16,32},{17,1},{32,48},{33,17},{48,0},{49,33},{2,18}... | collective-permute-start | bytes 2359304 | tf_op jit(solution)/shard_map/ppermute | solution.py:36
  107.3 5.0 %copy-start.6 = (bf16[256,768]{1,0:T(8,128)(2,1)}, bf16[256,768]{1,0:T(8,128)(2,1)S(1)}, u32[]{:S(2)}) copy-start(bf16[256,768]{1,0:T(8,128)(2,1)S(1)} %collective-permute-done.10.refs_7_) | copy-start | bytes 1179652
  107.3 14.8 %collective-permute-start.15 = (bf16[256,768]{1,0:T(8,128)(2,1)S(1)}, bf16[256,768]{1,0:T(8,128)(2,1)S(1)}, u32[]{:S(2)}, u32[]{:S(2)}) collective-permute-start(bf16[256,768]{1,0:T(8,128)(2,1)S(1)} %collective-permute-done.10.refs_7_), channel_id=1, source_target_pairs={{0,2},{1,7},{2,4},{3,1},{4,6},{5,3},{6,0},{7,5},{8,10},{9,15},{10,... | collective-permute-start | bytes 1179656 | tf_op jit(solution)/shard_map/ppermute | solution.py:36
  111.0 1.3 copy-start.7
  126.2 6.4 %collective-permute-start.20 = (f32[1024,512]{1,0:T(8,128)S(1)}, f32[1024,512]{1,0:T(8,128)S(1)}, u32[]{:S(2)}, u32[]{:S(2)}) collective-permute-start(f32[1024,512]{1,0:T(8,128)S(1)} %shard_map.70), channel_id=1, source_target_pairs={{0,1},{1,0},{2,3},{3,2},{4,5},{5,4},{6,7},{7,6},{8,9},{9,8},{10,11... | collective-permute-start | bytes 6291464 | tf_op jit(solution)/shard_map/ppermute | solution.py:183

commit v6 on v5

--- a/solution.py
+++ b/solution.py
@@ -127,7 +127,7 @@
     late = [p == 7 for p in used_a for _ in a_blocks[p]] + [q == 7 for q in used_b for _ in b_blocks[q]]
     operands = [table.reshape(-1)]
     operands += [
-        pltpu.with_memory_space_constraint(v, pltpu.VMEM if near else pltpu.HBM)
+        v if v is b_blocks[0][0] else pltpu.with_memory_space_constraint(v, pltpu.VMEM if near else pltpu.HBM)
         for v, near in zip(pieces, late)
     ]
     return pl.pallas_call(
@@ -184,7 +184,7 @@
 
 
 def gathers(a, b, first_product, *early):
-    part = a.shape[0] // 8 * 6
+    part = a.shape[0] // 16 * 9
 
     z_near = ring_step(a, "z")
     p_0 = swap(a[:part], "xl")
@@ -201,14 +201,14 @@
 
     p_1 = swap(after(a[part:], r), "xl")
     r_near = ring_step(after(r, y_other), "y")
-    r_other = ring_step(after(r, y_far, p_1), "y", -1)
+    r_other = ring_step(after(r, y_far, p_1, p_0_other), "y", -1)
     split = b.shape[0] // 2
     r_far_1 = swap(after(y_far[split:], p_1), "xh")
     p_1_near = ring_step(after(p_1, z_far, p_0_far), "z")
     first = first_product([[a], [z_near], [z_other], [z_far], [p_0, p_1]], [[b], [y_near], [y_other], [y_far], [r]])
     p_1_other = ring_step(after(p_1, z_far, p_0_far, *first), "z", -1)
     p_1_far = ring_step(p_1_near, "z")
-    r_far_0 = ring_step(after(r_near[:split], r_far_1), "y")
+    r_far_0 = ring_step(r_near[:split], "y")
     r_far = [r_far_0, r_far_1]
 
     a_blocks = [

time: 154 us -> 153 us (level); the launches traced: 153 us -> 150 us
  starting transfers between devices: 40.2 us -> 36.5 us
    ppermute x15, waiting for transfers between devices: 14.3 us -> 20 us  [ring_step(): return lax.ppermute(block, (axis, 'c'), pairs)]
    ppermute x6, waiting for transfers between devices: 42.9 us -> 38.2 us  [swap(): return lax.ppermute(block, axis, SWAP)]
    ppermute x6, starting transfers between devices: 12.5 us -> 10.4 us  [swap(): return lax.ppermute(block, axis, SWAP)]
    ppermute x15, starting transfers between devices: 27.7 us -> 26.1 us  [ring_step(): return lax.ppermute(block, (axis, 'c'), pairs)]
  transfers between devices with their start and end apart: 21 -> 21, of which waited for: 11 -> 9; matrix products, arithmetic and copies ran while one was open for 5% -> 4% of each run, Pallas kernels for 13% -> 13%
where the time goes in v6:
time: 153 us; the launch traced here: 150 us
  waiting for transfers between devices  58.2 us (38%)
  starting transfers between devices  36.5 us (24%)
  Pallas kernels  24.5 us (16%)
  blocking collectives  18.8 us (12%)
  local copies, waits for them, and re-layouts  9.42 us (6%)
  other arithmetic  2.16 us (1%)
    ppermute x6, waiting for transfers between devices, swap(): return lax.ppermute(block, axis, SWAP)  38.2 us
    ppermute x15, starting transfers between devices, ring_step(): return lax.ppermute(block, (axis, 'c'), pairs)  26.1 us
    pallas_call x4, Pallas kernels, product(): pl.pallas_call(kernel, out_shape=[jax.ShapeDtypeStruct((rows, width), jnp...  23.7 us
    ppermute x15, waiting for transfers between devices, ring_step(): return lax.ppermute(block, (axis, 'c'), pairs)  20 us
    all_to_all x1, blocking collectives, shards(): lax.all_to_all(turned, ('xl', 'z', 'c'), split_axis=0, concat_axis=1, til...  18.8 us
    ppermute x6, starting transfers between devices, swap(): return lax.ppermute(block, axis, SWAP)  10.4 us
  transfers between devices with their start and end apart: 21, of which 9 were waited for; matrix products, arithmetic and copies ran while one was open for 4% of the time, Pallas kernels for 13%

profile of v6, /device:TPU:1, one launch (start us, length us, event | category | flops | bytes accessed | tf_op | source)
XLA Modules:
  0.0 150.4 jit_solution(15864670913685465570)
XLA Ops:
  0.6 0.0 copy-start
  0.6 1.6 %constant_dynamic-slice_fusion.1 = (bf16[768,512]{1,0:T(8,128)(2,1)S(1)}, bf16[768,512]{1,0:T(8,128)(2,1)S(1)}) fusion(bf16[1536,512]{1,0:T(8,128)(2,1)} %param.5, s32[]{:T(128)S(6)} %select_n.62, s32[]{:T(128)S(6)} %select_n.63), kind=kLoop, calls=%fused_computation.10 | loop fusion | bytes 3145736 | tf_op jit(solution)/shard_map/dynamic_slice | solution.py:234
  2.2 1.5 collective-permute-start.5
  3.8 3.8 %collective-permute-start = (bf16[1024,768]{1,0:T(8,128)(2,1)S(1)}, bf16[1024,768]{1,0:T(8,128)(2,1)S(1)}, u32[]{:S(2)}, u32[]{:S(2)}) collective-permute-start(bf16[1024,768]{1,0:T(8,128)(2,1)S(1)} %copy-done), channel_id=1, source_target_pairs={{0,2},{1,7},{2,4},{3,1},{4,6},{5,3},{6,0},{7,5},{8,10},{9,15},{10,... | collective-permute-start | bytes 4718600 | tf_op jit(solution)/shard_map/ppermute | solution.py:36
  7.6 0.1 slice.21
  7.7 1.3 collective-permute-start.2
  8.9 0.2 pad_maximum_fusion.refs_6_.refs_10_.refs_12_
  9.2 1.4 collective-permute-start.12
  10.5 1.5 %collective-permute-start.11 = (bf16[768,1024]{1,0:T(8,128)(2,1)S(1)}, bf16[768,1024]{1,0:T(8,128)(2,1)}, u32[]{:S(2)}, u32[]{:S(2)}) collective-permute-start(bf16[768,1024]{1,0:T(8,128)(2,1)S(1)} %pad_maximum_fusion.refs_6_.refs_10_.refs_12_), channel_id=1, source_target_pairs={{0,16},{1,49},{16,32},{17,1},{32,48},{33,17},{48,0},{49,33},{2,18}... | collective-permute-start | bytes 4718600 | tf_op jit(solution)/shard_map/ppermute | solution.py:36
  12.1 16.2 %collective-permute-done.2.refs_4_ = bf16[576,768]{1,0:T(8,128)(2,1)} collective-permute-done((bf16[576,768]{1,0:T(8,128)(2,1)S(1)}, bf16[576,768]{1,0:T(8,128)(2,1)}, u32[]{:S(2)}, u32[]{:S(2)}) %collective-permute-start.2) | collective-permute-done | bytes 884768 | tf_op jit(solution)/shard_map/ppermute | solution.py:183
  28.3 2.7 %collective-permute-start.6 = (bf16[768,1024]{1,0:T(8,128)(2,1)S(1)}, bf16[768,1024]{1,0:T(8,128)(2,1)}, u32[]{:S(2)}, u32[]{:S(2)}) collective-permute-start(bf16[768,1024]{1,0:T(8,128)(2,1)S(1)} %pad_maximum_fusion.refs_6_.refs_10_.refs_12_), channel_id=1, source_target_pairs={{0,64},{64,0},{1,65},{65,1},{2,66},{66,2},{3,67},{67,3},{4,68},{68... | collective-permute-start | bytes 4718600 | tf_op jit(solution)/shard_map/ppermute | solution.py:183
  31.1 4.6 %collective-permute-done.refs_1_ = bf16[1024,768]{1,0:T(8,128)(2,1)S(1)} collective-permute-done((bf16[1024,768]{1,0:T(8,128)(2,1)S(1)}, bf16[1024,768]{1,0:T(8,128)(2,1)S(1)}, u32[]{:S(2)}, u32[]{:S(2)}) %collective-permute-start) | collective-permute-done | bytes 1572896 | tf_op jit(solution)/shard_map/ppermute | solution.py:36
  35.7 3.5 %collective-permute-start.3 = (bf16[576,768]{1,0:T(8,128)(2,1)}, bf16[576,768]{1,0:T(8,128)(2,1)}, u32[]{:S(2)}, u32[]{:S(2)}) collective-permute-start(bf16[576,768]{1,0:T(8,128)(2,1)} %collective-permute-done.2.refs_4_), channel_id=1, source_target_pairs={{0,2},{1,7},{2,4},{3,1},{4,6},{5,3},{6,0},{7,5},{8,10},{9,15},{10,... | collective-permute-start | bytes 2654216 | tf_op jit(solution)/shard_map/ppermute | solution.py:36
  39.2 5.7 %collective-permute-done.12.refs_8_.refs_12_.refs_14_ = bf16[768,1024]{1,0:T(8,128)(2,1)S(1)} collective-permute-done((bf16[768,1024]{1,0:T(8,128)(2,1)S(1)}, bf16[768,1024]{1,0:T(8,128)(2,1)S(1)}, u32[]{:S(2)}, u32[]{:S(2)}) %collective-permute-start.12) | collective-permute-done | bytes 1572896 | tf_op jit(solution)/shard_map/ppermute | solution.py:36
  44.9 0.4 collective-permute-done.11.refs_7_.refs_11_.refs_13_
  45.3 0.8 copy-done.2
  46.1 3.4 %collective-permute-start.13 = (bf16[768,1024]{1,0:T(8,128)(2,1)}, bf16[768,1024]{1,0:T(8,128)(2,1)}, u32[]{:S(2)}, u32[]{:S(2)}) collective-permute-start(bf16[768,1024]{1,0:T(8,128)(2,1)} %collective-permute-done.11.refs_7_.refs_11_.refs_13_), channel_id=1, source_target_pairs={{0,16},{1,49},{16,32},{17,1},{32,48},{33,17},{48,0},{49,33},{2,18}... | collective-permute-start | bytes 4718600 | tf_op jit(solution)/shard_map/ppermute | solution.py:36
  49.5 0.7 dynamic-slice_bitcast_fusion
  50.2 1.9 %fusion.2 = (f32[1024,128]{1,0:T(8,128)S(1)}, f32[1024,128]{1,0:T(8,128)S(1)}) fusion(f32[128]{0:T(128)S(1)} %get-tuple-element.47, f32[128]{0:T(128)S(1)} %get-tuple-element.48, f32[1024]{0:T(1024)S(1)} %convert_element_type.10, pred[]{:T(512)S(6)} %lt.43), kind=kLoop, calls=%fused_computation.5 | loop fusion | flops 524288 | bytes 1053697 | tf_op jit(solution)/shard_map/jit(_where)/select_n | solution.py:240
  52.2 2.7 %collective-permute-start.4 = (bf16[1024,768]{1,0:T(8,128)(2,1)}, bf16[1024,768]{1,0:T(8,128)(2,1)}, u32[]{:S(2)}, u32[]{:S(2)}) collective-permute-start(bf16[1024,768]{1,0:T(8,128)(2,1)} %copy-done.1), channel_id=1, source_target_pairs={{0,2},{1,7},{2,4},{3,1},{4,6},{5,3},{6,0},{7,5},{8,10},{9,15},{10,... | collective-permute-start | bytes 4718600 | tf_op jit(solution)/shard_map/ppermute | solution.py:36
  54.9 1.1 slice.22
  56.0 9.7 %collective-permute-done.6.refs_10_.refs_14_.refs_16_ = bf16[768,1024]{1,0:T(8,128)(2,1)} collective-permute-done((bf16[768,1024]{1,0:T(8,128)(2,1)S(1)}, bf16[768,1024]{1,0:T(8,128)(2,1)}, u32[]{:S(2)}, u32[]{:S(2)}) %collective-permute-start.6) | collective-permute-done | bytes 1572896 | tf_op jit(solution)/shard_map/ppermute | solution.py:183
  65.7 1.5 collective-permute-start.7
  67.2 3.0 %collective-permute-done.8.refs_8_ = bf16[576,768]{1,0:T(8,128)(2,1)} collective-permute-done((bf16[576,768]{1,0:T(8,128)(2,1)}, bf16[576,768]{1,0:T(8,128)(2,1)}, u32[]{:S(2)}, u32[]{:S(2)}) %collective-permute-start.8) | collective-permute-done | bytes 884768 | tf_op jit(solution)/shard_map/ppermute | solution.py:36
  70.2 12.3 %collective-permute-done.7.refs_5_ = bf16[448,768]{1,0:T(8,128)(2,1)} collective-permute-done((bf16[448,768]{1,0:T(8,128)(2,1)S(1)}, bf16[448,768]{1,0:T(8,128)(2,1)}, u32[]{:S(2)}, u32[]{:S(2)}) %collective-permute-start.7) | collective-permute-done | bytes 688160 | tf_op jit(solution)/shard_map/ppermute | solution.py:183
  82.5 1.3 collective-permute-start.17
  83.8 0.1 copy.9
  83.9 0.1 reshape.33.table_ref
  83.9 3.8 %collective-permute-done.9.refs_10_ = bf16[576,768]{1,0:T(8,128)(2,1)S(1)} collective-permute-done((bf16[576,768]{1,0:T(8,128)(2,1)}, bf16[576,768]{1,0:T(8,128)(2,1)S(1)}, u32[]{:S(2)}, u32[]{:S(2)}) %collective-permute-start.9) | collective-permute-done | bytes 884768 | tf_op jit(solution)/shard_map/ppermute | solution.py:36
  87.8 3.2 %collective-permute-start.10 = (bf16[448,768]{1,0:T(8,128)(2,1)}, bf16[448,768]{1,0:T(8,128)(2,1)S(1)}, u32[]{:S(2)}, u32[]{:S(2)}) collective-permute-start(bf16[448,768]{1,0:T(8,128)(2,1)} %collective-permute-done.7.refs_5_), channel_id=1, source_target_pairs={{0,2},{1,7},{2,4},{3,1},{4,6},{5,3},{6,0},{7,5},{8,10},{9,15},{10,... | collective-permute-start | bytes 2064392 | tf_op jit(solution)/shard_map/ppermute | solution.py:36
  91.0 5.6 %shard_map.67 = (f32[1024,512]{1,0:T(8,128)S(1)}, f32[1024,512]{1,0:T(8,128)S(1)}) custom-call(s32[16]{0:T(128)S(1)} %reshape.33.table_ref, bf16[1024,768]{1,0:T(8,128)(2,1)} %refs_0_.7, bf16[1024,768]{1,0:T(8,128)(2,1)} %copy-done.1, bf16[1024,768]{1,0:T(8,128)(2,1)} %collective-permute-done.1.refs_2_, bf16[1024,768]{1,0:T(8,128)(2,1)} %collective-permute-done.4.refs_3_, ...), custom_call_target="tpu_custom_call" | custom-call | flops 3221225472 | bytes 6291456 | tf_op jit(solution)/shard_map/pallas_call | solution.py:133
  96.6 0.1 collective-permute-start.14
  96.7 1.2 slice.29
  97.8 3.3 %collective-permute-start.19 = (bf16[384,1024]{1,0:T(8,128)(2,1)S(1)}, bf16[384,1024]{1,0:T(8,128)(2,1)S(1)}, u32[]{:S(2)}, u32[]{:S(2)}) collective-permute-start(bf16[384,1024]{1,0:T(8,128)(2,1)S(1)} %slice.29), channel_id=1, source_target_pairs={{0,64},{64,0},{1,65},{65,1},{2,66},{66,2},{3,67},{67,3},{4,68},{68... | collective-permute-start | bytes 2359304 | tf_op jit(solution)/shard_map/ppermute | solution.py:183
  101.1 1.2 slice.28
  102.3 2.4 %collective-permute-start.18 = (bf16[384,1024]{1,0:T(8,128)(2,1)S(1)}, bf16[384,1024]{1,0:T(8,128)(2,1)S(1)}, u32[]{:S(2)}, u32[]{:S(2)}) collective-permute-start(bf16[384,1024]{1,0:T(8,128)(2,1)S(1)} %slice.28), channel_id=1, source_target_pairs={{0,16},{1,49},{16,32},{17,1},{32,48},{33,17},{48,0},{49,33},{2,18}... | collective-permute-start | bytes 2359304 | tf_op jit(solution)/shard_map/ppermute | solution.py:36
  104.8 2.7 %collective-permute-start.15 = (bf16[448,768]{1,0:T(8,128)(2,1)S(1)}, bf16[448,768]{1,0:T(8,128)(2,1)S(1)}, u32[]{:S(2)}, u32[]{:S(2)}) collective-permute-start(bf16[448,768]{1,0:T(8,128)(2,1)S(1)} %collective-permute-done.10.refs_7_), channel_id=1, source_target_pairs={{0,2},{1,7},{2,4},{3,1},{4,6},{5,3},{6,0},{7,5},{8,10},{9,15},{10,... | collective-permute-start | bytes 2064392 | tf_op jit(solution)/shard_map/ppermute | solution.py:36
  107.4 2.5 %collective-permute-done.14.refs_9_ = bf16[448,768]{1,0:T(8,128)(2,1)S(1)} collective-permute-done((bf16[448,768]{1,0:T(8,128)(2,1)}, bf16[448,768]{1,0:T(8,128)(2,1)S(1)}, u32[]{:S(2)}, u32[]{:S(2)}) %collective-permute-start.14) | collective-permute-done | bytes 688160 | tf_op jit(solution)/shard_map/ppermute | solution.py:36
  109.9 0.9 copy-done.4
  110.7 9.8 %shard_map.68 = (f32[1024,512]{1,0:T(8,128)S(1)}, f32[1024,512]{1,0:T(8,128)S(1)}) custom-call(s32[16]{0:T(128)S(1)} %reshape.33.table_ref, bf16[1024,768]{1,0:T(8,128)(2,1)} %refs_0_.7, bf16[1024,768]{1,0:T(8,128)(2,1)} %copy-done.1, bf16[1024,768]{1,0:T(8,128)(2,1)} %collective-permute-done.1.refs_2_, bf16[1024,768]{1,0:T(8,128)(2,1)} %collective-permute-done.4.refs_3_, ...), custom_call_target="tpu_custom_call" | custom-call | flops 6442450944 | bytes 12582912 | tf_op jit(solution)/shard_map/pallas_call | solution.py:133
  120.6 4.2 %shard_map.70 = f32[1024,512]{1,0:T(8,128)S(1)} custom-call(s32[16]{0:T(128)S(1)} %reshape.33.table_ref, bf16[1024,768]{1,0:T(8,128)(2,1)} %refs_0_.7, bf16[1024,768]{1,0:T(8,128)(2,1)} %copy-done.1, bf16[1024,768]{1,0:T(8,128)(2,1)} %collective-permute-done.1.refs_2_, bf16[1024,768]{1,0:T(8,128)(2,1)} %collective-permute-done.4.refs_3_, ...), custom_call_target="tpu_custom_call" | custom-call | flops 1610612736 | bytes 4718592 | tf_op jit(solution)/shard_map/pallas_call | solution.py:133
  124.7 0.1 collective-permute-start.20
  124.8 4.2 %shard_map.69.refs_0_ = f32[1024,512]{1,0:T(8,128)S(1)} custom-call(s32[16]{0:T(128)S(1)} %reshape.33.table_ref, bf16[1024,768]{1,0:T(8,128)(2,1)} %refs_0_.7, bf16[1024,768]{1,0:T(8,128)(2,1)} %copy-done.1, bf16[1024,768]{1,0:T(8,128)(2,1)} %collective-permute-done.1.refs_2_, bf16[1024,768]{1,0:T(8,128)(2,1)} %collective-permute-done.4.refs_3_, ...), custom_call_target="tpu_custom_call" | custom-call | flops 1610612736 | bytes 4718592 | tf_op jit(solution)/shard_map/pallas_call | solution.py:133
  129.0 0.9 shard_map.71
  129.9 18.8 %all_to_all.19 = bf16[16,64,512]{2,1,0:T(8,128)(2,1)S(1)} all-to-all(bf16[16,64,512]{2,1,0:T(8,128)(2,1)S(1)} %bitcast.6), channel_id=1, replica_groups=mesh['xh'=2,'y'=4,'xl'=2,'z'=4,'c'=2] {'xl','z','c'}, dimensions={0} | all-to-all | bytes 2097152 | tf_op jit(solution)/shard_map/all_to_all | solution.py:254
  148.6 0.1 copy.11
  148.7 0.9 slice.30
  149.7 0.7 fusion.6
  (27 shorter events, 0.1 us)
Async XLA Ops:
  0.6 3.1 %copy-start = (bf16[1024,768]{1,0:T(8,128)(2,1)S(1)}, bf16[1024,768]{1,0:T(8,128)(2,1)}, u32[]{:S(2)}) copy-start(bf16[1024,768]{1,0:T(8,128)(2,1)} %refs_0_.7) | copy-start | bytes 4718596
  2.2 6.7 %collective-permute-start.5 = (bf16[768,512]{1,0:T(8,128)(2,1)S(1)}, bf16[768,512]{1,0:T(8,128)(2,1)S(1)}, u32[]{:S(2)}, u32[]{:S(2)}) collective-permute-start(bf16[768,512]{1,0:T(8,128)(2,1)S(1)} %get-tuple-element.42), channel_id=1, source_target_pairs={{0,1},{1,0},{2,3},{3,2},{4,5},{5,4},{6,7},{7,6},{8,9},{9,8},{10,11... | collective-permute-start | bytes 2359304 | tf_op jit(solution)/shard_map/ppermute | solution.py:183
  3.8 31.9 %collective-permute-start = (bf16[1024,768]{1,0:T(8,128)(2,1)S(1)}, bf16[1024,768]{1,0:T(8,128)(2,1)S(1)}, u32[]{:S(2)}, u32[]{:S(2)}) collective-permute-start(bf16[1024,768]{1,0:T(8,128)(2,1)S(1)} %copy-done), channel_id=1, source_target_pairs={{0,2},{1,7},{2,4},{3,1},{4,6},{5,3},{6,0},{7,5},{8,10},{9,15},{10,... | collective-permute-start | bytes 4718600 | tf_op jit(solution)/shard_map/ppermute | solution.py:36
  7.7 20.7 %collective-permute-start.2 = (bf16[576,768]{1,0:T(8,128)(2,1)S(1)}, bf16[576,768]{1,0:T(8,128)(2,1)}, u32[]{:S(2)}, u32[]{:S(2)}) collective-permute-start(bf16[576,768]{1,0:T(8,128)(2,1)S(1)} %slice.21), channel_id=1, source_target_pairs={{0,8},{8,0},{1,9},{9,1},{2,10},{10,2},{3,11},{11,3},{4,12},{12,4},... | collective-permute-start | bytes 2654216 | tf_op jit(solution)/shard_map/ppermute | solution.py:183
  8.9 40.5 %copy-start.5 = (s32[1024]{0:T(1024)S(1)}, s32[1024]{0:T(1024)}, u32[]{:S(2)}) copy-start(s32[1024]{0:T(1024)} %param.6) | copy-start | bytes 12292
  9.2 35.8 %collective-permute-start.12 = (bf16[768,1024]{1,0:T(8,128)(2,1)S(1)}, bf16[768,1024]{1,0:T(8,128)(2,1)S(1)}, u32[]{:S(2)}, u32[]{:S(2)}) collective-permute-start(bf16[768,1024]{1,0:T(8,128)(2,1)S(1)} %pad_maximum_fusion.refs_6_.refs_10_.refs_12_), channel_id=1, source_target_pairs={{0,48},{1,17},{16,0},{17,33},{32,16},{33,49},{48,32},{49,1},{2,50}... | collective-permute-start | bytes 4718600 | tf_op jit(solution)/shard_map/ppermute | solution.py:36
  10.5 34.7 %collective-permute-start.11 = (bf16[768,1024]{1,0:T(8,128)(2,1)S(1)}, bf16[768,1024]{1,0:T(8,128)(2,1)}, u32[]{:S(2)}, u32[]{:S(2)}) collective-permute-start(bf16[768,1024]{1,0:T(8,128)(2,1)S(1)} %pad_maximum_fusion.refs_6_.refs_10_.refs_12_), channel_id=1, source_target_pairs={{0,16},{1,49},{16,32},{17,1},{32,48},{33,17},{48,0},{49,33},{2,18}... | collective-permute-start | bytes 4718600 | tf_op jit(solution)/shard_map/ppermute | solution.py:36
  12.1 38.1 %collective-permute-start.1 = (bf16[1024,768]{1,0:T(8,128)(2,1)S(1)}, bf16[1024,768]{1,0:T(8,128)(2,1)}, u32[]{:S(2)}, u32[]{:S(2)}) collective-permute-start(bf16[1024,768]{1,0:T(8,128)(2,1)S(1)} %copy-done), channel_id=1, source_target_pairs={{0,6},{1,3},{2,0},{3,5},{4,2},{5,7},{6,4},{7,1},{8,14},{9,11},{10,... | collective-permute-start | bytes 4718600 | tf_op jit(solution)/shard_map/ppermute | solution.py:36
  28.3 37.4 %collective-permute-start.6 = (bf16[768,1024]{1,0:T(8,128)(2,1)S(1)}, bf16[768,1024]{1,0:T(8,128)(2,1)}, u32[]{:S(2)}, u32[]{:S(2)}) collective-permute-start(bf16[768,1024]{1,0:T(8,128)(2,1)S(1)} %pad_maximum_fusion.refs_6_.refs_10_.refs_12_), channel_id=1, source_target_pairs={{0,64},{64,0},{1,65},{65,1},{2,66},{66,2},{3,67},{67,3},{4,68},{68... | collective-permute-start | bytes 4718600 | tf_op jit(solution)/shard_map/ppermute | solution.py:183
  35.7 9.6 %copy-start.1 = (bf16[1024,768]{1,0:T(8,128)(2,1)}, bf16[1024,768]{1,0:T(8,128)(2,1)S(1)}, u32[]{:S(2)}) copy-start(bf16[1024,768]{1,0:T(8,128)(2,1)S(1)} %collective-permute-done.refs_1_) | copy-start | bytes 4718596
  35.7 16.5 %collective-permute-start.3 = (bf16[576,768]{1,0:T(8,128)(2,1)}, bf16[576,768]{1,0:T(8,128)(2,1)}, u32[]{:S(2)}, u32[]{:S(2)}) collective-permute-start(bf16[576,768]{1,0:T(8,128)(2,1)} %collective-permute-done.2.refs_4_), channel_id=1, source_target_pairs={{0,2},{1,7},{2,4},{3,1},{4,6},{5,3},{6,0},{7,5},{8,10},{9,15},{10,... | collective-permute-start | bytes 2654216 | tf_op jit(solution)/shard_map/ppermute | solution.py:36
  44.9 1.1 copy-start.2
  46.1 36.4 %collective-permute-start.13 = (bf16[768,1024]{1,0:T(8,128)(2,1)}, bf16[768,1024]{1,0:T(8,128)(2,1)}, u32[]{:S(2)}, u32[]{:S(2)}) collective-permute-start(bf16[768,1024]{1,0:T(8,128)(2,1)} %collective-permute-done.11.refs_7_.refs_11_.refs_13_), channel_id=1, source_target_pairs={{0,16},{1,49},{16,32},{17,1},{32,48},{33,17},{48,0},{49,33},{2,18}... | collective-permute-start | bytes 4718600 | tf_op jit(solution)/shard_map/ppermute | solution.py:36
  50.2 20.0 %collective-permute-start.8 = (bf16[576,768]{1,0:T(8,128)(2,1)}, bf16[576,768]{1,0:T(8,128)(2,1)}, u32[]{:S(2)}, u32[]{:S(2)}) collective-permute-start(bf16[576,768]{1,0:T(8,128)(2,1)} %collective-permute-done.2.refs_4_), channel_id=1, source_target_pairs={{0,6},{1,3},{2,0},{3,5},{4,2},{5,7},{6,4},{7,1},{8,14},{9,11},{10,... | collective-permute-start | bytes 2654216 | tf_op jit(solution)/shard_map/ppermute | solution.py:36
  52.2 35.6 %collective-permute-start.4 = (bf16[1024,768]{1,0:T(8,128)(2,1)}, bf16[1024,768]{1,0:T(8,128)(2,1)}, u32[]{:S(2)}, u32[]{:S(2)}) collective-permute-start(bf16[1024,768]{1,0:T(8,128)(2,1)} %copy-done.1), channel_id=1, source_target_pairs={{0,2},{1,7},{2,4},{3,1},{4,6},{5,3},{6,0},{7,5},{8,10},{9,15},{10,... | collective-permute-start | bytes 4718600 | tf_op jit(solution)/shard_map/ppermute | solution.py:36
  65.7 16.8 %collective-permute-start.7 = (bf16[448,768]{1,0:T(8,128)(2,1)S(1)}, bf16[448,768]{1,0:T(8,128)(2,1)}, u32[]{:S(2)}, u32[]{:S(2)}) collective-permute-start(bf16[448,768]{1,0:T(8,128)(2,1)S(1)} %slice.22), channel_id=1, source_target_pairs={{0,8},{8,0},{1,9},{9,1},{2,10},{10,2},{3,11},{11,3},{4,12},{12,4},... | collective-permute-start | bytes 2064392 | tf_op jit(solution)/shard_map/ppermute | solution.py:183
  70.2 17.6 %collective-permute-start.9 = (bf16[576,768]{1,0:T(8,128)(2,1)}, bf16[576,768]{1,0:T(8,128)(2,1)S(1)}, u32[]{:S(2)}, u32[]{:S(2)}) collective-permute-start(bf16[576,768]{1,0:T(8,128)(2,1)} %collective-permute-done.3.refs_6_), channel_id=1, source_target_pairs={{0,2},{1,7},{2,4},{3,1},{4,6},{5,3},{6,0},{7,5},{8,10},{9,15},{10,... | collective-permute-start | bytes 2654216 | tf_op jit(solution)/shard_map/ppermute | solution.py:36
  70.2 31.0 %collective-permute-start.16 = (bf16[768,1024]{1,0:T(8,128)(2,1)}, bf16[768,1024]{1,0:T(8,128)(2,1)}, u32[]{:S(2)}, u32[]{:S(2)}) collective-permute-start(bf16[768,1024]{1,0:T(8,128)(2,1)} %collective-permute-done.6.refs_10_.refs_14_.refs_16_), channel_id=1, source_target_pairs={{0,16},{1,49},{16,32},{17,1},{32,48},{33,17},{48,0},{49,33},{2,18}... | collective-permute-start | bytes 4718600 | tf_op jit(solution)/shard_map/ppermute | solution.py:36
  82.5 27.4 %collective-permute-start.17 = (bf16[768,1024]{1,0:T(8,128)(2,1)}, bf16[768,1024]{1,0:T(8,128)(2,1)}, u32[]{:S(2)}, u32[]{:S(2)}) collective-permute-start(bf16[768,1024]{1,0:T(8,128)(2,1)} %collective-permute-done.6.refs_10_.refs_14_.refs_16_), channel_id=1, source_target_pairs={{0,48},{1,17},{16,0},{17,33},{32,16},{33,49},{48,32},{49,1},{2,50}... | collective-permute-start | bytes 4718600 | tf_op jit(solution)/shard_map/ppermute | solution.py:36
  87.8 17.0 %collective-permute-start.10 = (bf16[448,768]{1,0:T(8,128)(2,1)}, bf16[448,768]{1,0:T(8,128)(2,1)S(1)}, u32[]{:S(2)}, u32[]{:S(2)}) collective-permute-start(bf16[448,768]{1,0:T(8,128)(2,1)} %collective-permute-done.7.refs_5_), channel_id=1, source_target_pairs={{0,2},{1,7},{2,4},{3,1},{4,6},{5,3},{6,0},{7,5},{8,10},{9,15},{10,... | collective-permute-start | bytes 2064392 | tf_op jit(solution)/shard_map/ppermute | solution.py:36
  96.6 13.3 %collective-permute-start.14 = (bf16[448,768]{1,0:T(8,128)(2,1)}, bf16[448,768]{1,0:T(8,128)(2,1)S(1)}, u32[]{:S(2)}, u32[]{:S(2)}) collective-permute-start(bf16[448,768]{1,0:T(8,128)(2,1)} %collective-permute-done.7.refs_5_), channel_id=1, source_target_pairs={{0,6},{1,3},{2,0},{3,5},{4,2},{5,7},{6,4},{7,1},{8,14},{9,11},{10,... | collective-permute-start | bytes 2064392 | tf_op jit(solution)/shard_map/ppermute | solution.py:36
  97.8 22.7 %collective-permute-start.19 = (bf16[384,1024]{1,0:T(8,128)(2,1)S(1)}, bf16[384,1024]{1,0:T(8,128)(2,1)S(1)}, u32[]{:S(2)}, u32[]{:S(2)}) collective-permute-start(bf16[384,1024]{1,0:T(8,128)(2,1)S(1)} %slice.29), channel_id=1, source_target_pairs={{0,64},{64,0},{1,65},{65,1},{2,66},{66,2},{3,67},{67,3},{4,68},{68... | collective-permute-start | bytes 2359304 | tf_op jit(solution)/shard_map/ppermute | solution.py:183
  102.3 18.2 %collective-permute-start.18 = (bf16[384,1024]{1,0:T(8,128)(2,1)S(1)}, bf16[384,1024]{1,0:T(8,128)(2,1)S(1)}, u32[]{:S(2)}, u32[]{:S(2)}) collective-permute-start(bf16[384,1024]{1,0:T(8,128)(2,1)S(1)} %slice.28), channel_id=1, source_target_pairs={{0,16},{1,49},{16,32},{17,1},{32,48},{33,17},{48,0},{49,33},{2,18}... | collective-permute-start | bytes 2359304 | tf_op jit(solution)/shard_map/ppermute | solution.py:36
  104.8 5.1 %copy-start.3 = (bf16[448,768]{1,0:T(8,128)(2,1)}, bf16[448,768]{1,0:T(8,128)(2,1)S(1)}, u32[]{:S(2)}) copy-start(bf16[448,768]{1,0:T(8,128)(2,1)S(1)} %collective-permute-done.10.refs_7_) | copy-start | bytes 2064388
  104.8 15.8 %collective-permute-start.15 = (bf16[448,768]{1,0:T(8,128)(2,1)S(1)}, bf16[448,768]{1,0:T(8,128)(2,1)S(1)}, u32[]{:S(2)}, u32[]{:S(2)}) collective-permute-start(bf16[448,768]{1,0:T(8,128)(2,1)S(1)} %collective-permute-done.10.refs_7_), channel_id=1, source_target_pairs={{0,2},{1,7},{2,4},{3,1},{4,6},{5,3},{6,0},{7,5},{8,10},{9,15},{10,... | collective-permute-start | bytes 2064392 | tf_op jit(solution)/shard_map/ppermute | solution.py:36
  109.9 0.9 copy-start.4
  124.7 4.3 %collective-permute-start.20 = (f32[1024,512]{1,0:T(8,128)S(1)}, f32[1024,512]{1,0:T(8,128)S(1)}, u32[]{:S(2)}, u32[]{:S(2)}) collective-permute-start(f32[1024,512]{1,0:T(8,128)S(1)} %shard_map.70), channel_id=1, source_target_pairs={{0,1},{1,0},{2,3},{3,2},{4,5},{5,4},{6,7},{7,6},{8,9},{9,8},{10,11... | collective-permute-start | bytes 6291464 | tf_op jit(solution)/shard_map/ppermute | solution.py:183

commit v7 on v6

--- a/solution.py
+++ b/solution.py
@@ -193,10 +193,10 @@
     y_other = ring_step(b, "y", -1)
 
     r = swap(after(b, p_0), "xh")
-    p_0_near = ring_step(after(p_0, z_near), "z")
+    p_0_near = ring_step(after(p_0, z_near, *early), "z")
     p_0_other = ring_step(after(p_0, z_other), "z", -1)
     y_far = ring_step(after(y_near, y_other), "y")
-    z_far = ring_step(after(z_near, p_0_near, *early), "z")
+    z_far = ring_step(after(z_near, p_0_near), "z")
     p_0_far = ring_step(after(p_0_near, p_0_other), "z")
 
     p_1 = swap(after(a[part:], r), "xl")

time: 153 us -> 152 us (level)
  waiting for transfers between devices: 58.2 us -> 53.3 us
  starting transfers between devices: 36.5 us -> 39.5 us
    ppermute x15, waiting for transfers between devices: 20 us -> 16.6 us  [ring_step(): return lax.ppermute(block, (axis, 'c'), pairs)]
    ppermute x15, starting transfers between devices: 26.1 us -> 29.1 us  [ring_step(): return lax.ppermute(block, (axis, 'c'), pairs)]
    ppermute x6, waiting for transfers between devices: 38.2 us -> 36.7 us  [swap(): return lax.ppermute(block, axis, SWAP)]
  transfers between devices with their start and end apart: 21 -> 21, of which waited for: 9 -> 10; matrix products, arithmetic and copies ran while one was open for 4% -> 5% of each run, Pallas kernels for 13% -> 13%
where the time goes in v7:
time: 152 us; the launch traced here: 150 us
  waiting for transfers between devices  53.3 us (35%)
  starting transfers between devices  39.5 us (26%)
  Pallas kernels  24.7 us (16%)
  blocking collectives  19.3 us (13%)
  local copies, waits for them, and re-layouts  10.7 us (7%)
  other arithmetic  2.16 us (1%)
    ppermute x6, waiting for transfers between devices, swap(): return lax.ppermute(block, axis, SWAP)  36.7 us
    ppermute x15, starting transfers between devices, ring_step(): return lax.ppermute(block, (axis, 'c'), pairs)  29.1 us
    pallas_call x4, Pallas kernels, product(): pl.pallas_call(kernel, out_shape=[jax.ShapeDtypeStruct((rows, width), jnp...  23.8 us
    all_to_all x1, blocking collectives, shards(): lax.all_to_all(turned, ('xl', 'z', 'c'), split_axis=0, concat_axis=1, til...  19.3 us
    ppermute x15, waiting for transfers between devices, ring_step(): return lax.ppermute(block, (axis, 'c'), pairs)  16.6 us
    ppermute x6, starting transfers between devices, swap(): return lax.ppermute(block, axis, SWAP)  10.4 us
  transfers between devices with their start and end apart: 21, of which 10 were waited for; matrix products, arithmetic and copies ran while one was open for 5% of the time, Pallas kernels for 13%

profile of v7, /device:TPU:1, one launch (start us, length us, event | category | flops | bytes accessed | tf_op | source)
XLA Modules:
  0.0 150.4 jit_solution(17661243636203754653)
XLA Ops:
  0.6 1.5 constant_dynamic-slice_fusion.1
  2.1 1.5 collective-permute-start.5
  3.6 3.8 %collective-permute-start = (bf16[1024,768]{1,0:T(8,128)(2,1)}, bf16[1024,768]{1,0:T(8,128)(2,1)}, u32[]{:S(2)}, u32[]{:S(2)}) collective-permute-start(bf16[1024,768]{1,0:T(8,128)(2,1)} %refs_0_.7), channel_id=1, source_target_pairs={{0,2},{1,7},{2,4},{3,1},{4,6},{5,3},{6,0},{7,5},{8,10},{9,15},{10,... | collective-permute-start | bytes 4718600 | tf_op jit(solution)/shard_map/ppermute | solution.py:36
  7.5 1.3 slice.21
  8.7 1.3 collective-permute-start.2
  10.0 0.2 pad_maximum_fusion.refs_6_.refs_10_.refs_12_
  10.2 1.4 collective-permute-start.12
  11.6 1.5 %collective-permute-start.11 = (bf16[768,1024]{1,0:T(8,128)(2,1)S(1)}, bf16[768,1024]{1,0:T(8,128)(2,1)}, u32[]{:S(2)}, u32[]{:S(2)}) collective-permute-start(bf16[768,1024]{1,0:T(8,128)(2,1)S(1)} %pad_maximum_fusion.refs_6_.refs_10_.refs_12_), channel_id=1, source_target_pairs={{0,16},{1,49},{16,32},{17,1},{32,48},{33,17},{48,0},{49,33},{2,18}... | collective-permute-start | bytes 4718600 | tf_op jit(solution)/shard_map/ppermute | solution.py:36
  13.1 16.1 %collective-permute-done.2.refs_4_ = bf16[576,768]{1,0:T(8,128)(2,1)S(1)} collective-permute-done((bf16[576,768]{1,0:T(8,128)(2,1)S(1)}, bf16[576,768]{1,0:T(8,128)(2,1)S(1)}, u32[]{:S(2)}, u32[]{:S(2)}) %collective-permute-start.2) | collective-permute-done | bytes 884768 | tf_op jit(solution)/shard_map/ppermute | solution.py:183
  29.3 2.7 %collective-permute-start.6 = (bf16[768,1024]{1,0:T(8,128)(2,1)S(1)}, bf16[768,1024]{1,0:T(8,128)(2,1)}, u32[]{:S(2)}, u32[]{:S(2)}) collective-permute-start(bf16[768,1024]{1,0:T(8,128)(2,1)S(1)} %pad_maximum_fusion.refs_6_.refs_10_.refs_12_), channel_id=1, source_target_pairs={{0,64},{64,0},{1,65},{65,1},{2,66},{66,2},{3,67},{67,3},{4,68},{68... | collective-permute-start | bytes 4718600 | tf_op jit(solution)/shard_map/ppermute | solution.py:183
  32.1 0.7 dynamic-slice_bitcast_fusion
  32.7 1.9 %fusion.2 = (f32[1024,128]{1,0:T(8,128)S(1)}, f32[1024,128]{1,0:T(8,128)S(1)}) fusion(f32[128]{0:T(128)S(1)} %get-tuple-element.47, f32[128]{0:T(128)S(1)} %get-tuple-element.48, f32[1024]{0:T(1024)S(1)} %convert_element_type.10, pred[]{:T(512)S(6)} %lt.43), kind=kLoop, calls=%fused_computation.5 | loop fusion | flops 524288 | bytes 1053697 | tf_op jit(solution)/shard_map/jit(_where)/select_n | solution.py:240
  34.7 0.5 collective-permute-done.refs_1_
  35.2 3.4 %collective-permute-start.3 = (bf16[576,768]{1,0:T(8,128)(2,1)S(1)}, bf16[576,768]{1,0:T(8,128)(2,1)}, u32[]{:S(2)}, u32[]{:S(2)}) collective-permute-start(bf16[576,768]{1,0:T(8,128)(2,1)S(1)} %collective-permute-done.2.refs_4_), channel_id=1, source_target_pairs={{0,2},{1,7},{2,4},{3,1},{4,6},{5,3},{6,0},{7,5},{8,10},{9,15},{10,... | collective-permute-start | bytes 2654216 | tf_op jit(solution)/shard_map/ppermute | solution.py:36
  38.6 7.5 %collective-permute-done.12.refs_8_.refs_12_.refs_14_ = bf16[768,1024]{1,0:T(8,128)(2,1)} collective-permute-done((bf16[768,1024]{1,0:T(8,128)(2,1)S(1)}, bf16[768,1024]{1,0:T(8,128)(2,1)}, u32[]{:S(2)}, u32[]{:S(2)}) %collective-permute-start.12) | collective-permute-done | bytes 1572896 | tf_op jit(solution)/shard_map/ppermute | solution.py:36
  46.1 0.1 collective-permute-done.11.refs_7_.refs_11_.refs_13_
  46.2 3.5 %collective-permute-start.13 = (bf16[768,1024]{1,0:T(8,128)(2,1)}, bf16[768,1024]{1,0:T(8,128)(2,1)}, u32[]{:S(2)}, u32[]{:S(2)}) collective-permute-start(bf16[768,1024]{1,0:T(8,128)(2,1)} %collective-permute-done.11.refs_7_.refs_11_.refs_13_), channel_id=1, source_target_pairs={{0,16},{1,49},{16,32},{17,1},{32,48},{33,17},{48,0},{49,33},{2,18}... | collective-permute-start | bytes 4718600 | tf_op jit(solution)/shard_map/ppermute | solution.py:36
  49.8 2.8 %collective-permute-done.3.refs_6_ = bf16[576,768]{1,0:T(8,128)(2,1)} collective-permute-done((bf16[576,768]{1,0:T(8,128)(2,1)S(1)}, bf16[576,768]{1,0:T(8,128)(2,1)}, u32[]{:S(2)}, u32[]{:S(2)}) %collective-permute-start.3) | collective-permute-done | bytes 884768 | tf_op jit(solution)/shard_map/ppermute | solution.py:36
  52.6 3.5 %collective-permute-start.4 = (bf16[1024,768]{1,0:T(8,128)(2,1)}, bf16[1024,768]{1,0:T(8,128)(2,1)}, u32[]{:S(2)}, u32[]{:S(2)}) collective-permute-start(bf16[1024,768]{1,0:T(8,128)(2,1)} %collective-permute-done.refs_1_), channel_id=1, source_target_pairs={{0,2},{1,7},{2,4},{3,1},{4,6},{5,3},{6,0},{7,5},{8,10},{9,15},{10,... | collective-permute-start | bytes 4718600 | tf_op jit(solution)/shard_map/ppermute | solution.py:36
  56.1 1.1 slice.22
  57.2 9.2 %collective-permute-done.6.refs_10_.refs_14_.refs_16_ = bf16[768,1024]{1,0:T(8,128)(2,1)} collective-permute-done((bf16[768,1024]{1,0:T(8,128)(2,1)S(1)}, bf16[768,1024]{1,0:T(8,128)(2,1)}, u32[]{:S(2)}, u32[]{:S(2)}) %collective-permute-start.6) | collective-permute-done | bytes 1572896 | tf_op jit(solution)/shard_map/ppermute | solution.py:183
  66.4 1.5 %collective-permute-start.7 = (bf16[448,768]{1,0:T(8,128)(2,1)S(1)}, bf16[448,768]{1,0:T(8,128)(2,1)}, u32[]{:S(2)}, u32[]{:S(2)}) collective-permute-start(bf16[448,768]{1,0:T(8,128)(2,1)S(1)} %slice.22), channel_id=1, source_target_pairs={{0,8},{8,0},{1,9},{9,1},{2,10},{10,2},{3,11},{11,3},{4,12},{12,4},... | collective-permute-start | bytes 2064392 | tf_op jit(solution)/shard_map/ppermute | solution.py:183
  67.9 1.0 collective-permute-done.8.refs_8_
  68.9 0.9 copy-done.1
  69.8 2.3 %collective-permute-start.16 = (bf16[768,1024]{1,0:T(8,128)(2,1)}, bf16[768,1024]{1,0:T(8,128)(2,1)}, u32[]{:S(2)}, u32[]{:S(2)}) collective-permute-start(bf16[768,1024]{1,0:T(8,128)(2,1)} %collective-permute-done.6.refs_10_.refs_14_.refs_16_), channel_id=1, source_target_pairs={{0,16},{1,49},{16,32},{17,1},{32,48},{33,17},{48,0},{49,33},{2,18}... | collective-permute-start | bytes 4718600 | tf_op jit(solution)/shard_map/ppermute | solution.py:36
  72.2 11.4 %collective-permute-done.7.refs_5_ = bf16[448,768]{1,0:T(8,128)(2,1)} collective-permute-done((bf16[448,768]{1,0:T(8,128)(2,1)S(1)}, bf16[448,768]{1,0:T(8,128)(2,1)}, u32[]{:S(2)}, u32[]{:S(2)}) %collective-permute-start.7) | collective-permute-done | bytes 688160 | tf_op jit(solution)/shard_map/ppermute | solution.py:183
  83.5 1.3 collective-permute-start.17
  84.8 0.1 copy.9
  84.9 0.1 reshape.33.table_ref
  85.0 2.9 %collective-permute-done.9.refs_10_ = bf16[576,768]{1,0:T(8,128)(2,1)S(1)} collective-permute-done((bf16[576,768]{1,0:T(8,128)(2,1)}, bf16[576,768]{1,0:T(8,128)(2,1)S(1)}, u32[]{:S(2)}, u32[]{:S(2)}) %collective-permute-start.9) | collective-permute-done | bytes 884768 | tf_op jit(solution)/shard_map/ppermute | solution.py:36
  87.9 2.8 %collective-permute-start.10 = (bf16[448,768]{1,0:T(8,128)(2,1)}, bf16[448,768]{1,0:T(8,128)(2,1)S(1)}, u32[]{:S(2)}, u32[]{:S(2)}) collective-permute-start(bf16[448,768]{1,0:T(8,128)(2,1)} %collective-permute-done.7.refs_5_), channel_id=1, source_target_pairs={{0,2},{1,7},{2,4},{3,1},{4,6},{5,3},{6,0},{7,5},{8,10},{9,15},{10,... | collective-permute-start | bytes 2064392 | tf_op jit(solution)/shard_map/ppermute | solution.py:36
  90.7 5.6 %shard_map.67 = (f32[1024,512]{1,0:T(8,128)S(1)}, f32[1024,512]{1,0:T(8,128)S(1)}) custom-call(s32[16]{0:T(128)S(1)} %reshape.33.table_ref, bf16[1024,768]{1,0:T(8,128)(2,1)} %refs_0_.7, bf16[1024,768]{1,0:T(8,128)(2,1)} %collective-permute-done.refs_1_, bf16[1024,768]{1,0:T(8,128)(2,1)} %collective-permute-done.1.refs_2_, ...), custom_call_target="tpu_custom_call" | custom-call | flops 3221225472 | bytes 6291456 | tf_op jit(solution)/shard_map/pallas_call | solution.py:133
  96.4 1.2 slice.29
  97.6 3.3 %collective-permute-start.19 = (bf16[384,1024]{1,0:T(8,128)(2,1)S(1)}, bf16[384,1024]{1,0:T(8,128)(2,1)S(1)}, u32[]{:S(2)}, u32[]{:S(2)}) collective-permute-start(bf16[384,1024]{1,0:T(8,128)(2,1)S(1)} %slice.29), channel_id=1, source_target_pairs={{0,64},{64,0},{1,65},{65,1},{2,66},{66,2},{3,67},{67,3},{4,68},{68... | collective-permute-start | bytes 2359304 | tf_op jit(solution)/shard_map/ppermute | solution.py:183
  100.9 1.2 slice.28
  102.1 2.8 %collective-permute-start.18 = (bf16[384,1024]{1,0:T(8,128)(2,1)S(1)}, bf16[384,1024]{1,0:T(8,128)(2,1)S(1)}, u32[]{:S(2)}, u32[]{:S(2)}) collective-permute-start(bf16[384,1024]{1,0:T(8,128)(2,1)S(1)} %slice.28), channel_id=1, source_target_pairs={{0,16},{1,49},{16,32},{17,1},{32,48},{33,17},{48,0},{49,33},{2,18}... | collective-permute-start | bytes 2359304 | tf_op jit(solution)/shard_map/ppermute | solution.py:36
  104.9 2.7 %collective-permute-start.15 = (bf16[448,768]{1,0:T(8,128)(2,1)S(1)}, bf16[448,768]{1,0:T(8,128)(2,1)S(1)}, u32[]{:S(2)}, u32[]{:S(2)}) collective-permute-start(bf16[448,768]{1,0:T(8,128)(2,1)S(1)} %collective-permute-done.10.refs_7_), channel_id=1, source_target_pairs={{0,2},{1,7},{2,4},{3,1},{4,6},{5,3},{6,0},{7,5},{8,10},{9,15},{10,... | collective-permute-start | bytes 2064392 | tf_op jit(solution)/shard_map/ppermute | solution.py:36
  107.5 1.7 %collective-permute-done.14.refs_9_ = bf16[448,768]{1,0:T(8,128)(2,1)S(1)} collective-permute-done((bf16[448,768]{1,0:T(8,128)(2,1)}, bf16[448,768]{1,0:T(8,128)(2,1)S(1)}, u32[]{:S(2)}, u32[]{:S(2)}) %collective-permute-start.14) | collective-permute-done | bytes 688160 | tf_op jit(solution)/shard_map/ppermute | solution.py:36
  109.2 0.9 copy-done.3
  110.1 9.8 %shard_map.68 = (f32[1024,512]{1,0:T(8,128)S(1)}, f32[1024,512]{1,0:T(8,128)S(1)}) custom-call(s32[16]{0:T(128)S(1)} %reshape.33.table_ref, bf16[1024,768]{1,0:T(8,128)(2,1)} %refs_0_.7, bf16[1024,768]{1,0:T(8,128)(2,1)} %collective-permute-done.refs_1_, bf16[1024,768]{1,0:T(8,128)(2,1)} %collective-permute-done.1.refs_2_, ...), custom_call_target="tpu_custom_call" | custom-call | flops 6442450944 | bytes 12582912 | tf_op jit(solution)/shard_map/pallas_call | solution.py:133
  120.0 4.2 %shard_map.70 = f32[1024,512]{1,0:T(8,128)S(1)} custom-call(s32[16]{0:T(128)S(1)} %reshape.33.table_ref, bf16[1024,768]{1,0:T(8,128)(2,1)} %refs_0_.7, bf16[1024,768]{1,0:T(8,128)(2,1)} %collective-permute-done.refs_1_, bf16[1024,768]{1,0:T(8,128)(2,1)} %collective-permute-done.1.refs_2_, bf16[1024,768]{1,0:T(8,128)(2,1)} %collective-permute-done.4.refs_3_, ...), custom_call_target="tpu_custom_call" | custom-call | flops 1610612736 | bytes 4718592 | tf_op jit(solution)/shard_map/pallas_call | solution.py:133
  124.2 0.1 collective-permute-start.20
  124.3 4.2 %shard_map.69.refs_0_ = f32[1024,512]{1,0:T(8,128)S(1)} custom-call(s32[16]{0:T(128)S(1)} %reshape.33.table_ref, bf16[1024,768]{1,0:T(8,128)(2,1)} %refs_0_.7, bf16[1024,768]{1,0:T(8,128)(2,1)} %collective-permute-done.refs_1_, bf16[1024,768]{1,0:T(8,128)(2,1)} %collective-permute-done.1.refs_2_, bf16[1024,768]{1,0:T(8,128)(2,1)} %collective-permute-done.4.refs_3_, ...), custom_call_target="tpu_custom_call" | custom-call | flops 1610612736 | bytes 4718592 | tf_op jit(solution)/shard_map/pallas_call | solution.py:133
  128.4 0.9 shard_map.71
  129.4 19.3 %all_to_all.19 = bf16[16,64,512]{2,1,0:T(8,128)(2,1)S(1)} all-to-all(bf16[16,64,512]{2,1,0:T(8,128)(2,1)S(1)} %bitcast.6), channel_id=1, replica_groups=mesh['xh'=2,'y'=4,'xl'=2,'z'=4,'c'=2] {'xl','z','c'}, dimensions={0} | all-to-all | bytes 2097152 | tf_op jit(solution)/shard_map/all_to_all | solution.py:254
  148.6 0.1 copy.11
  148.7 0.9 slice.30
  149.7 0.7 fusion.6
  (25 shorter events, 0.1 us)
Async XLA Ops:
  2.1 7.9 %collective-permute-start.5 = (bf16[768,512]{1,0:T(8,128)(2,1)S(1)}, bf16[768,512]{1,0:T(8,128)(2,1)S(1)}, u32[]{:S(2)}, u32[]{:S(2)}) collective-permute-start(bf16[768,512]{1,0:T(8,128)(2,1)S(1)} %get-tuple-element.42), channel_id=1, source_target_pairs={{0,1},{1,0},{2,3},{3,2},{4,5},{5,4},{6,7},{7,6},{8,9},{9,8},{10,11... | collective-permute-start | bytes 2359304 | tf_op jit(solution)/shard_map/ppermute | solution.py:183
  3.6 31.6 %collective-permute-start = (bf16[1024,768]{1,0:T(8,128)(2,1)}, bf16[1024,768]{1,0:T(8,128)(2,1)}, u32[]{:S(2)}, u32[]{:S(2)}) collective-permute-start(bf16[1024,768]{1,0:T(8,128)(2,1)} %refs_0_.7), channel_id=1, source_target_pairs={{0,2},{1,7},{2,4},{3,1},{4,6},{5,3},{6,0},{7,5},{8,10},{9,15},{10,... | collective-permute-start | bytes 4718600 | tf_op jit(solution)/shard_map/ppermute | solution.py:36
  8.7 20.6 %collective-permute-start.2 = (bf16[576,768]{1,0:T(8,128)(2,1)S(1)}, bf16[576,768]{1,0:T(8,128)(2,1)S(1)}, u32[]{:S(2)}, u32[]{:S(2)}) collective-permute-start(bf16[576,768]{1,0:T(8,128)(2,1)S(1)} %slice.21), channel_id=1, source_target_pairs={{0,8},{8,0},{1,9},{9,1},{2,10},{10,2},{3,11},{11,3},{4,12},{12,4},... | collective-permute-start | bytes 2654216 | tf_op jit(solution)/shard_map/ppermute | solution.py:183
  10.0 22.0 %copy-start.4 = (s32[1024]{0:T(1024)S(1)}, s32[1024]{0:T(1024)}, u32[]{:S(2)}) copy-start(s32[1024]{0:T(1024)} %param.6) | copy-start | bytes 12292
  10.2 35.9 %collective-permute-start.12 = (bf16[768,1024]{1,0:T(8,128)(2,1)S(1)}, bf16[768,1024]{1,0:T(8,128)(2,1)}, u32[]{:S(2)}, u32[]{:S(2)}) collective-permute-start(bf16[768,1024]{1,0:T(8,128)(2,1)S(1)} %pad_maximum_fusion.refs_6_.refs_10_.refs_12_), channel_id=1, source_target_pairs={{0,48},{1,17},{16,0},{17,33},{32,16},{33,49},{48,32},{49,1},{2,50}... | collective-permute-start | bytes 4718600 | tf_op jit(solution)/shard_map/ppermute | solution.py:36
  11.6 34.6 %collective-permute-start.11 = (bf16[768,1024]{1,0:T(8,128)(2,1)S(1)}, bf16[768,1024]{1,0:T(8,128)(2,1)}, u32[]{:S(2)}, u32[]{:S(2)}) collective-permute-start(bf16[768,1024]{1,0:T(8,128)(2,1)S(1)} %pad_maximum_fusion.refs_6_.refs_10_.refs_12_), channel_id=1, source_target_pairs={{0,16},{1,49},{16,32},{17,1},{32,48},{33,17},{48,0},{49,33},{2,18}... | collective-permute-start | bytes 4718600 | tf_op jit(solution)/shard_map/ppermute | solution.py:36
  13.1 36.6 %collective-permute-start.1 = (bf16[1024,768]{1,0:T(8,128)(2,1)}, bf16[1024,768]{1,0:T(8,128)(2,1)}, u32[]{:S(2)}, u32[]{:S(2)}) collective-permute-start(bf16[1024,768]{1,0:T(8,128)(2,1)} %refs_0_.7), channel_id=1, source_target_pairs={{0,6},{1,3},{2,0},{3,5},{4,2},{5,7},{6,4},{7,1},{8,14},{9,11},{10,... | collective-permute-start | bytes 4718600 | tf_op jit(solution)/shard_map/ppermute | solution.py:36
  29.3 38.7 %copy-start = (bf16[576,768]{1,0:T(8,128)(2,1)}, bf16[576,768]{1,0:T(8,128)(2,1)S(1)}, u32[]{:S(2)}) copy-start(bf16[576,768]{1,0:T(8,128)(2,1)S(1)} %collective-permute-done.2.refs_4_) | copy-start | bytes 2654212
  29.3 37.1 %collective-permute-start.6 = (bf16[768,1024]{1,0:T(8,128)(2,1)S(1)}, bf16[768,1024]{1,0:T(8,128)(2,1)}, u32[]{:S(2)}, u32[]{:S(2)}) collective-permute-start(bf16[768,1024]{1,0:T(8,128)(2,1)S(1)} %pad_maximum_fusion.refs_6_.refs_10_.refs_12_), channel_id=1, source_target_pairs={{0,64},{64,0},{1,65},{65,1},{2,66},{66,2},{3,67},{67,3},{4,68},{68... | collective-permute-start | bytes 4718600 | tf_op jit(solution)/shard_map/ppermute | solution.py:183
  35.2 17.4 %collective-permute-start.3 = (bf16[576,768]{1,0:T(8,128)(2,1)S(1)}, bf16[576,768]{1,0:T(8,128)(2,1)}, u32[]{:S(2)}, u32[]{:S(2)}) collective-permute-start(bf16[576,768]{1,0:T(8,128)(2,1)S(1)} %collective-permute-done.2.refs_4_), channel_id=1, source_target_pairs={{0,2},{1,7},{2,4},{3,1},{4,6},{5,3},{6,0},{7,5},{8,10},{9,15},{10,... | collective-permute-start | bytes 2654216 | tf_op jit(solution)/shard_map/ppermute | solution.py:36
  46.2 37.3 %collective-permute-start.13 = (bf16[768,1024]{1,0:T(8,128)(2,1)}, bf16[768,1024]{1,0:T(8,128)(2,1)}, u32[]{:S(2)}, u32[]{:S(2)}) collective-permute-start(bf16[768,1024]{1,0:T(8,128)(2,1)} %collective-permute-done.11.refs_7_.refs_11_.refs_13_), channel_id=1, source_target_pairs={{0,16},{1,49},{16,32},{17,1},{32,48},{33,17},{48,0},{49,33},{2,18}... | collective-permute-start | bytes 4718600 | tf_op jit(solution)/shard_map/ppermute | solution.py:36
  49.8 19.1 %collective-permute-start.8 = (bf16[576,768]{1,0:T(8,128)(2,1)S(1)}, bf16[576,768]{1,0:T(8,128)(2,1)S(1)}, u32[]{:S(2)}, u32[]{:S(2)}) collective-permute-start(bf16[576,768]{1,0:T(8,128)(2,1)S(1)} %collective-permute-done.2.refs_4_), channel_id=1, source_target_pairs={{0,6},{1,3},{2,0},{3,5},{4,2},{5,7},{6,4},{7,1},{8,14},{9,11},{10,... | collective-permute-start | bytes 2654216 | tf_op jit(solution)/shard_map/ppermute | solution.py:36
  52.6 35.3 %collective-permute-start.4 = (bf16[1024,768]{1,0:T(8,128)(2,1)}, bf16[1024,768]{1,0:T(8,128)(2,1)}, u32[]{:S(2)}, u32[]{:S(2)}) collective-permute-start(bf16[1024,768]{1,0:T(8,128)(2,1)} %collective-permute-done.refs_1_), channel_id=1, source_target_pairs={{0,2},{1,7},{2,4},{3,1},{4,6},{5,3},{6,0},{7,5},{8,10},{9,15},{10,... | collective-permute-start | bytes 4718600 | tf_op jit(solution)/shard_map/ppermute | solution.py:36
  66.4 17.1 %collective-permute-start.7 = (bf16[448,768]{1,0:T(8,128)(2,1)S(1)}, bf16[448,768]{1,0:T(8,128)(2,1)}, u32[]{:S(2)}, u32[]{:S(2)}) collective-permute-start(bf16[448,768]{1,0:T(8,128)(2,1)S(1)} %slice.22), channel_id=1, source_target_pairs={{0,8},{8,0},{1,9},{9,1},{2,10},{10,2},{3,11},{11,3},{4,12},{12,4},... | collective-permute-start | bytes 2064392 | tf_op jit(solution)/shard_map/ppermute | solution.py:183
  68.9 0.9 copy-start.1
  69.8 18.1 %collective-permute-start.9 = (bf16[576,768]{1,0:T(8,128)(2,1)}, bf16[576,768]{1,0:T(8,128)(2,1)S(1)}, u32[]{:S(2)}, u32[]{:S(2)}) collective-permute-start(bf16[576,768]{1,0:T(8,128)(2,1)} %collective-permute-done.3.refs_6_), channel_id=1, source_target_pairs={{0,2},{1,7},{2,4},{3,1},{4,6},{5,3},{6,0},{7,5},{8,10},{9,15},{10,... | collective-permute-start | bytes 2654216 | tf_op jit(solution)/shard_map/ppermute | solution.py:36
  69.8 31.0 %collective-permute-start.16 = (bf16[768,1024]{1,0:T(8,128)(2,1)}, bf16[768,1024]{1,0:T(8,128)(2,1)}, u32[]{:S(2)}, u32[]{:S(2)}) collective-permute-start(bf16[768,1024]{1,0:T(8,128)(2,1)} %collective-permute-done.6.refs_10_.refs_14_.refs_16_), channel_id=1, source_target_pairs={{0,16},{1,49},{16,32},{17,1},{32,48},{33,17},{48,0},{49,33},{2,18}... | collective-permute-start | bytes 4718600 | tf_op jit(solution)/shard_map/ppermute | solution.py:36
  83.5 25.7 %collective-permute-start.17 = (bf16[768,1024]{1,0:T(8,128)(2,1)}, bf16[768,1024]{1,0:T(8,128)(2,1)}, u32[]{:S(2)}, u32[]{:S(2)}) collective-permute-start(bf16[768,1024]{1,0:T(8,128)(2,1)} %collective-permute-done.6.refs_10_.refs_14_.refs_16_), channel_id=1, source_target_pairs={{0,48},{1,17},{16,0},{17,33},{32,16},{33,49},{48,32},{49,1},{2,50}... | collective-permute-start | bytes 4718600 | tf_op jit(solution)/shard_map/ppermute | solution.py:36
  87.9 17.0 %collective-permute-start.10 = (bf16[448,768]{1,0:T(8,128)(2,1)}, bf16[448,768]{1,0:T(8,128)(2,1)S(1)}, u32[]{:S(2)}, u32[]{:S(2)}) collective-permute-start(bf16[448,768]{1,0:T(8,128)(2,1)} %collective-permute-done.7.refs_5_), channel_id=1, source_target_pairs={{0,2},{1,7},{2,4},{3,1},{4,6},{5,3},{6,0},{7,5},{8,10},{9,15},{10,... | collective-permute-start | bytes 2064392 | tf_op jit(solution)/shard_map/ppermute | solution.py:36
  96.3 12.9 %collective-permute-start.14 = (bf16[448,768]{1,0:T(8,128)(2,1)}, bf16[448,768]{1,0:T(8,128)(2,1)S(1)}, u32[]{:S(2)}, u32[]{:S(2)}) collective-permute-start(bf16[448,768]{1,0:T(8,128)(2,1)} %collective-permute-done.7.refs_5_), channel_id=1, source_target_pairs={{0,6},{1,3},{2,0},{3,5},{4,2},{5,7},{6,4},{7,1},{8,14},{9,11},{10,... | collective-permute-start | bytes 2064392 | tf_op jit(solution)/shard_map/ppermute | solution.py:36
  97.6 22.4 %collective-permute-start.19 = (bf16[384,1024]{1,0:T(8,128)(2,1)S(1)}, bf16[384,1024]{1,0:T(8,128)(2,1)S(1)}, u32[]{:S(2)}, u32[]{:S(2)}) collective-permute-start(bf16[384,1024]{1,0:T(8,128)(2,1)S(1)} %slice.29), channel_id=1, source_target_pairs={{0,64},{64,0},{1,65},{65,1},{2,66},{66,2},{3,67},{67,3},{4,68},{68... | collective-permute-start | bytes 2359304 | tf_op jit(solution)/shard_map/ppermute | solution.py:183
  102.1 17.9 %collective-permute-start.18 = (bf16[384,1024]{1,0:T(8,128)(2,1)S(1)}, bf16[384,1024]{1,0:T(8,128)(2,1)S(1)}, u32[]{:S(2)}, u32[]{:S(2)}) collective-permute-start(bf16[384,1024]{1,0:T(8,128)(2,1)S(1)} %slice.28), channel_id=1, source_target_pairs={{0,16},{1,49},{16,32},{17,1},{32,48},{33,17},{48,0},{49,33},{2,18}... | collective-permute-start | bytes 2359304 | tf_op jit(solution)/shard_map/ppermute | solution.py:36
  104.9 4.4 %copy-start.2 = (bf16[448,768]{1,0:T(8,128)(2,1)}, bf16[448,768]{1,0:T(8,128)(2,1)S(1)}, u32[]{:S(2)}) copy-start(bf16[448,768]{1,0:T(8,128)(2,1)S(1)} %collective-permute-done.10.refs_7_) | copy-start | bytes 2064388
  104.9 15.1 %collective-permute-start.15 = (bf16[448,768]{1,0:T(8,128)(2,1)S(1)}, bf16[448,768]{1,0:T(8,128)(2,1)S(1)}, u32[]{:S(2)}, u32[]{:S(2)}) collective-permute-start(bf16[448,768]{1,0:T(8,128)(2,1)S(1)} %collective-permute-done.10.refs_7_), channel_id=1, source_target_pairs={{0,2},{1,7},{2,4},{3,1},{4,6},{5,3},{6,0},{7,5},{8,10},{9,15},{10,... | collective-permute-start | bytes 2064392 | tf_op jit(solution)/shard_map/ppermute | solution.py:36
  109.2 0.9 copy-start.3
  124.2 4.3 %collective-permute-start.20 = (f32[1024,512]{1,0:T(8,128)S(1)}, f32[1024,512]{1,0:T(8,128)S(1)}, u32[]{:S(2)}, u32[]{:S(2)}) collective-permute-start(f32[1024,512]{1,0:T(8,128)S(1)} %shard_map.70), channel_id=1, source_target_pairs={{0,1},{1,0},{2,3},{3,2},{4,5},{5,4},{6,7},{7,6},{8,9},{9,8},{10,11... | collective-permute-start | bytes 6291464 | tf_op jit(solution)/shard_map/ppermute | solution.py:183

commit v8 on v7

--- a/solution.py
+++ b/solution.py
@@ -201,7 +201,7 @@
 
     p_1 = swap(after(a[part:], r), "xl")
     r_near = ring_step(after(r, y_other), "y")
-    r_other = ring_step(after(r, y_far, p_1, p_0_other), "y", -1)
+    r_other = ring_step(after(r, y_far, p_1), "y", -1)
     split = b.shape[0] // 2
     r_far_1 = swap(after(y_far[split:], p_1), "xh")
     p_1_near = ring_step(after(p_1, z_far, p_0_far), "z")

time: 152 us -> 152 us (level)
  no operation moved by 1% of the time
where the time goes in v8:
time: 152 us; the launch traced here: 150 us
  waiting for transfers between devices  53.3 us (35%)
  starting transfers between devices  39.5 us (26%)
  Pallas kernels  24.7 us (16%)
  blocking collectives  19.3 us (13%)
  local copies, waits for them, and re-layouts  10.7 us (7%)
  other arithmetic  2.16 us (1%)
    ppermute x6, waiting for transfers between devices, swap(): return lax.ppermute(block, axis, SWAP)  36.7 us
    ppermute x15, starting transfers between devices, ring_step(): return lax.ppermute(block, (axis, 'c'), pairs)  29.1 us
    pallas_call x4, Pallas kernels, product(): pl.pallas_call(kernel, out_shape=[jax.ShapeDtypeStruct((rows, width), jnp...  23.8 us
    all_to_all x1, blocking collectives, shards(): lax.all_to_all(turned, ('xl', 'z', 'c'), split_axis=0, concat_axis=1, til...  19.3 us
    ppermute x15, waiting for transfers between devices, ring_step(): return lax.ppermute(block, (axis, 'c'), pairs)  16.6 us
    ppermute x6, starting transfers between devices, swap(): return lax.ppermute(block, axis, SWAP)  10.4 us
  transfers between devices with their start and end apart: 21, of which 10 were waited for; matrix products, arithmetic and copies ran while one was open for 5% of the time, Pallas kernels for 13%

profile of v8, /device:TPU:1, one launch (start us, length us, event | category | flops | bytes accessed | tf_op | source)
XLA Modules:
  0.0 150.4 jit_solution(17661243636203754653)
XLA Ops:
  0.6 1.5 constant_dynamic-slice_fusion.1
  2.1 1.5 collective-permute-start.5
  3.6 3.8 %collective-permute-start = (bf16[1024,768]{1,0:T(8,128)(2,1)}, bf16[1024,768]{1,0:T(8,128)(2,1)}, u32[]{:S(2)}, u32[]{:S(2)}) collective-permute-start(bf16[1024,768]{1,0:T(8,128)(2,1)} %refs_0_.7), channel_id=1, source_target_pairs={{0,2},{1,7},{2,4},{3,1},{4,6},{5,3},{6,0},{7,5},{8,10},{9,15},{10,... | collective-permute-start | bytes 4718600 | tf_op jit(solution)/shard_map/ppermute | solution.py:36
  7.5 1.3 slice.21
  8.7 1.3 collective-permute-start.2
  10.0 0.2 pad_maximum_fusion.refs_6_.refs_10_.refs_12_
  10.2 1.4 collective-permute-start.12
  11.6 1.5 %collective-permute-start.11 = (bf16[768,1024]{1,0:T(8,128)(2,1)S(1)}, bf16[768,1024]{1,0:T(8,128)(2,1)}, u32[]{:S(2)}, u32[]{:S(2)}) collective-permute-start(bf16[768,1024]{1,0:T(8,128)(2,1)S(1)} %pad_maximum_fusion.refs_6_.refs_10_.refs_12_), channel_id=1, source_target_pairs={{0,16},{1,49},{16,32},{17,1},{32,48},{33,17},{48,0},{49,33},{2,18}... | collective-permute-start | bytes 4718600 | tf_op jit(solution)/shard_map/ppermute | solution.py:36
  13.1 16.1 %collective-permute-done.2.refs_4_ = bf16[576,768]{1,0:T(8,128)(2,1)S(1)} collective-permute-done((bf16[576,768]{1,0:T(8,128)(2,1)S(1)}, bf16[576,768]{1,0:T(8,128)(2,1)S(1)}, u32[]{:S(2)}, u32[]{:S(2)}) %collective-permute-start.2) | collective-permute-done | bytes 884768 | tf_op jit(solution)/shard_map/ppermute | solution.py:183
  29.3 2.7 %collective-permute-start.6 = (bf16[768,1024]{1,0:T(8,128)(2,1)S(1)}, bf16[768,1024]{1,0:T(8,128)(2,1)}, u32[]{:S(2)}, u32[]{:S(2)}) collective-permute-start(bf16[768,1024]{1,0:T(8,128)(2,1)S(1)} %pad_maximum_fusion.refs_6_.refs_10_.refs_12_), channel_id=1, source_target_pairs={{0,64},{64,0},{1,65},{65,1},{2,66},{66,2},{3,67},{67,3},{4,68},{68... | collective-permute-start | bytes 4718600 | tf_op jit(solution)/shard_map/ppermute | solution.py:183
  32.1 0.7 dynamic-slice_bitcast_fusion
  32.7 1.9 %fusion.2 = (f32[1024,128]{1,0:T(8,128)S(1)}, f32[1024,128]{1,0:T(8,128)S(1)}) fusion(f32[128]{0:T(128)S(1)} %get-tuple-element.47, f32[128]{0:T(128)S(1)} %get-tuple-element.48, f32[1024]{0:T(1024)S(1)} %convert_element_type.10, pred[]{:T(512)S(6)} %lt.43), kind=kLoop, calls=%fused_computation.5 | loop fusion | flops 524288 | bytes 1053697 | tf_op jit(solution)/shard_map/jit(_where)/select_n | solution.py:240
  34.7 0.5 collective-permute-done.refs_1_
  35.2 3.4 %collective-permute-start.3 = (bf16[576,768]{1,0:T(8,128)(2,1)S(1)}, bf16[576,768]{1,0:T(8,128)(2,1)}, u32[]{:S(2)}, u32[]{:S(2)}) collective-permute-start(bf16[576,768]{1,0:T(8,128)(2,1)S(1)} %collective-permute-done.2.refs_4_), channel_id=1, source_target_pairs={{0,2},{1,7},{2,4},{3,1},{4,6},{5,3},{6,0},{7,5},{8,10},{9,15},{10,... | collective-permute-start | bytes 2654216 | tf_op jit(solution)/shard_map/ppermute | solution.py:36
  38.6 7.5 %collective-permute-done.12.refs_8_.refs_12_.refs_14_ = bf16[768,1024]{1,0:T(8,128)(2,1)} collective-permute-done((bf16[768,1024]{1,0:T(8,128)(2,1)S(1)}, bf16[768,1024]{1,0:T(8,128)(2,1)}, u32[]{:S(2)}, u32[]{:S(2)}) %collective-permute-start.12) | collective-permute-done | bytes 1572896 | tf_op jit(solution)/shard_map/ppermute | solution.py:36
  46.1 0.1 collective-permute-done.11.refs_7_.refs_11_.refs_13_
  46.2 3.5 %collective-permute-start.13 = (bf16[768,1024]{1,0:T(8,128)(2,1)}, bf16[768,1024]{1,0:T(8,128)(2,1)}, u32[]{:S(2)}, u32[]{:S(2)}) collective-permute-start(bf16[768,1024]{1,0:T(8,128)(2,1)} %collective-permute-done.11.refs_7_.refs_11_.refs_13_), channel_id=1, source_target_pairs={{0,16},{1,49},{16,32},{17,1},{32,48},{33,17},{48,0},{49,33},{2,18}... | collective-permute-start | bytes 4718600 | tf_op jit(solution)/shard_map/ppermute | solution.py:36
  49.8 2.8 %collective-permute-done.3.refs_6_ = bf16[576,768]{1,0:T(8,128)(2,1)} collective-permute-done((bf16[576,768]{1,0:T(8,128)(2,1)S(1)}, bf16[576,768]{1,0:T(8,128)(2,1)}, u32[]{:S(2)}, u32[]{:S(2)}) %collective-permute-start.3) | collective-permute-done | bytes 884768 | tf_op jit(solution)/shard_map/ppermute | solution.py:36
  52.6 3.5 %collective-permute-start.4 = (bf16[1024,768]{1,0:T(8,128)(2,1)}, bf16[1024,768]{1,0:T(8,128)(2,1)}, u32[]{:S(2)}, u32[]{:S(2)}) collective-permute-start(bf16[1024,768]{1,0:T(8,128)(2,1)} %collective-permute-done.refs_1_), channel_id=1, source_target_pairs={{0,2},{1,7},{2,4},{3,1},{4,6},{5,3},{6,0},{7,5},{8,10},{9,15},{10,... | collective-permute-start | bytes 4718600 | tf_op jit(solution)/shard_map/ppermute | solution.py:36
  56.1 1.1 slice.22
  57.2 9.2 %collective-permute-done.6.refs_10_.refs_14_.refs_16_ = bf16[768,1024]{1,0:T(8,128)(2,1)} collective-permute-done((bf16[768,1024]{1,0:T(8,128)(2,1)S(1)}, bf16[768,1024]{1,0:T(8,128)(2,1)}, u32[]{:S(2)}, u32[]{:S(2)}) %collective-permute-start.6) | collective-permute-done | bytes 1572896 | tf_op jit(solution)/shard_map/ppermute | solution.py:183
  66.4 1.5 %collective-permute-start.7 = (bf16[448,768]{1,0:T(8,128)(2,1)S(1)}, bf16[448,768]{1,0:T(8,128)(2,1)}, u32[]{:S(2)}, u32[]{:S(2)}) collective-permute-start(bf16[448,768]{1,0:T(8,128)(2,1)S(1)} %slice.22), channel_id=1, source_target_pairs={{0,8},{8,0},{1,9},{9,1},{2,10},{10,2},{3,11},{11,3},{4,12},{12,4},... | collective-permute-start | bytes 2064392 | tf_op jit(solution)/shard_map/ppermute | solution.py:183
  67.9 1.0 collective-permute-done.8.refs_8_
  68.9 0.9 copy-done.1
  69.8 2.3 %collective-permute-start.16 = (bf16[768,1024]{1,0:T(8,128)(2,1)}, bf16[768,1024]{1,0:T(8,128)(2,1)}, u32[]{:S(2)}, u32[]{:S(2)}) collective-permute-start(bf16[768,1024]{1,0:T(8,128)(2,1)} %collective-permute-done.6.refs_10_.refs_14_.refs_16_), channel_id=1, source_target_pairs={{0,16},{1,49},{16,32},{17,1},{32,48},{33,17},{48,0},{49,33},{2,18}... | collective-permute-start | bytes 4718600 | tf_op jit(solution)/shard_map/ppermute | solution.py:36
  72.2 11.4 %collective-permute-done.7.refs_5_ = bf16[448,768]{1,0:T(8,128)(2,1)} collective-permute-done((bf16[448,768]{1,0:T(8,128)(2,1)S(1)}, bf16[448,768]{1,0:T(8,128)(2,1)}, u32[]{:S(2)}, u32[]{:S(2)}) %collective-permute-start.7) | collective-permute-done | bytes 688160 | tf_op jit(solution)/shard_map/ppermute | solution.py:183
  83.5 1.3 collective-permute-start.17
  84.8 0.1 copy.9
  84.9 0.1 reshape.33.table_ref
  85.0 2.9 %collective-permute-done.9.refs_10_ = bf16[576,768]{1,0:T(8,128)(2,1)S(1)} collective-permute-done((bf16[576,768]{1,0:T(8,128)(2,1)}, bf16[576,768]{1,0:T(8,128)(2,1)S(1)}, u32[]{:S(2)}, u32[]{:S(2)}) %collective-permute-start.9) | collective-permute-done | bytes 884768 | tf_op jit(solution)/shard_map/ppermute | solution.py:36
  87.9 2.8 %collective-permute-start.10 = (bf16[448,768]{1,0:T(8,128)(2,1)}, bf16[448,768]{1,0:T(8,128)(2,1)S(1)}, u32[]{:S(2)}, u32[]{:S(2)}) collective-permute-start(bf16[448,768]{1,0:T(8,128)(2,1)} %collective-permute-done.7.refs_5_), channel_id=1, source_target_pairs={{0,2},{1,7},{2,4},{3,1},{4,6},{5,3},{6,0},{7,5},{8,10},{9,15},{10,... | collective-permute-start | bytes 2064392 | tf_op jit(solution)/shard_map/ppermute | solution.py:36
  90.7 5.6 %shard_map.67 = (f32[1024,512]{1,0:T(8,128)S(1)}, f32[1024,512]{1,0:T(8,128)S(1)}) custom-call(s32[16]{0:T(128)S(1)} %reshape.33.table_ref, bf16[1024,768]{1,0:T(8,128)(2,1)} %refs_0_.7, bf16[1024,768]{1,0:T(8,128)(2,1)} %collective-permute-done.refs_1_, bf16[1024,768]{1,0:T(8,128)(2,1)} %collective-permute-done.1.refs_2_, ...), custom_call_target="tpu_custom_call" | custom-call | flops 3221225472 | bytes 6291456 | tf_op jit(solution)/shard_map/pallas_call | solution.py:133
  96.4 1.2 slice.29
  97.6 3.3 %collective-permute-start.19 = (bf16[384,1024]{1,0:T(8,128)(2,1)S(1)}, bf16[384,1024]{1,0:T(8,128)(2,1)S(1)}, u32[]{:S(2)}, u32[]{:S(2)}) collective-permute-start(bf16[384,1024]{1,0:T(8,128)(2,1)S(1)} %slice.29), channel_id=1, source_target_pairs={{0,64},{64,0},{1,65},{65,1},{2,66},{66,2},{3,67},{67,3},{4,68},{68... | collective-permute-start | bytes 2359304 | tf_op jit(solution)/shard_map/ppermute | solution.py:183
  100.9 1.2 slice.28
  102.1 2.8 %collective-permute-start.18 = (bf16[384,1024]{1,0:T(8,128)(2,1)S(1)}, bf16[384,1024]{1,0:T(8,128)(2,1)S(1)}, u32[]{:S(2)}, u32[]{:S(2)}) collective-permute-start(bf16[384,1024]{1,0:T(8,128)(2,1)S(1)} %slice.28), channel_id=1, source_target_pairs={{0,16},{1,49},{16,32},{17,1},{32,48},{33,17},{48,0},{49,33},{2,18}... | collective-permute-start | bytes 2359304 | tf_op jit(solution)/shard_map/ppermute | solution.py:36
  104.9 2.7 %collective-permute-start.15 = (bf16[448,768]{1,0:T(8,128)(2,1)S(1)}, bf16[448,768]{1,0:T(8,128)(2,1)S(1)}, u32[]{:S(2)}, u32[]{:S(2)}) collective-permute-start(bf16[448,768]{1,0:T(8,128)(2,1)S(1)} %collective-permute-done.10.refs_7_), channel_id=1, source_target_pairs={{0,2},{1,7},{2,4},{3,1},{4,6},{5,3},{6,0},{7,5},{8,10},{9,15},{10,... | collective-permute-start | bytes 2064392 | tf_op jit(solution)/shard_map/ppermute | solution.py:36
  107.5 1.7 %collective-permute-done.14.refs_9_ = bf16[448,768]{1,0:T(8,128)(2,1)S(1)} collective-permute-done((bf16[448,768]{1,0:T(8,128)(2,1)}, bf16[448,768]{1,0:T(8,128)(2,1)S(1)}, u32[]{:S(2)}, u32[]{:S(2)}) %collective-permute-start.14) | collective-permute-done | bytes 688160 | tf_op jit(solution)/shard_map/ppermute | solution.py:36
  109.2 0.9 copy-done.3
  110.1 9.8 %shard_map.68 = (f32[1024,512]{1,0:T(8,128)S(1)}, f32[1024,512]{1,0:T(8,128)S(1)}) custom-call(s32[16]{0:T(128)S(1)} %reshape.33.table_ref, bf16[1024,768]{1,0:T(8,128)(2,1)} %refs_0_.7, bf16[1024,768]{1,0:T(8,128)(2,1)} %collective-permute-done.refs_1_, bf16[1024,768]{1,0:T(8,128)(2,1)} %collective-permute-done.1.refs_2_, ...), custom_call_target="tpu_custom_call" | custom-call | flops 6442450944 | bytes 12582912 | tf_op jit(solution)/shard_map/pallas_call | solution.py:133
  120.0 4.2 %shard_map.70 = f32[1024,512]{1,0:T(8,128)S(1)} custom-call(s32[16]{0:T(128)S(1)} %reshape.33.table_ref, bf16[1024,768]{1,0:T(8,128)(2,1)} %refs_0_.7, bf16[1024,768]{1,0:T(8,128)(2,1)} %collective-permute-done.refs_1_, bf16[1024,768]{1,0:T(8,128)(2,1)} %collective-permute-done.1.refs_2_, bf16[1024,768]{1,0:T(8,128)(2,1)} %collective-permute-done.4.refs_3_, ...), custom_call_target="tpu_custom_call" | custom-call | flops 1610612736 | bytes 4718592 | tf_op jit(solution)/shard_map/pallas_call | solution.py:133
  124.2 0.1 collective-permute-start.20
  124.3 4.2 %shard_map.69.refs_0_ = f32[1024,512]{1,0:T(8,128)S(1)} custom-call(s32[16]{0:T(128)S(1)} %reshape.33.table_ref, bf16[1024,768]{1,0:T(8,128)(2,1)} %refs_0_.7, bf16[1024,768]{1,0:T(8,128)(2,1)} %collective-permute-done.refs_1_, bf16[1024,768]{1,0:T(8,128)(2,1)} %collective-permute-done.1.refs_2_, bf16[1024,768]{1,0:T(8,128)(2,1)} %collective-permute-done.4.refs_3_, ...), custom_call_target="tpu_custom_call" | custom-call | flops 1610612736 | bytes 4718592 | tf_op jit(solution)/shard_map/pallas_call | solution.py:133
  128.4 0.9 shard_map.71
  129.4 19.3 %all_to_all.19 = bf16[16,64,512]{2,1,0:T(8,128)(2,1)S(1)} all-to-all(bf16[16,64,512]{2,1,0:T(8,128)(2,1)S(1)} %bitcast.6), channel_id=1, replica_groups=mesh['xh'=2,'y'=4,'xl'=2,'z'=4,'c'=2] {'xl','z','c'}, dimensions={0} | all-to-all | bytes 2097152 | tf_op jit(solution)/shard_map/all_to_all | solution.py:254
  148.6 0.1 copy.11
  148.7 0.9 slice.30
  149.7 0.7 fusion.6
  (25 shorter events, 0.1 us)
Async XLA Ops:
  2.1 7.9 %collective-permute-start.5 = (bf16[768,512]{1,0:T(8,128)(2,1)S(1)}, bf16[768,512]{1,0:T(8,128)(2,1)S(1)}, u32[]{:S(2)}, u32[]{:S(2)}) collective-permute-start(bf16[768,512]{1,0:T(8,128)(2,1)S(1)} %get-tuple-element.42), channel_id=1, source_target_pairs={{0,1},{1,0},{2,3},{3,2},{4,5},{5,4},{6,7},{7,6},{8,9},{9,8},{10,11... | collective-permute-start | bytes 2359304 | tf_op jit(solution)/shard_map/ppermute | solution.py:183
  3.6 31.6 %collective-permute-start = (bf16[1024,768]{1,0:T(8,128)(2,1)}, bf16[1024,768]{1,0:T(8,128)(2,1)}, u32[]{:S(2)}, u32[]{:S(2)}) collective-permute-start(bf16[1024,768]{1,0:T(8,128)(2,1)} %refs_0_.7), channel_id=1, source_target_pairs={{0,2},{1,7},{2,4},{3,1},{4,6},{5,3},{6,0},{7,5},{8,10},{9,15},{10,... | collective-permute-start | bytes 4718600 | tf_op jit(solution)/shard_map/ppermute | solution.py:36
  8.7 20.6 %collective-permute-start.2 = (bf16[576,768]{1,0:T(8,128)(2,1)S(1)}, bf16[576,768]{1,0:T(8,128)(2,1)S(1)}, u32[]{:S(2)}, u32[]{:S(2)}) collective-permute-start(bf16[576,768]{1,0:T(8,128)(2,1)S(1)} %slice.21), channel_id=1, source_target_pairs={{0,8},{8,0},{1,9},{9,1},{2,10},{10,2},{3,11},{11,3},{4,12},{12,4},... | collective-permute-start | bytes 2654216 | tf_op jit(solution)/shard_map/ppermute | solution.py:183
  10.0 22.0 %copy-start.4 = (s32[1024]{0:T(1024)S(1)}, s32[1024]{0:T(1024)}, u32[]{:S(2)}) copy-start(s32[1024]{0:T(1024)} %param.6) | copy-start | bytes 12292
  10.2 35.9 %collective-permute-start.12 = (bf16[768,1024]{1,0:T(8,128)(2,1)S(1)}, bf16[768,1024]{1,0:T(8,128)(2,1)}, u32[]{:S(2)}, u32[]{:S(2)}) collective-permute-start(bf16[768,1024]{1,0:T(8,128)(2,1)S(1)} %pad_maximum_fusion.refs_6_.refs_10_.refs_12_), channel_id=1, source_target_pairs={{0,48},{1,17},{16,0},{17,33},{32,16},{33,49},{48,32},{49,1},{2,50}... | collective-permute-start | bytes 4718600 | tf_op jit(solution)/shard_map/ppermute | solution.py:36
  11.6 34.6 %collective-permute-start.11 = (bf16[768,1024]{1,0:T(8,128)(2,1)S(1)}, bf16[768,1024]{1,0:T(8,128)(2,1)}, u32[]{:S(2)}, u32[]{:S(2)}) collective-permute-start(bf16[768,1024]{1,0:T(8,128)(2,1)S(1)} %pad_maximum_fusion.refs_6_.refs_10_.refs_12_), channel_id=1, source_target_pairs={{0,16},{1,49},{16,32},{17,1},{32,48},{33,17},{48,0},{49,33},{2,18}... | collective-permute-start | bytes 4718600 | tf_op jit(solution)/shard_map/ppermute | solution.py:36
  13.1 36.6 %collective-permute-start.1 = (bf16[1024,768]{1,0:T(8,128)(2,1)}, bf16[1024,768]{1,0:T(8,128)(2,1)}, u32[]{:S(2)}, u32[]{:S(2)}) collective-permute-start(bf16[1024,768]{1,0:T(8,128)(2,1)} %refs_0_.7), channel_id=1, source_target_pairs={{0,6},{1,3},{2,0},{3,5},{4,2},{5,7},{6,4},{7,1},{8,14},{9,11},{10,... | collective-permute-start | bytes 4718600 | tf_op jit(solution)/shard_map/ppermute | solution.py:36
  29.3 38.7 %copy-start = (bf16[576,768]{1,0:T(8,128)(2,1)}, bf16[576,768]{1,0:T(8,128)(2,1)S(1)}, u32[]{:S(2)}) copy-start(bf16[576,768]{1,0:T(8,128)(2,1)S(1)} %collective-permute-done.2.refs_4_) | copy-start | bytes 2654212
  29.3 37.1 %collective-permute-start.6 = (bf16[768,1024]{1,0:T(8,128)(2,1)S(1)}, bf16[768,1024]{1,0:T(8,128)(2,1)}, u32[]{:S(2)}, u32[]{:S(2)}) collective-permute-start(bf16[768,1024]{1,0:T(8,128)(2,1)S(1)} %pad_maximum_fusion.refs_6_.refs_10_.refs_12_), channel_id=1, source_target_pairs={{0,64},{64,0},{1,65},{65,1},{2,66},{66,2},{3,67},{67,3},{4,68},{68... | collective-permute-start | bytes 4718600 | tf_op jit(solution)/shard_map/ppermute | solution.py:183
  35.2 17.4 %collective-permute-start.3 = (bf16[576,768]{1,0:T(8,128)(2,1)S(1)}, bf16[576,768]{1,0:T(8,128)(2,1)}, u32[]{:S(2)}, u32[]{:S(2)}) collective-permute-start(bf16[576,768]{1,0:T(8,128)(2,1)S(1)} %collective-permute-done.2.refs_4_), channel_id=1, source_target_pairs={{0,2},{1,7},{2,4},{3,1},{4,6},{5,3},{6,0},{7,5},{8,10},{9,15},{10,... | collective-permute-start | bytes 2654216 | tf_op jit(solution)/shard_map/ppermute | solution.py:36
  46.2 37.3 %collective-permute-start.13 = (bf16[768,1024]{1,0:T(8,128)(2,1)}, bf16[768,1024]{1,0:T(8,128)(2,1)}, u32[]{:S(2)}, u32[]{:S(2)}) collective-permute-start(bf16[768,1024]{1,0:T(8,128)(2,1)} %collective-permute-done.11.refs_7_.refs_11_.refs_13_), channel_id=1, source_target_pairs={{0,16},{1,49},{16,32},{17,1},{32,48},{33,17},{48,0},{49,33},{2,18}... | collective-permute-start | bytes 4718600 | tf_op jit(solution)/shard_map/ppermute | solution.py:36
  49.8 19.1 %collective-permute-start.8 = (bf16[576,768]{1,0:T(8,128)(2,1)S(1)}, bf16[576,768]{1,0:T(8,128)(2,1)S(1)}, u32[]{:S(2)}, u32[]{:S(2)}) collective-permute-start(bf16[576,768]{1,0:T(8,128)(2,1)S(1)} %collective-permute-done.2.refs_4_), channel_id=1, source_target_pairs={{0,6},{1,3},{2,0},{3,5},{4,2},{5,7},{6,4},{7,1},{8,14},{9,11},{10,... | collective-permute-start | bytes 2654216 | tf_op jit(solution)/shard_map/ppermute | solution.py:36
  52.6 35.3 %collective-permute-start.4 = (bf16[1024,768]{1,0:T(8,128)(2,1)}, bf16[1024,768]{1,0:T(8,128)(2,1)}, u32[]{:S(2)}, u32[]{:S(2)}) collective-permute-start(bf16[1024,768]{1,0:T(8,128)(2,1)} %collective-permute-done.refs_1_), channel_id=1, source_target_pairs={{0,2},{1,7},{2,4},{3,1},{4,6},{5,3},{6,0},{7,5},{8,10},{9,15},{10,... | collective-permute-start | bytes 4718600 | tf_op jit(solution)/shard_map/ppermute | solution.py:36
  66.4 17.1 %collective-permute-start.7 = (bf16[448,768]{1,0:T(8,128)(2,1)S(1)}, bf16[448,768]{1,0:T(8,128)(2,1)}, u32[]{:S(2)}, u32[]{:S(2)}) collective-permute-start(bf16[448,768]{1,0:T(8,128)(2,1)S(1)} %slice.22), channel_id=1, source_target_pairs={{0,8},{8,0},{1,9},{9,1},{2,10},{10,2},{3,11},{11,3},{4,12},{12,4},... | collective-permute-start | bytes 2064392 | tf_op jit(solution)/shard_map/ppermute | solution.py:183
  68.9 0.9 copy-start.1
  69.8 18.1 %collective-permute-start.9 = (bf16[576,768]{1,0:T(8,128)(2,1)}, bf16[576,768]{1,0:T(8,128)(2,1)S(1)}, u32[]{:S(2)}, u32[]{:S(2)}) collective-permute-start(bf16[576,768]{1,0:T(8,128)(2,1)} %collective-permute-done.3.refs_6_), channel_id=1, source_target_pairs={{0,2},{1,7},{2,4},{3,1},{4,6},{5,3},{6,0},{7,5},{8,10},{9,15},{10,... | collective-permute-start | bytes 2654216 | tf_op jit(solution)/shard_map/ppermute | solution.py:36
  69.8 31.0 %collective-permute-start.16 = (bf16[768,1024]{1,0:T(8,128)(2,1)}, bf16[768,1024]{1,0:T(8,128)(2,1)}, u32[]{:S(2)}, u32[]{:S(2)}) collective-permute-start(bf16[768,1024]{1,0:T(8,128)(2,1)} %collective-permute-done.6.refs_10_.refs_14_.refs_16_), channel_id=1, source_target_pairs={{0,16},{1,49},{16,32},{17,1},{32,48},{33,17},{48,0},{49,33},{2,18}... | collective-permute-start | bytes 4718600 | tf_op jit(solution)/shard_map/ppermute | solution.py:36
  83.5 25.7 %collective-permute-start.17 = (bf16[768,1024]{1,0:T(8,128)(2,1)}, bf16[768,1024]{1,0:T(8,128)(2,1)}, u32[]{:S(2)}, u32[]{:S(2)}) collective-permute-start(bf16[768,1024]{1,0:T(8,128)(2,1)} %collective-permute-done.6.refs_10_.refs_14_.refs_16_), channel_id=1, source_target_pairs={{0,48},{1,17},{16,0},{17,33},{32,16},{33,49},{48,32},{49,1},{2,50}... | collective-permute-start | bytes 4718600 | tf_op jit(solution)/shard_map/ppermute | solution.py:36
  87.9 17.0 %collective-permute-start.10 = (bf16[448,768]{1,0:T(8,128)(2,1)}, bf16[448,768]{1,0:T(8,128)(2,1)S(1)}, u32[]{:S(2)}, u32[]{:S(2)}) collective-permute-start(bf16[448,768]{1,0:T(8,128)(2,1)} %collective-permute-done.7.refs_5_), channel_id=1, source_target_pairs={{0,2},{1,7},{2,4},{3,1},{4,6},{5,3},{6,0},{7,5},{8,10},{9,15},{10,... | collective-permute-start | bytes 2064392 | tf_op jit(solution)/shard_map/ppermute | solution.py:36
  96.3 12.9 %collective-permute-start.14 = (bf16[448,768]{1,0:T(8,128)(2,1)}, bf16[448,768]{1,0:T(8,128)(2,1)S(1)}, u32[]{:S(2)}, u32[]{:S(2)}) collective-permute-start(bf16[448,768]{1,0:T(8,128)(2,1)} %collective-permute-done.7.refs_5_), channel_id=1, source_target_pairs={{0,6},{1,3},{2,0},{3,5},{4,2},{5,7},{6,4},{7,1},{8,14},{9,11},{10,... | collective-permute-start | bytes 2064392 | tf_op jit(solution)/shard_map/ppermute | solution.py:36
  97.6 22.4 %collective-permute-start.19 = (bf16[384,1024]{1,0:T(8,128)(2,1)S(1)}, bf16[384,1024]{1,0:T(8,128)(2,1)S(1)}, u32[]{:S(2)}, u32[]{:S(2)}) collective-permute-start(bf16[384,1024]{1,0:T(8,128)(2,1)S(1)} %slice.29), channel_id=1, source_target_pairs={{0,64},{64,0},{1,65},{65,1},{2,66},{66,2},{3,67},{67,3},{4,68},{68... | collective-permute-start | bytes 2359304 | tf_op jit(solution)/shard_map/ppermute | solution.py:183
  102.1 17.9 %collective-permute-start.18 = (bf16[384,1024]{1,0:T(8,128)(2,1)S(1)}, bf16[384,1024]{1,0:T(8,128)(2,1)S(1)}, u32[]{:S(2)}, u32[]{:S(2)}) collective-permute-start(bf16[384,1024]{1,0:T(8,128)(2,1)S(1)} %slice.28), channel_id=1, source_target_pairs={{0,16},{1,49},{16,32},{17,1},{32,48},{33,17},{48,0},{49,33},{2,18}... | collective-permute-start | bytes 2359304 | tf_op jit(solution)/shard_map/ppermute | solution.py:36
  104.9 4.4 %copy-start.2 = (bf16[448,768]{1,0:T(8,128)(2,1)}, bf16[448,768]{1,0:T(8,128)(2,1)S(1)}, u32[]{:S(2)}) copy-start(bf16[448,768]{1,0:T(8,128)(2,1)S(1)} %collective-permute-done.10.refs_7_) | copy-start | bytes 2064388
  104.9 15.1 %collective-permute-start.15 = (bf16[448,768]{1,0:T(8,128)(2,1)S(1)}, bf16[448,768]{1,0:T(8,128)(2,1)S(1)}, u32[]{:S(2)}, u32[]{:S(2)}) collective-permute-start(bf16[448,768]{1,0:T(8,128)(2,1)S(1)} %collective-permute-done.10.refs_7_), channel_id=1, source_target_pairs={{0,2},{1,7},{2,4},{3,1},{4,6},{5,3},{6,0},{7,5},{8,10},{9,15},{10,... | collective-permute-start | bytes 2064392 | tf_op jit(solution)/shard_map/ppermute | solution.py:36
  109.2 0.9 copy-start.3
  124.2 4.3 %collective-permute-start.20 = (f32[1024,512]{1,0:T(8,128)S(1)}, f32[1024,512]{1,0:T(8,128)S(1)}, u32[]{:S(2)}, u32[]{:S(2)}) collective-permute-start(f32[1024,512]{1,0:T(8,128)S(1)} %shard_map.70), channel_id=1, source_target_pairs={{0,1},{1,0},{2,3},{3,2},{4,5},{5,4},{6,7},{7,6},{8,9},{9,8},{10,11... | collective-permute-start | bytes 6291464 | tf_op jit(solution)/shard_map/ppermute | solution.py:183
